TPU v7x, 32 devices: a whole 2x2x4 slice. The times are simulated.
32 devices in a mesh: section: 4 (over y, x), dp: 8 (over z, core).
Axes of the slice: x: 2, y: 2, z: 4, core: 2. Of those that a mesh axis runs over, the one named last changes fastest.
Arguments:
- images: bfloat16 [4, 6144, 512], P(None, 'dp'), may hold values from -6 to 6
- counts: int32 [4, 8], P(None, 'dp'), may hold values from 384 to 768, as said below
- pool_index: int32 [4, 8, 192], P(None, 'dp'), may hold values from 0 to 3
- conv_w: float32 [2, 4608, 512], P(None, 'dp'), may hold values from -0.09375 to 0.09375
- squeeze_w: float32 [2, 3, 512, 128], P(None, None, 'dp'), may hold values from -0.25 to 0.25
- expand_w: float32 [2, 3, 128, 512], P(None, None, 'dp'), may hold values from -1 to 1
- gain: float32 [2, 512], replicated, may hold values from 0.25 to 1.75
- bias: float32 [2, 512], replicated, may hold values from -3 to 3
- cotangent: bfloat16 [4, 3, 1536, 512], P(None, None, 'dp'), may hold values from -6 to 6
Outputs:
- task_out: bfloat16 [4, 3, 1536, 512], P('section', None, 'dp')
- image_grad: bfloat16 [4, 6144, 512], P('section', 'dp')
- conv_grad: float32 [2, 4608, 512], P(None, 'dp')
- squeeze_grad: float32 [2, 3, 512, 128], P(None, None, 'dp')
- expand_grad: float32 [2, 3, 128, 512], P(None, None, 'dp')
- gain_grad: float32 [2, 512], replicated
- bias_grad: float32 [2, 512], replicated
Inputs may be any that keep to these rules, and one draw needn't show every extreme that they name: `counts`: in every micro-batch some device has all 768 slots valid.
All inputs are finite; a program needn't handle non-finite values.
Results may differ from a plain program's by a relative error of at most 0.013.
The roundings to bfloat16 on the way count: a program that leaves them out, or rounds other values in their place, can miss the bound.
Values may be sent and summed in bfloat16 or wider, within the bound.
A program may use at most 512 MiB of HBM per device.

v0:
```python
import jax
import jax.numpy as jnp
from jax import lax
from jax.sharding import PartitionSpec as P

EPS = 1e-05


def as_sent(value):
    return jax.tree.map(lambda a: a.astype(jnp.bfloat16) if a.dtype == jnp.float32 else a, value)


def padded_2(value, sides, width):
    for axis, dim in sides:
        size, length = (lax.axis_size(axis), value.shape[dim])
        up = [(i, (i + 1) % size) for i in range(size - 1)]
        down = [(j, i) for i, j in up]
        last = lax.slice_in_dim(value, length - width, length, axis=dim)
        leading = lax.slice_in_dim(value, 0, width, axis=dim)
        before = lax.ppermute(last, axis, up)
        after = lax.ppermute(leading, axis, down)
        value = jnp.concatenate([before, value, after], axis=dim)
    return value


def passed_along(value, axis, by):
    length = lax.axis_size(axis)
    pairs = [(i, i + by) for i in range(length) if 0 <= i + by < length]
    return lax.ppermute(value, axis, pairs)


def from_behind(value, axis, by):
    length = lax.axis_size(axis)
    return lax.ppermute(value, axis, [(i, (i + by) % length) for i in range(length)])


def gelu_back(point, upstream):
    return jax.vjp(jax.nn.gelu, point)[1](upstream)[0]


def store_at(buffer, value, where_idx, live):
    return jnp.where(live, lax.dynamic_update_index_in_dim(buffer, value, where_idx, 0), buffer)


def take_at(buffer, where_idx):
    return lax.dynamic_index_in_dim(buffer, where_idx, 0, keepdims=False)


def conv_taps(padded, w_taps):
    height = padded.shape[0] - 2
    columns = padded.shape[1]
    widened = jnp.pad(padded, ((0, 0), (1, 1), (0, 0)))
    mask_count = jnp.zeros((height * columns, w_taps.shape[2]), jnp.float32)
    for tap in range(9):
        piece = widened[tap // 3 : tap // 3 + height, tap % 3 : tap % 3 + columns].reshape(
            height * columns, -1
        )
        mask_count = mask_count + jnp.dot(piece, w_taps[tap], preferred_element_type=jnp.float32)
    return mask_count


def conv_input_grad(d_padded, w_taps):
    height = d_padded.shape[0] - 2
    columns = d_padded.shape[1]
    widened = jnp.pad(d_padded, ((0, 0), (1, 1), (0, 0)))
    mask_count = jnp.zeros((height * columns, w_taps.shape[1]), jnp.float32)
    for tap in range(9):
        row_start = 2 - tap // 3
        col_start = 2 - tap % 3
        piece = widened[row_start : row_start + height, col_start : col_start + columns].reshape(
            height * columns, -1
        )
        mask_count = mask_count + lax.dot_general(
            piece, w_taps[tap], (((1,), (1,)), ((), ())), preferred_element_type=jnp.float32
        )
    return mask_count


def conv_weight_grad(padded, d_hidden):
    height = padded.shape[0] - 2
    columns = padded.shape[1]
    widened = jnp.pad(padded, ((0, 0), (1, 1), (0, 0)))
    parts = []
    for tap in range(9):
        piece = widened[tap // 3 : tap // 3 + height, tap % 3 : tap % 3 + columns].reshape(
            height * columns, -1
        )
        parts.append(
            lax.dot_general(
                piece, d_hidden, (((0,), (0,)), ((), ())), preferred_element_type=jnp.float32
            )
        )
    return jnp.concatenate(parts, 0)


def attend_forward(merged_low, w_squeeze, w_expand):
    squeezed = jnp.einsum("tpc,tcb->tpb", merged_low, w_squeeze, preferred_element_type=jnp.float32)
    excited = jax.nn.gelu(squeezed).astype(jnp.bfloat16)
    expanded = jnp.einsum("tpb,tbc->tpc", excited, w_expand, preferred_element_type=jnp.float32)
    return (squeezed, expanded)


def attend_backward(d_task, gated_from, squeezed, expanded, w_squeeze, w_expand):
    gate_val = jax.nn.sigmoid(expanded)
    d_expanded = (d_task * gated_from[None] * gate_val * (1.0 - gate_val)).astype(jnp.bfloat16)
    d_excited = jnp.einsum("tpc,tbc->tpb", d_expanded, w_expand, preferred_element_type=jnp.float32)
    d_squeezed = gelu_back(squeezed, d_excited).astype(jnp.bfloat16)
    d_merged = jnp.einsum("tpb,tcb->tpc", d_squeezed, w_squeeze, preferred_element_type=jnp.float32)
    return (d_merged, d_expanded, d_squeezed)


def attend_weight(merged_low, squeezed, d_expanded, d_squeezed):
    excited = jax.nn.gelu(squeezed).astype(jnp.bfloat16)
    grad_squeeze = jnp.einsum(
        "tpc,tpb->tcb", merged_low, d_squeezed, preferred_element_type=jnp.float32
    )
    grad_expand = jnp.einsum(
        "tpb,tpc->tbc", excited, d_expanded, preferred_element_type=jnp.float32
    )
    return (grad_squeeze, grad_expand)


def pool_pick(field, pick_idx):
    tasks = field.shape[0]
    width = field.shape[2]
    half_rows = pick_idx.shape[0]
    half_columns = pick_idx.shape[1]
    windows = field.reshape(tasks, half_rows, 2, half_columns, 2, width)
    picked = jnp.zeros((tasks, half_rows, half_columns, width), jnp.float32)
    for corner in range(4):
        hit = (pick_idx == corner)[None, :, :, None]
        picked = picked + jnp.where(hit, windows[:, :, corner // 2, :, corner % 2, :], 0.0)
    return picked.reshape(tasks, half_rows * half_columns, width)


def pool_spread(d_pooled, pick_idx):
    tasks = d_pooled.shape[0]
    width = d_pooled.shape[2]
    half_rows = pick_idx.shape[0]
    half_columns = pick_idx.shape[1]
    grid = d_pooled.reshape(tasks, half_rows, half_columns, width)
    row_parts = []
    for row_off in range(2):
        col_parts = [
            jnp.where((pick_idx == 2 * row_off + col_off)[None, :, :, None], grid, 0.0)
            for col_off in range(2)
        ]
        row_parts.append(jnp.stack(col_parts, 3))
    return jnp.stack(row_parts, 2).reshape(tasks, half_rows * 2 * half_columns * 2, width)


def on_device(images, counts, pool_index, conv_w, squeeze_w, expand_w, gain, bias, cotangent):
    rank_here = lax.axis_index("section")
    rank_count = lax.axis_size("section")
    last_rank = rank_count - 1
    micro = images.shape[0]
    pixels = images.shape[1]
    width = images.shape[2]
    tasks = squeeze_w.shape[1]
    layers = conv_w.shape[0]
    rows_dev = 2 * pool_index.shape[1]
    columns = 2 * pool_index.shape[2]
    layer_here = rank_here // 2
    is_conv = rank_here % 2 == 0
    is_first_gate = rank_here == 1
    is_last = rank_here == last_rank
    w_conv, w_squeeze, w_expand = (
        lax.all_gather(take_at(conv_w, layer_here).astype(jnp.bfloat16), "dp", axis=0, tiled=True),
        lax.all_gather(
            take_at(squeeze_w, layer_here).astype(jnp.bfloat16), "dp", axis=1, tiled=True
        ),
        lax.all_gather(
            take_at(expand_w, layer_here).astype(jnp.bfloat16), "dp", axis=1, tiled=True
        ),
    )
    w_taps = w_conv.reshape(9, width, width)
    bottle = w_squeeze.shape[2]
    norm_scale = take_at(gain, layer_here)
    beta = take_at(bias, layer_here)
    valid_counts = counts[:, 0]
    slot_rows = jnp.arange(pixels, dtype=jnp.int32)[:, None]
    ticks = micro + rank_count - 1
    back_delay = rank_count - 1

    def merge_tasks(shared_in, tasks_in):
        extra = jnp.where(is_last, tasks_in.astype(jnp.float32), 0.0)
        return (shared_in.astype(jnp.float32)[None] + extra).astype(jnp.bfloat16)

    def conv_branch(padded, merged_low):
        return (
            conv_taps(padded, w_taps),
            jnp.zeros((tasks, pixels, bottle), jnp.float32),
            jnp.zeros((tasks, pixels, width), jnp.float32),
        )

    def gate_branch(padded, merged_low):
        squeezed, expanded = attend_forward(merged_low, w_squeeze, w_expand)
        return (jnp.zeros((pixels, width), jnp.float32), squeezed, expanded)

    def quiet_gate_back(d_task, gated_from, squeezed, expanded):
        return (
            jnp.zeros((tasks, pixels, width), jnp.float32),
            jnp.zeros((tasks, pixels, width), jnp.bfloat16),
            jnp.zeros((tasks, pixels, bottle), jnp.bfloat16),
        )

    def gate_back(d_task, gated_from, squeezed, expanded):
        return attend_backward(d_task, gated_from, squeezed, expanded, w_squeeze, w_expand)

    def input_grad_fn(d_padded):
        return conv_input_grad(d_padded, w_taps)

    def no_input_grad(d_padded):
        return jnp.zeros((pixels, width), jnp.float32)

    def no_conv_weight(padded, d_hidden):
        return jnp.zeros((9 * width, width), jnp.float32)

    def no_gate_weight(merged_low, squeezed, d_expanded, d_squeezed):
        return (
            jnp.zeros((tasks, width, bottle), jnp.float32),
            jnp.zeros((tasks, bottle, width), jnp.float32),
        )

    zero_field = jnp.zeros((pixels, width), jnp.bfloat16)
    zero_tasks = jnp.zeros((tasks, pixels, width), jnp.bfloat16)
    state = {
        "recv_shared": zero_field,
        "recv_tasks": zero_tasks,
        "back_shared": zero_field,
        "back_tasks": zero_tasks,
        "task_store": jnp.zeros((micro, tasks, pixels, width), jnp.bfloat16),
        "dtask_store": jnp.zeros((micro, tasks, pixels, width), jnp.bfloat16),
        "kept_pad": jnp.zeros((micro, rows_dev + 2, columns, width), jnp.bfloat16),
        "kept_tasks": jnp.zeros((micro, tasks, pixels, width), jnp.bfloat16),
        "kept_hidden": jnp.zeros((micro, pixels, width), jnp.float32),
        "kept_squeezed": jnp.zeros((micro, tasks, pixels, bottle), jnp.float32),
        "kept_expanded": jnp.zeros((micro, tasks, pixels, width), jnp.float32),
        "centres": jnp.zeros((micro, width), jnp.float32),
        "inv_spreads": jnp.ones((micro, width), jnp.float32),
        "totals": jnp.ones((micro,), jnp.float32),
        "results": jnp.zeros((micro, tasks, pixels // 4, width), jnp.bfloat16),
        "input_grads": jnp.zeros((micro, pixels, width), jnp.bfloat16),
        "gain_sum": jnp.zeros((width,), jnp.float32),
        "bias_sum": jnp.zeros((width,), jnp.float32),
        "grad_conv": jnp.zeros((9 * width, width), jnp.float32),
        "grad_squeeze": jnp.zeros((tasks, width, bottle), jnp.float32),
        "grad_expand": jnp.zeros((tasks, bottle, width), jnp.float32),
    }
    for tick in range(ticks):
        forward_updated = dict(state)
        forward_micro_now = tick - rank_here
        forward_live = (forward_micro_now >= 0) & (forward_micro_now < micro)
        forward_slot = jnp.clip(forward_micro_now, 0, micro - 1)
        forward_valid_mask = (
            (slot_rows < take_at(valid_counts, forward_slot)) & forward_live
        ).astype(jnp.float32)
        first_in = (forward_valid_mask * take_at(images, forward_slot).astype(jnp.float32)).astype(
            jnp.bfloat16
        )
        forward_shared_in = jnp.where(rank_here == 0, first_in, state["recv_shared"])
        forward_tasks_in = state["recv_tasks"]
        forward_padded = padded_2(
            as_sent(forward_shared_in.reshape(rows_dev, columns, width)), (("dp", 0),), 1
        )
        forward_merged_low = merge_tasks(forward_shared_in, forward_tasks_in)
        forward_hidden, forward_squeezed, forward_expanded = lax.cond(
            is_conv, conv_branch, gate_branch, forward_padded, forward_merged_low
        )
        first_sum, second_sum, count_sum = lax.psum(
            (
                jnp.sum(forward_valid_mask * forward_hidden, 0),
                jnp.sum(forward_valid_mask * forward_hidden * forward_hidden, 0),
                jnp.sum(forward_valid_mask),
            ),
            "dp",
        )
        forward_mask_count = jnp.where(forward_live, count_sum, 1.0)
        forward_centre = first_sum / forward_mask_count
        spread = second_sum / forward_mask_count - forward_centre * forward_centre
        forward_inverse_deviation = lax.rsqrt(spread + EPS)
        forward_normed = (
            norm_scale * (forward_hidden - forward_centre) * forward_inverse_deviation + beta
        )
        forward_shared_f = forward_shared_in.astype(jnp.float32)
        conv_out = (forward_valid_mask * jax.nn.gelu(forward_normed)).astype(jnp.bfloat16)
        task_val = (
            forward_valid_mask[None] * jax.nn.sigmoid(forward_expanded) * forward_shared_f[None]
        )
        shared_out = jnp.where(is_conv, conv_out, forward_shared_in)
        tasks_out = jnp.where(is_first_gate, task_val.astype(jnp.bfloat16), forward_tasks_in)
        pooled = pool_pick(task_val, take_at(pool_index, forward_slot)).astype(jnp.bfloat16)
        forward_updated["kept_pad"] = store_at(
            state["kept_pad"], forward_padded, forward_slot, forward_live
        )
        forward_updated["kept_tasks"] = store_at(
            state["kept_tasks"], forward_tasks_in, forward_slot, forward_live
        )
        forward_updated["kept_hidden"] = store_at(
            state["kept_hidden"], forward_hidden, forward_slot, forward_live
        )
        forward_updated["kept_squeezed"] = store_at(
            state["kept_squeezed"], forward_squeezed, forward_slot, forward_live
        )
        forward_updated["kept_expanded"] = store_at(
            state["kept_expanded"], forward_expanded, forward_slot, forward_live
        )
        forward_updated["centres"] = store_at(
            state["centres"], forward_centre, forward_slot, forward_live
        )
        forward_updated["inv_spreads"] = store_at(
            state["inv_spreads"], forward_inverse_deviation, forward_slot, forward_live
        )
        forward_updated["totals"] = store_at(
            state["totals"], forward_mask_count, forward_slot, forward_live
        )
        forward_updated["results"] = store_at(
            state["results"], pooled, forward_slot, forward_live & is_last
        )
        forward_updated["recv_shared"], forward_updated["recv_tasks"] = (
            passed_along(as_sent(shared_out), "section", 1).astype(shared_out.dtype),
            passed_along(as_sent(tasks_out), "section", 1).astype(tasks_out.dtype),
        )
        state = forward_updated
    for tick in range(ticks):
        updated = dict(state)
        micro_now = tick - (back_delay - rank_here)
        live = (micro_now >= 0) & (micro_now < micro)
        slot = jnp.clip(micro_now, 0, micro - 1)
        valid_mask = ((slot_rows < take_at(valid_counts, slot)) & live).astype(jnp.float32)
        d_tasks_in = state["back_tasks"]
        d_shared_in = state["back_shared"].astype(jnp.float32)
        backward_padded = take_at(state["kept_pad"], slot)
        backward_shared_in = backward_padded[1:-1].reshape(pixels, width)
        shared_f = backward_shared_in.astype(jnp.float32)
        backward_tasks_in = take_at(state["kept_tasks"], slot)
        hidden = take_at(state["kept_hidden"], slot)
        backward_squeezed = take_at(state["kept_squeezed"], slot)
        backward_expanded = take_at(state["kept_expanded"], slot)
        centre = take_at(state["centres"], slot)
        inverse_deviation = take_at(state["inv_spreads"], slot)
        mask_count = take_at(state["totals"], slot)
        spread_seed = pool_spread(
            take_at(cotangent, slot).astype(jnp.float32), take_at(pool_index, slot)
        )
        backward_d_task = jnp.where(is_last, spread_seed, 0.0) + jnp.where(
            is_first_gate, d_tasks_in.astype(jnp.float32), 0.0
        )
        backward_merged_low = merge_tasks(backward_shared_in, backward_tasks_in)
        backward_gated_from = valid_mask * shared_f
        d_merged, backward_d_expanded, backward_d_squeezed = lax.cond(
            is_conv,
            quiet_gate_back,
            gate_back,
            backward_d_task,
            backward_gated_from,
            backward_squeezed,
            backward_expanded,
        )
        d_direct = valid_mask * jnp.sum(backward_d_task * jax.nn.sigmoid(backward_expanded), 0)
        d_gate_total = jnp.where(is_first_gate, d_shared_in, 0.0) + jnp.sum(d_merged, 0) + d_direct
        centered_values = (hidden - centre) * inverse_deviation
        normed = norm_scale * (hidden - centre) * inverse_deviation + beta
        norm_gradient = jnp.where(is_conv, gelu_back(normed, valid_mask * d_shared_in), 0.0)
        normalized_gradient = norm_scale * norm_gradient
        mean_term, slope_term = lax.psum(
            (jnp.sum(normalized_gradient, 0), jnp.sum(normalized_gradient * centered_values, 0)),
            "dp",
        )
        backward_d_hidden = (
            valid_mask
            * inverse_deviation
            * (
                normalized_gradient
                - mean_term / mask_count
                - centered_values * slope_term / mask_count
            )
        ).astype(jnp.bfloat16)
        backward_d_padded = padded_2(
            backward_d_hidden.reshape(rows_dev, columns, width), (("dp", 0),), 1
        )
        d_conv_in = lax.cond(is_conv, input_grad_fn, no_input_grad, backward_d_padded)
        updated["gain_sum"] = state["gain_sum"] + jnp.sum(norm_gradient * centered_values, 0)
        updated["bias_sum"] = state["bias_sum"] + jnp.sum(norm_gradient, 0)
        updated["input_grads"] = store_at(
            state["input_grads"],
            (valid_mask * d_conv_in).astype(jnp.bfloat16),
            slot,
            live & (rank_here == 0),
        )
        updated["grad_conv"] = state["grad_conv"] + lax.cond(
            is_conv, conv_weight_grad, no_conv_weight, backward_padded, backward_d_hidden
        )
        squeeze_piece, expand_piece = lax.cond(
            is_conv,
            no_gate_weight,
            attend_weight,
            backward_merged_low,
            backward_squeezed,
            backward_d_expanded,
            backward_d_squeezed,
        )
        updated["grad_squeeze"] = state["grad_squeeze"] + squeeze_piece
        updated["grad_expand"] = state["grad_expand"] + expand_piece
        shared_back = jnp.where(is_conv, d_conv_in, d_gate_total).astype(jnp.bfloat16)
        tasks_back = jnp.where(is_last, d_merged.astype(jnp.bfloat16), d_tasks_in)
        updated["back_shared"], updated["back_tasks"] = (
            passed_along(shared_back, "section", -1),
            passed_along(as_sent(tasks_back), "section", -1).astype(tasks_back.dtype),
        )
        state = updated
    grad_conv = state["grad_conv"]
    grad_squeeze = state["grad_squeeze"]
    grad_expand = state["grad_expand"]
    conv_part, squeeze_part, expand_part = (
        lax.psum_scatter(grad_conv, "dp", scatter_dimension=0, tiled=True),
        lax.psum_scatter(grad_squeeze, "dp", scatter_dimension=1, tiled=True),
        lax.psum_scatter(grad_expand, "dp", scatter_dimension=1, tiled=True),
    )
    layer_hit = jnp.arange(layers) == layer_here
    conv_grad, squeeze_grad, expand_grad = (
        lax.psum(
            jnp.where(layer_hit[:, None, None], conv_part[None], 0.0).astype(jnp.bfloat16),
            "section",
        ).astype(jnp.float32),
        lax.psum(
            jnp.where(layer_hit[:, None, None, None], squeeze_part[None], 0.0).astype(jnp.bfloat16),
            "section",
        ).astype(jnp.float32),
        lax.psum(
            jnp.where(layer_hit[:, None, None, None], expand_part[None], 0.0).astype(jnp.bfloat16),
            "section",
        ).astype(jnp.float32),
    )
    gain_grad, bias_grad = lax.psum(
        (
            jnp.where(layer_hit[:, None], state["gain_sum"][None], 0.0),
            jnp.where(layer_hit[:, None], state["bias_sum"][None], 0.0),
        ),
        ("section", "dp"),
    )
    share = micro // rank_count
    own_start = rank_here * share
    results = state["results"]
    input_grads = state["input_grads"]
    out_block = jnp.where(
        is_last,
        lax.dynamic_slice_in_dim(results, own_start, share, 0),
        jnp.zeros((share, tasks, pixels // 4, width), jnp.bfloat16),
    )
    grad_block = jnp.where(
        rank_here == 0,
        lax.dynamic_slice_in_dim(input_grads, own_start, share, 0),
        jnp.zeros((share, pixels, width), jnp.bfloat16),
    )
    for step in range(1, rank_count):
        target = (rank_here + step) % rank_count
        sent_out = lax.dynamic_slice_in_dim(results, target * share, share, 0)
        sent_grad = lax.dynamic_slice_in_dim(input_grads, target * share, share, 0)
        got_out, got_grad = (
            from_behind(as_sent(sent_out), "section", step).astype(sent_out.dtype),
            from_behind(as_sent(sent_grad), "section", step).astype(sent_grad.dtype),
        )
        source = (rank_here - step) % rank_count
        out_block = jnp.where(source == last_rank, got_out, out_block)
        grad_block = jnp.where(source == 0, got_grad, grad_block)
    return (out_block, grad_block, conv_grad, squeeze_grad, expand_grad, gain_grad, bias_grad)


def solution(mesh):
    placed = (
        P(None, "dp", None),
        P(None, "dp"),
        P(None, "dp", None),
        P(None, "dp", None),
        P(None, None, "dp", None),
        P(None, None, "dp", None),
        P(),
        P(),
        P(None, None, "dp", None),
    )
    return jax.shard_map(
        on_device,
        mesh=mesh,
        in_specs=placed,
        out_specs=(
            P("section", None, "dp", None),
            P("section", "dp", None),
            P(None, "dp", None),
            P(None, None, "dp", None),
            P(None, None, "dp", None),
            P(),
            P(),
        ),
        check_vma=False,
    )
```

profile of v0, /device:TPU:0, one launch (start us, length us, event | category | flops | bytes accessed | tf_op | source)
XLA Modules:
  0.0 2954.2 jit_solution(4518067326952642342)
XLA Ops:
  258.2 26.4 collective-permute-done.2
  312.7 90.6 %select_n.2374 = f32[4,3,768,512]{3,0,2,1:T(4,128)} dynamic-update-slice(f32[4,3,768,512]{3,0,2,1:T(4,128)} %broadcast_in_dim.1060, f32[1,3,768,512]{3,0,2,1:T(1,128)} %select_n.2373, s32[]{:T(128)S(6)} %min.43, s32[]{:T(128)} %constant.1074.clone.1, s32[]{:T(128)} %constant.1074.clone.1, s32[]{:T(128)} %constant.1074.clone.1) | dynamic-update-slice | bytes 9437188 | tf_op jit(solution)/shard_map/jit(_where)/select_n | solution.py:42
  415.8 27.9 conditional.36
  493.0 27.1 collective-permute-done.6
  530.0 90.7 %select_n.2378 = f32[4,3,768,512]{3,0,2,1:T(4,128)} dynamic-update-slice(f32[4,3,768,512]{3,0,2,1:T(4,128)} %select_n.2374, f32[1,3,768,512]{3,0,2,1:T(1,128)} %broadcast_select_fusion.5, s32[]{:T(128)S(6)} %min.44, s32[]{:T(128)} %constant.1074.clone.1, s32[]{:T(128)} %constant.1074.clone.1, s32[]{:T(128)} %constant.1074.clone.1) | dynamic-update-slice | bytes 9437188 | tf_op jit(solution)/shard_map/jit(_where)/select_n | solution.py:42
  633.1 19.8 conditional.37
  704.1 27.3 collective-permute-done.10
  741.4 90.7 %select_n.2382 = f32[4,3,768,512]{3,0,2,1:T(4,128)} dynamic-update-slice(f32[4,3,768,512]{3,0,2,1:T(4,128)} %select_n.2378, f32[1,3,768,512]{3,0,2,1:T(1,128)} %broadcast_select_fusion.4, s32[]{:T(128)S(6)} %min.45, s32[]{:T(128)} %constant.1074.clone.1, s32[]{:T(128)} %constant.1074.clone.1, s32[]{:T(128)} %constant.1074.clone.1) | dynamic-update-slice | bytes 9437188 | tf_op jit(solution)/shard_map/jit(_where)/select_n | solution.py:42
  844.7 19.9 conditional.38
  917.1 26.4 collective-permute-done.14
  953.2 90.7 %select_n.2386 = f32[4,3,768,512]{3,0,2,1:T(4,128)} dynamic-update-slice(f32[4,3,768,512]{3,0,2,1:T(4,128)} %select_n.2382, f32[1,3,768,512]{3,0,2,1:T(1,128)} %broadcast_select_fusion.3, s32[]{:T(128)S(6)} %min.46, s32[]{:T(128)} %constant.1074.clone.1, s32[]{:T(128)} %constant.1074.clone.1, s32[]{:T(128)} %constant.1074.clone.1) | dynamic-update-slice | bytes 9437188 | tf_op jit(solution)/shard_map/jit(_where)/select_n | solution.py:42
  1056.4 19.9 conditional.39
  1129.5 26.9 collective-permute-done.18
  1166.2 90.7 %select_n.2390 = f32[4,3,768,512]{3,0,2,1:T(4,128)} dynamic-update-slice(f32[4,3,768,512]{3,0,2,1:T(4,128)} %select_n.2386, f32[1,3,768,512]{3,0,2,1:T(1,128)} %broadcast_select_fusion.2, s32[]{:T(128)S(6)} %min.47, s32[]{:T(128)} %constant.1074.clone.1, s32[]{:T(128)} %constant.1074.clone.1, s32[]{:T(128)} %constant.1074.clone.1) | dynamic-update-slice | bytes 9437188 | tf_op jit(solution)/shard_map/jit(_where)/select_n | solution.py:42
  1268.9 19.8 conditional.40
  1341.3 27.4 collective-permute-done.22
  1377.7 90.8 %select_n.2394 = f32[4,3,768,512]{3,0,2,1:T(4,128)} dynamic-update-slice(f32[4,3,768,512]{3,0,2,1:T(4,128)} %select_n.2390, f32[1,3,768,512]{3,0,2,1:T(1,128)} %broadcast_select_fusion.1, s32[]{:T(128)S(6)} %min.48, s32[]{:T(128)} %constant.1074.clone.1, s32[]{:T(128)} %constant.1074.clone.1, s32[]{:T(128)} %constant.1074.clone.1) | dynamic-update-slice | bytes 9437188 | tf_op jit(solution)/shard_map/jit(_where)/select_n | solution.py:42
  1561.5 90.6 %select_n.2398 = f32[4,3,768,512]{3,0,2,1:T(4,128)} dynamic-update-slice(f32[4,3,768,512]{3,0,2,1:T(4,128)} %select_n.2394, f32[1,3,768,512]{3,0,2,1:T(1,128)} %broadcast_select_fusion, s32[]{:T(128)S(6)} %min.49, s32[]{:T(128)} %constant.1074.clone.1, s32[]{:T(128)} %constant.1074.clone.1, s32[]{:T(128)} %constant.1074.clone.1) | dynamic-update-slice | bytes 9437188 | tf_op jit(solution)/shard_map/jit(_where)/select_n | solution.py:42
  1664.1 69.5 %constant_dynamic-slice_fusion.9 = (f32[1,3,768,512]{3,0,2,1:T(1,128)}, f32[1,3,768,512]{3,0,2,1:T(1,128)}, f32[1,3,768,512]{3,0,2,1:T(1,128)}, f32[1,3,768,512]...) fusion(f32[4,3,768,512]{3,0,2,1:T(4,128)} %select_n.2398, ...), kind=kLoop, calls=%fused_computation.1557 | loop fusion | flops 5505024 | bytes 62914584 | tf_op jit(solution)/shard_map/jit(dynamic_index_in_dim)/dynamic_slice | solution.py:46
  1770.4 28.5 collective-permute-done.31
  1875.6 18.9 collective-permute-done.35
  1969.4 19.8 collective-permute-done.39
  2241.4 21.6 collective-permute-done.50
  2516.3 27.0 add_add_fusion.14
  2560.9 18.9 select_n.2128
  2597.6 18.9 select_n.2144
  2634.3 18.9 select_n.2157
  2671.3 18.9 select_n.2170
  2707.9 18.9 select_n.2183
  2744.6 18.9 select_n.2196
  2786.9 18.9 select_n.2209
  2874.4 66.3 %all-reduce.21 = (f32[2,512]{1,0:T(2,128)}, f32[2,512]{1,0:T(2,128)}) all-reduce(f32[2,512]{1,0:T(2,128)S(1)} %get-tuple-element.1751, f32[2,512]{1,0:T(2,128)S(1)} %get-tuple-element.1750), channel_id=1, replica_groups=mesh['section'=4,'dp'=8] {'section','dp'}, use_global_device_ids=true, to_apply=%region_165.166 | all-reduce | flops 2048 | bytes 16384 | tf_op jit(solution)/shard_map/psum | solution.py:435
  (1337 shorter events, 1992.8 us)
Async XLA Ops:
  7.2 185.3 %all-gather.5.cloned.1.call-start = ((), (), s32[]{:S(2)}) async-start(), calls=%async_computation.6 | async-start | bytes 5308416 | tf_op jit(solution)/shard_map/all_gather | solution.py:168
  12.2 177.9 %collective-permute-start.1 = (bf16[1,384,512]{2,1,0:T(8,128)(2,1)}, bf16[1,384,512]{2,1,0:T(8,128)(2,1)}, u32[]{:S(2)}, u32[]{:S(2)}) collective-permute-start(bf16[1,384,512]{2,1,0:T(8,128)(2,1)} %get-tuple-element.1695), channel_id=1, source_target_pairs={{1,0},{2,1},{3,2},{4,3},{5,4},{6,5},{7,6},{9,8},{10,9},{11,10},{12... | collective-permute-start | bytes 1179656 | tf_op jit(solution)/shard_map/ppermute | solution.py:21
  13.5 176.6 %collective-permute-start = (bf16[1,384,512]{2,1,0:T(8,128)(2,1)}, bf16[1,384,512]{2,1,0:T(8,128)(2,1)}, u32[]{:S(2)}, u32[]{:S(2)}) collective-permute-start(bf16[1,384,512]{2,1,0:T(8,128)(2,1)} %get-tuple-element.1694), channel_id=1, source_target_pairs={{0,1},{1,2},{2,3},{3,4},{4,5},{5,6},{6,7},{8,9},{9,10},{10,11},{11... | collective-permute-start | bytes 1179656 | tf_op jit(solution)/shard_map/ppermute | solution.py:20
  18.2 2826.6 %reduce-scatter.6.cloned.1.call-start = ((), (), s32[]{:S(2)}) async-start(), calls=%async_computation.4 | async-start | bytes 884736 | tf_op jit(solution)/shard_map/reduce_scatter | solution.py:417
  215.0 198.5 %collective-permute-start.3 = (bf16[3,768,512]{2,1,0:T(8,128)(2,1)}, bf16[3,768,512]{2,1,0:T(8,128)(2,1)}, u32[]{:S(2)}, u32[]{:S(2)}) collective-permute-start(bf16[3,768,512]{2,1,0:T(8,128)(2,1)} %get-tuple-element.1393), channel_id=1, source_target_pairs={{0,8},{8,16},{16,24},{1,9},{9,17},{17,25},{2,10},{10,18},{18,26},{... | collective-permute-start | bytes 7077896 | tf_op jit(solution)/shard_map/ppermute | solution.py:29
  288.2 119.8 %collective-permute-start.5 = (bf16[1,384,512]{2,1,0:T(8,128)(2,1)}, bf16[1,384,512]{2,1,0:T(8,128)(2,1)S(1)}, u32[]{:S(2)}, u32[]{:S(2)}) collective-permute-start(bf16[1,384,512]{2,1,0:T(8,128)(2,1)} %get-tuple-element.1693), channel_id=1, source_target_pairs={{1,0},{2,1},{3,2},{4,3},{5,4},{6,5},{7,6},{9,8},{10,9},{11,10},{12... | collective-permute-start | bytes 1179656 | tf_op jit(solution)/shard_map/ppermute | solution.py:21
  289.5 118.5 %collective-permute-start.4 = (bf16[1,384,512]{2,1,0:T(8,128)(2,1)}, bf16[1,384,512]{2,1,0:T(8,128)(2,1)}, u32[]{:S(2)}, u32[]{:S(2)}) collective-permute-start(bf16[1,384,512]{2,1,0:T(8,128)(2,1)} %get-tuple-element.1692), channel_id=1, source_target_pairs={{0,1},{1,2},{2,3},{3,4},{4,5},{5,6},{6,7},{8,9},{9,10},{10,11},{11... | collective-permute-start | bytes 1179656 | tf_op jit(solution)/shard_map/ppermute | solution.py:20
  450.4 180.5 %collective-permute-start.7 = (bf16[3,768,512]{2,1,0:T(8,128)(2,1)}, bf16[3,768,512]{2,1,0:T(8,128)(2,1)}, u32[]{:S(2)}, u32[]{:S(2)}) collective-permute-start(bf16[3,768,512]{2,1,0:T(8,128)(2,1)} %get-tuple-element.1389), channel_id=1, source_target_pairs={{0,8},{8,16},{16,24},{1,9},{9,17},{17,25},{2,10},{10,18},{18,26},{... | collective-permute-start | bytes 7077896 | tf_op jit(solution)/shard_map/ppermute | solution.py:29
  522.7 102.9 %collective-permute-start.9 = (bf16[1,384,512]{2,1,0:T(8,128)(2,1)}, bf16[1,384,512]{2,1,0:T(8,128)(2,1)S(1)}, u32[]{:S(2)}, u32[]{:S(2)}) collective-permute-start(bf16[1,384,512]{2,1,0:T(8,128)(2,1)} %get-tuple-element.1691), channel_id=1, source_target_pairs={{1,0},{2,1},{3,2},{4,3},{5,4},{6,5},{7,6},{9,8},{10,9},{11,10},{12... | collective-permute-start | bytes 1179656 | tf_op jit(solution)/shard_map/ppermute | solution.py:21
  524.0 101.6 %collective-permute-start.8 = (bf16[1,384,512]{2,1,0:T(8,128)(2,1)}, bf16[1,384,512]{2,1,0:T(8,128)(2,1)}, u32[]{:S(2)}, u32[]{:S(2)}) collective-permute-start(bf16[1,384,512]{2,1,0:T(8,128)(2,1)} %get-tuple-element.1690), channel_id=1, source_target_pairs={{0,1},{1,2},{2,3},{3,4},{4,5},{5,6},{6,7},{8,9},{9,10},{10,11},{11... | collective-permute-start | bytes 1179656 | tf_op jit(solution)/shard_map/ppermute | solution.py:20
  659.6 182.8 %collective-permute-start.11 = (bf16[3,768,512]{2,1,0:T(8,128)(2,1)}, bf16[3,768,512]{2,1,0:T(8,128)(2,1)}, u32[]{:S(2)}, u32[]{:S(2)}) collective-permute-start(bf16[3,768,512]{2,1,0:T(8,128)(2,1)} %get-tuple-element.1385), channel_id=1, source_target_pairs={{0,8},{8,16},{16,24},{1,9},{9,17},{17,25},{2,10},{10,18},{18,26},{... | collective-permute-start | bytes 7077896 | tf_op jit(solution)/shard_map/ppermute | solution.py:29
  733.9 103.1 %collective-permute-start.13 = (bf16[1,384,512]{2,1,0:T(8,128)(2,1)}, bf16[1,384,512]{2,1,0:T(8,128)(2,1)S(1)}, u32[]{:S(2)}, u32[]{:S(2)}) collective-permute-start(bf16[1,384,512]{2,1,0:T(8,128)(2,1)} %get-tuple-element.1689), channel_id=1, source_target_pairs={{1,0},{2,1},{3,2},{4,3},{5,4},{6,5},{7,6},{9,8},{10,9},{11,10},{12... | collective-permute-start | bytes 1179656 | tf_op jit(solution)/shard_map/ppermute | solution.py:21
  735.2 101.8 %collective-permute-start.12 = (bf16[1,384,512]{2,1,0:T(8,128)(2,1)}, bf16[1,384,512]{2,1,0:T(8,128)(2,1)}, u32[]{:S(2)}, u32[]{:S(2)}) collective-permute-start(bf16[1,384,512]{2,1,0:T(8,128)(2,1)} %get-tuple-element.1688), channel_id=1, source_target_pairs={{0,1},{1,2},{2,3},{3,4},{4,5},{5,6},{6,7},{8,9},{9,10},{10,11},{11... | collective-permute-start | bytes 1179656 | tf_op jit(solution)/shard_map/ppermute | solution.py:20
  871.3 182.9 %collective-permute-start.15 = (bf16[3,768,512]{2,1,0:T(8,128)(2,1)}, bf16[3,768,512]{2,1,0:T(8,128)(2,1)}, u32[]{:S(2)}, u32[]{:S(2)}) collective-permute-start(bf16[3,768,512]{2,1,0:T(8,128)(2,1)} %get-tuple-element.1381), channel_id=1, source_target_pairs={{0,8},{8,16},{16,24},{1,9},{9,17},{17,25},{2,10},{10,18},{18,26},{... | collective-permute-start | bytes 7077896 | tf_op jit(solution)/shard_map/ppermute | solution.py:29
  945.9 102.9 %collective-permute-start.17 = (bf16[1,384,512]{2,1,0:T(8,128)(2,1)}, bf16[1,384,512]{2,1,0:T(8,128)(2,1)S(1)}, u32[]{:S(2)}, u32[]{:S(2)}) collective-permute-start(bf16[1,384,512]{2,1,0:T(8,128)(2,1)} %get-tuple-element.1687), channel_id=1, source_target_pairs={{1,0},{2,1},{3,2},{4,3},{5,4},{6,5},{7,6},{9,8},{10,9},{11,10},{12... | collective-permute-start | bytes 1179656 | tf_op jit(solution)/shard_map/ppermute | solution.py:21
  947.2 101.6 %collective-permute-start.16 = (bf16[1,384,512]{2,1,0:T(8,128)(2,1)}, bf16[1,384,512]{2,1,0:T(8,128)(2,1)}, u32[]{:S(2)}, u32[]{:S(2)}) collective-permute-start(bf16[1,384,512]{2,1,0:T(8,128)(2,1)} %get-tuple-element.1686), channel_id=1, source_target_pairs={{0,1},{1,2},{2,3},{3,4},{4,5},{5,6},{6,7},{8,9},{9,10},{10,11},{11... | collective-permute-start | bytes 1179656 | tf_op jit(solution)/shard_map/ppermute | solution.py:20
  1083.0 183.6 %collective-permute-start.19 = (bf16[3,768,512]{2,1,0:T(8,128)(2,1)}, bf16[3,768,512]{2,1,0:T(8,128)(2,1)}, u32[]{:S(2)}, u32[]{:S(2)}) collective-permute-start(bf16[3,768,512]{2,1,0:T(8,128)(2,1)} %get-tuple-element.1377), channel_id=1, source_target_pairs={{0,8},{8,16},{16,24},{1,9},{9,17},{17,25},{2,10},{10,18},{18,26},{... | collective-permute-start | bytes 7077896 | tf_op jit(solution)/shard_map/ppermute | solution.py:29
  1158.9 102.3 %collective-permute-start.21 = (bf16[1,384,512]{2,1,0:T(8,128)(2,1)}, bf16[1,384,512]{2,1,0:T(8,128)(2,1)S(1)}, u32[]{:S(2)}, u32[]{:S(2)}) collective-permute-start(bf16[1,384,512]{2,1,0:T(8,128)(2,1)} %get-tuple-element.1685), channel_id=1, source_target_pairs={{1,0},{2,1},{3,2},{4,3},{5,4},{6,5},{7,6},{9,8},{10,9},{11,10},{12... | collective-permute-start | bytes 1179656 | tf_op jit(solution)/shard_map/ppermute | solution.py:21
  1160.2 101.1 %collective-permute-start.20 = (bf16[1,384,512]{2,1,0:T(8,128)(2,1)}, bf16[1,384,512]{2,1,0:T(8,128)(2,1)}, u32[]{:S(2)}, u32[]{:S(2)}) collective-permute-start(bf16[1,384,512]{2,1,0:T(8,128)(2,1)} %get-tuple-element.1684), channel_id=1, source_target_pairs={{0,1},{1,2},{2,3},{3,4},{4,5},{5,6},{6,7},{8,9},{9,10},{10,11},{11... | collective-permute-start | bytes 1179656 | tf_op jit(solution)/shard_map/ppermute | solution.py:20
  1295.3 187.2 %collective-permute-start.23 = (bf16[3,768,512]{2,1,0:T(8,128)(2,1)}, bf16[3,768,512]{2,1,0:T(8,128)(2,1)}, u32[]{:S(2)}, u32[]{:S(2)}) collective-permute-start(bf16[3,768,512]{2,1,0:T(8,128)(2,1)} %get-tuple-element.1373), channel_id=1, source_target_pairs={{0,8},{8,16},{16,24},{1,9},{9,17},{17,25},{2,10},{10,18},{18,26},{... | collective-permute-start | bytes 7077896 | tf_op jit(solution)/shard_map/ppermute | solution.py:29
  1372.1 100.7 %collective-permute-start.25 = (bf16[1,384,512]{2,1,0:T(8,128)(2,1)}, bf16[1,384,512]{2,1,0:T(8,128)(2,1)S(1)}, u32[]{:S(2)}, u32[]{:S(2)}) collective-permute-start(bf16[1,384,512]{2,1,0:T(8,128)(2,1)} %get-tuple-element.1683), channel_id=1, source_target_pairs={{1,0},{2,1},{3,2},{4,3},{5,4},{6,5},{7,6},{9,8},{10,9},{11,10},{12... | collective-permute-start | bytes 1179656 | tf_op jit(solution)/shard_map/ppermute | solution.py:21
  1373.4 99.5 %collective-permute-start.24 = (bf16[1,384,512]{2,1,0:T(8,128)(2,1)}, bf16[1,384,512]{2,1,0:T(8,128)(2,1)}, u32[]{:S(2)}, u32[]{:S(2)}) collective-permute-start(bf16[1,384,512]{2,1,0:T(8,128)(2,1)} %get-tuple-element.1682), channel_id=1, source_target_pairs={{0,1},{1,2},{2,3},{3,4},{4,5},{5,6},{6,7},{8,9},{9,10},{10,11},{11... | collective-permute-start | bytes 1179656 | tf_op jit(solution)/shard_map/ppermute | solution.py:20
  1545.9 198.6 %collective-permute-start.30 = (bf16[1,384,512]{2,1,0:T(8,128)(2,1)}, bf16[1,384,512]{2,1,0:T(8,128)(2,1)}, u32[]{:S(2)}, u32[]{:S(2)}) collective-permute-start(bf16[1,384,512]{2,1,0:T(8,128)(2,1)} %get-tuple-element.1681), channel_id=1, source_target_pairs={{1,0},{2,1},{3,2},{4,3},{5,4},{6,5},{7,6},{9,8},{10,9},{11,10},{12... | collective-permute-start | bytes 1179656 | tf_op jit(solution)/shard_map/ppermute | solution.py:21
  1547.2 197.3 %collective-permute-start.29 = (bf16[1,384,512]{2,1,0:T(8,128)(2,1)}, bf16[1,384,512]{2,1,0:T(8,128)(2,1)}, u32[]{:S(2)}, u32[]{:S(2)}) collective-permute-start(bf16[1,384,512]{2,1,0:T(8,128)(2,1)} %get-tuple-element.1680), channel_id=1, source_target_pairs={{0,1},{1,2},{2,3},{3,4},{4,5},{5,6},{6,7},{8,9},{9,10},{10,11},{11... | collective-permute-start | bytes 1179656 | tf_op jit(solution)/shard_map/ppermute | solution.py:20
  1963.7 114.2 %collective-permute-start.42 = (bf16[3,768,512]{2,1,0:T(8,128)(2,1)}, bf16[3,768,512]{2,1,0:T(8,128)(2,1)}, u32[]{:S(2)}, u32[]{:S(2)}) collective-permute-start(bf16[3,768,512]{2,1,0:T(8,128)(2,1)} %broadcast_select_fusion.75), channel_id=1, source_target_pairs={{8,0},{16,8},{24,16},{9,1},{17,9},{25,17},{10,2},{18,10},{26,18},{... | collective-permute-start | bytes 7077896 | tf_op jit(solution)/shard_map/ppermute | solution.py:29
  2299.2 176.1 %collective-permute-start.51 = (bf16[768,512]{1,0:T(8,128)(2,1)}, bf16[768,512]{1,0:T(8,128)(2,1)}, u32[]{:S(2)}, u32[]{:S(2)}) collective-permute-start(bf16[768,512]{1,0:T(8,128)(2,1)} %fusion.742), channel_id=1, source_target_pairs={{8,0},{16,8},{24,16},{9,1},{17,9},{25,17},{10,2},{18,10},{26,18},{... | collective-permute-start | bytes 2359304 | tf_op jit(solution)/shard_map/ppermute | solution.py:29
  2356.1 490.3 %reduce-scatter.8.cloned.1.call-start = ((), (), s32[]{:S(2)}) async-start(), calls=%async_computation.5 | async-start | bytes 884736 | tf_op jit(solution)/shard_map/reduce_scatter | solution.py:418
  2516.3 331.7 %reduce-scatter.4.cloned.1.call-start = ((), (), s32[]{:S(2)}) async-start(), calls=%async_computation.3 | async-start | bytes 10616832 | tf_op jit(solution)/shard_map/reduce_scatter | solution.py:416
  2543.4 399.5 %all-reduce.39.cloned.1.call-start = ((), (), s32[]{:S(2)}) async-start(), calls=%async_computation.7 | async-start | bytes 2752512 | tf_op jit(solution)/shard_map/psum | solution.py:422
  2843.4 97.3 %collective-permute-start.54 = (bf16[1,768,512]{2,1,0:T(8,128)(2,1)}, bf16[1,768,512]{2,1,0:T(8,128)(2,1)S(1)}, u32[]{:S(2)}, u32[]{:S(2)}) collective-permute-start(bf16[1,768,512]{2,1,0:T(8,128)(2,1)} %get-tuple-element.1655), channel_id=1, source_target_pairs={{0,24},{8,0},{16,8},{24,16},{1,25},{9,1},{17,9},{25,17},{2,26},{10... | collective-permute-start | bytes 2359304 | tf_op jit(solution)/shard_map/ppermute | solution.py:34
  2843.4 97.3 %collective-permute-start.55 = (bf16[1,768,512]{2,1,0:T(8,128)(2,1)}, bf16[1,768,512]{2,1,0:T(8,128)(2,1)}, u32[]{:S(2)}, u32[]{:S(2)}) collective-permute-start(bf16[1,768,512]{2,1,0:T(8,128)(2,1)} %get-tuple-element.1654), channel_id=1, source_target_pairs={{0,16},{8,24},{16,0},{24,8},{1,17},{9,25},{17,1},{25,9},{2,18},{10... | collective-permute-start | bytes 2359304 | tf_op jit(solution)/shard_map/ppermute | solution.py:34
  2850.6 90.1 %collective-permute-start.56 = (bf16[1,768,512]{2,1,0:T(8,128)(2,1)}, bf16[1,768,512]{2,1,0:T(8,128)(2,1)}, u32[]{:S(2)}, u32[]{:S(2)}) collective-permute-start(bf16[1,768,512]{2,1,0:T(8,128)(2,1)} %get-tuple-element.1653), channel_id=1, source_target_pairs={{0,8},{8,16},{16,24},{24,0},{1,9},{9,17},{17,25},{25,1},{2,10},{10... | collective-permute-start | bytes 2359304 | tf_op jit(solution)/shard_map/ppermute | solution.py:34
  (308 other events, 4943.4 us)
Sparse Core Ops, SparseCore 0:
  18.3 54.4 all-gather.4
  2356.2 95.7 reduce-scatter.5
  2516.4 28.0 reduce-scatter.7
  2546.7 97.7 reduce-scatter.3
  2850.7 86.8 all-reduce.38
where the time goes:
time: 3000 us; the launch traced here: 2950 us
  local copies, waits for them, and re-layouts  1200 us (40%)
  other arithmetic  756 us (25%)
  waiting for transfers between devices  310 us (10%)
  blocking collectives  299 us (10%)
  matrix products  180 us (6%)
  starting transfers between devices  169 us (6%)
    select_n x31, local copies, waits for them, and re-layouts, store_at(): jnp.where(live, lax.dynamic_update_index_in_dim(buffer, value, where_idx,...  783 us
    ppermute x24, waiting for transfers between devices, passed_along(): return lax.ppermute(value, axis, pairs)  293 us
    select_n x68, other arithmetic, store_at(): jnp.where(live, lax.dynamic_update_index_in_dim(buffer, value, where_idx,...  239 us
    psum x7, blocking collectives, on_device(): lax.psum((jnp.sum(forward_valid_mask * forward_hidden, 0), jnp.sum(forwar...  106 us
    dot_general x63, matrix products, conv_weight_grad(): lax.dot_general(piece, d_hidden, (((0,), (0,)), ((), ())), preferred_elem...  101 us
    psum x7, blocking collectives, on_device(): lax.psum((jnp.sum(normalized_gradient, 0), jnp.sum(normalized_gradient *...  96.4 us
    ppermute x24, starting transfers between devices, passed_along(): return lax.ppermute(value, axis, pairs)  93.5 us
    select_n x11, local copies, waits for them, and re-layouts, on_device(): jnp.where(is_last, spread_seed, 0.0)  70.3 us
  transfers between devices with their start and end apart: 63, of which 18 were waited for; matrix products, arithmetic and copies ran while one was open for 62% of the time, Pallas kernels for 0%

commit v1 on v0

v1 whole, which is shorter than its diff:
```python
import jax
import jax.numpy as jnp
from jax import lax
from jax.sharding import PartitionSpec as P

EPS = 1e-05
BF16 = jnp.bfloat16
F32 = jnp.float32


def gelu_back(point, upstream):
    return jax.vjp(jax.nn.gelu, point)[1](upstream)[0]


def with_halo(value, axis):
    size = lax.axis_size(axis)
    up = [(i, i + 1) for i in range(size - 1)]
    down = [(j, i) for i, j in up]
    before = lax.ppermute(value[-1:], axis, up)
    after = lax.ppermute(value[:1], axis, down)
    return jnp.concatenate([before, value, after], axis=0)


def conv(padded, taps):
    out = lax.conv_general_dilated(
        padded[None],
        taps,
        (1, 1),
        ((0, 0), (1, 1)),
        dimension_numbers=("NHWC", "HWIO", "NHWC"),
        preferred_element_type=F32,
    )
    return out.reshape(-1, out.shape[-1])


def conv_input_grad(d_padded, taps):
    out = lax.conv_general_dilated(
        d_padded[None],
        taps[::-1, ::-1],
        (1, 1),
        ((0, 0), (1, 1)),
        dimension_numbers=("NHWC", "HWOI", "NHWC"),
        preferred_element_type=F32,
    )
    return out.reshape(-1, out.shape[-1])


def conv_weight_grad(padded, d_hidden):
    out = lax.conv_general_dilated(
        padded[None],
        d_hidden[None],
        (1, 1),
        ((0, 0), (1, 1)),
        dimension_numbers=("CHWN", "IHWO", "HWNC"),
        preferred_element_type=F32,
    )
    return out.reshape(-1, out.shape[-1])


def gate_forward(source, w_squeeze, w_expand):
    squeezed = jnp.einsum("tpc,tcb->tpb", source, w_squeeze, preferred_element_type=F32)
    excited = jax.nn.gelu(squeezed).astype(BF16)
    expanded = jnp.einsum("tpb,tbc->tpc", excited, w_expand, preferred_element_type=F32)
    return squeezed, excited, jax.nn.sigmoid(expanded)


def gate_backward(d_task, field, source, squeezed, excited, gate_val, w_squeeze, w_expand):
    d_expanded = (d_task * field[None] * gate_val * (1.0 - gate_val)).astype(BF16)
    d_excited = jnp.einsum("tpc,tbc->tpb", d_expanded, w_expand, preferred_element_type=F32)
    d_squeezed = gelu_back(squeezed, d_excited).astype(BF16)
    d_source = jnp.einsum("tpb,tcb->tpc", d_squeezed, w_squeeze, preferred_element_type=F32)
    grad_squeeze = jnp.einsum("tpc,tpb->tcb", source, d_squeezed, preferred_element_type=F32)
    grad_expand = jnp.einsum("tpb,tpc->tbc", excited, d_expanded, preferred_element_type=F32)
    return d_source, grad_squeeze, grad_expand


def pool_pick(field, pick):
    tasks, _, width = field.shape
    half_rows, half_columns = pick.shape
    windows = field.reshape(tasks, half_rows, 2, half_columns, 2, width)
    picked = jnp.zeros((tasks, half_rows, half_columns, width), F32)
    for corner in range(4):
        hit = (pick == corner)[None, :, :, None]
        picked = picked + jnp.where(hit, windows[:, :, corner // 2, :, corner % 2, :], 0.0)
    return picked.reshape(tasks, half_rows * half_columns, width)


def pool_spread(d_pooled, pick):
    tasks, _, width = d_pooled.shape
    half_rows, half_columns = pick.shape
    grid = d_pooled.reshape(tasks, half_rows, half_columns, width)
    rows = [
        jnp.stack(
            [jnp.where((pick == 2 * dy + dx)[None, :, :, None], grid, 0.0) for dx in range(2)], 3
        )
        for dy in range(2)
    ]
    return jnp.stack(rows, 2).reshape(tasks, half_rows * 2 * half_columns * 2, width)


def on_device(images, counts, pool_index, conv_w, squeeze_w, expand_w, gain, bias, cotangent):
    sections = lax.axis_size("section")
    here = lax.axis_index("section")
    micro, pixels, width = images.shape
    layers = conv_w.shape[0]
    tasks = squeeze_w.shape[1]
    rows = 2 * pool_index.shape[1]
    columns = 2 * pool_index.shape[2]
    share = micro // sections

    def own(value):
        return lax.dynamic_slice_in_dim(value, here * share, share, 0)

    images, counts, pool_index, cotangent = (
        own(images),
        own(counts),
        own(pool_index),
        own(cotangent),
    )

    def gather(value, axis):
        return lax.all_gather(value.astype(BF16), "dp", axis=axis, tiled=True)

    taps = [gather(conv_w[l], 0).reshape(3, 3, width, width) for l in range(layers)]
    w_squeeze = [gather(squeeze_w[l], 1) for l in range(layers)]
    w_expand = [gather(expand_w[l], 1) for l in range(layers)]
    slots = jnp.arange(pixels, dtype=jnp.int32)[:, None]

    def block_forward(field, mask, total, layer):
        padded = with_halo(field.reshape(rows, columns, width), "dp")
        hidden = conv(padded, taps[layer])
        sums = lax.psum(
            jnp.stack([jnp.sum(mask * hidden, 0), jnp.sum(mask * hidden * hidden, 0)]), "dp"
        )
        centre = sums[0] / total
        inverse = lax.rsqrt(sums[1] / total - centre * centre + EPS)
        normed = gain[layer] * (hidden - centre) * inverse + bias[layer]
        out = (mask * jax.nn.gelu(normed)).astype(BF16)
        return out, (padded, hidden, centre, inverse)

    def block_backward(d_out, kept, mask, total, layer):
        padded, hidden, centre, inverse = kept
        centred = (hidden - centre) * inverse
        normed = gain[layer] * (hidden - centre) * inverse + bias[layer]
        d_norm = gelu_back(normed, mask * d_out)
        gain_sum = jnp.sum(d_norm * centred, 0)
        bias_sum = jnp.sum(d_norm, 0)
        sums = gain[layer] * lax.psum(jnp.stack([bias_sum, gain_sum]), "dp")
        d_hidden = (
            mask * inverse * (gain[layer] * d_norm - sums[0] / total - centred * sums[1] / total)
        ).astype(BF16)
        d_hidden = d_hidden.reshape(rows, columns, width)
        d_x = conv_input_grad(with_halo(d_hidden, "dp"), taps[layer])
        return d_x, conv_weight_grad(padded, d_hidden), gain_sum, bias_sum

    outs, image_grads = [], []
    grads = None
    totals = lax.psum(counts[:, 0], "dp").astype(F32)
    for m in range(share):
        total = totals[m]
        mask = (slots < counts[m, 0]).astype(F32)
        first_in = jnp.where(slots < counts[m, 0], images[m], jnp.zeros((), BF16))
        f1, kept_0 = block_forward(first_in, mask, total, 0)
        f1_f = f1.astype(F32)
        source_0 = jnp.broadcast_to(f1[None], (tasks, pixels, width))
        squeezed_0, excited_0, gate_0 = gate_forward(source_0, w_squeeze[0], w_expand[0])
        t1 = (mask[None] * gate_0 * f1_f[None]).astype(BF16)
        f2, kept_1 = block_forward(f1, mask, total, 1)
        f2_f = f2.astype(F32)
        source_1 = (f2_f[None] + t1.astype(F32)).astype(BF16)
        squeezed_1, excited_1, gate_1 = gate_forward(source_1, w_squeeze[1], w_expand[1])
        outs.append(pool_pick(mask[None] * gate_1 * f2_f[None], pool_index[m]).astype(BF16))

        d_task = pool_spread(cotangent[m].astype(F32), pool_index[m])
        d_source, gs_1, ge_1 = gate_backward(
            d_task, mask * f2_f, source_1, squeezed_1, excited_1, gate_1, w_squeeze[1], w_expand[1]
        )
        d_f2 = (jnp.sum(d_source, 0) + mask * jnp.sum(d_task * gate_1, 0)).astype(BF16)
        d_t1 = d_source.astype(BF16).astype(F32)
        d_x1, gc_1, gain_1, bias_1 = block_backward(d_f2.astype(F32), kept_1, mask, total, 1)
        d_source, gs_0, ge_0 = gate_backward(
            d_t1, mask * f1_f, source_0, squeezed_0, excited_0, gate_0, w_squeeze[0], w_expand[0]
        )
        d_f1 = (
            d_x1.astype(BF16).astype(F32)
            + jnp.sum(d_source, 0)
            + mask * jnp.sum(d_t1 * gate_0, 0)
        ).astype(BF16)
        d_x0, gc_0, gain_0, bias_0 = block_backward(d_f1.astype(F32), kept_0, mask, total, 0)
        image_grads.append((mask * d_x0).astype(BF16))
        here_grads = [
            [gc_0, gc_1],
            [gs_0, gs_1],
            [ge_0, ge_1],
            jnp.stack([gain_0, gain_1]),
            jnp.stack([bias_0, bias_1]),
        ]
        grads = here_grads if grads is None else jax.tree.map(jnp.add, grads, here_grads)

    def reduced(value, axis):
        part = lax.psum_scatter(value, "dp", scatter_dimension=axis, tiled=True)
        return lax.psum(part.astype(BF16), "section").astype(F32)

    conv_grad = jnp.stack([reduced(g, 0) for g in grads[0]])
    squeeze_grad = jnp.stack([reduced(g, 1) for g in grads[1]])
    expand_grad = jnp.stack([reduced(g, 1) for g in grads[2]])
    gain_grad, bias_grad = lax.psum((grads[3], grads[4]), ("section", "dp"))
    return (
        jnp.stack(outs),
        jnp.stack(image_grads),
        conv_grad,
        squeeze_grad,
        expand_grad,
        gain_grad,
        bias_grad,
    )


def solution(mesh):
    placed = (
        P(None, "dp", None),
        P(None, "dp"),
        P(None, "dp", None),
        P(None, "dp", None),
        P(None, None, "dp", None),
        P(None, None, "dp", None),
        P(),
        P(),
        P(None, None, "dp", None),
    )
    return jax.shard_map(
        on_device,
        mesh=mesh,
        in_specs=placed,
        out_specs=(
            P("section", None, "dp", None),
            P("section", "dp", None),
            P(None, "dp", None),
            P(None, None, "dp", None),
            P(None, None, "dp", None),
            P(),
            P(),
        ),
        check_vma=False,
    )
```

time: 3000 us -> 680 us (0.23); the launches traced: 2950 us -> 671 us
  local copies, waits for them, and re-layouts: 1200 us -> 73.9 us
  other arithmetic: 756 us -> 66.1 us
  starting transfers between devices: 169 us -> 19.9 us
  waiting for transfers between devices: 310 us -> 201 us
  blocking collectives: 299 us -> 193 us
  matrix products: 180 us -> 101 us
    select_n x44 -> x0, local copies, waits for them, and re-layouts: 855 us -> none  [the longest x31 783 us: store_at(): jnp.where(live, lax.dynamic_update_index_in_dim(buffer, value, where_idx,...]
    select_n x101 -> x3, other arithmetic: 376 us -> 2.98 us  [the longest x2 1.53 us: on_device(): first_in = jnp.where(slots < counts[m, 0], images[m], jnp.zeros((), BF16))]
    ppermute x58 -> x8, waiting for transfers between devices: 310 us -> 0.02 us  [the longest x4 0.01 us: with_halo(): before = lax.ppermute(value[-1:], axis, up)]
    psum x15 -> x6, blocking collectives: 269 us -> 110 us  [the longest x1 40.9 us: on_device(): gain_grad, bias_grad = lax.psum((grads[3], grads[4]), ('section', 'dp'))]
    ppermute x58 -> x8, starting transfers between devices: 169 us -> 18.6 us  [the longest x4 13.3 us: with_halo(): before = lax.ppermute(value[-1:], axis, up)]
    dot_general x189 -> x12, matrix products: 180 us -> 33.9 us  [the longest x2 11.1 us: gate_forward(): jnp.einsum('tpb,tbc->tpc', excited, w_expand, preferred_element_type=F32)]
    reduce_scatter x3 -> x6, waiting for transfers between devices: 0.01 us -> 111 us  [reduced(): part = lax.psum_scatter(value, 'dp', scatter_dimension=axis, tiled=True)]
    convert_element_type x55 -> x10, other arithmetic: 121 us -> 15 us  [the longest x4 9.19 us: block_backward(): d_hidden = (mask * inverse * (gain[layer] * d_norm - sums[0] / total - ce...]
  transfers between devices with their start and end apart: 63 -> 18, of which waited for: 18 -> 4; matrix products, arithmetic and copies ran while one was open for 62% -> 30% of each run, Pallas kernels for 0% -> 0%
where the time goes in v1:
time: 680 us; the launch traced here: 671 us
  waiting for transfers between devices  201 us (30%)
  blocking collectives  193 us (28%)
  matrix products  101 us (15%)
  local copies, waits for them, and re-layouts  73.9 us (11%)
  other arithmetic  66.1 us (10%)
  starting transfers between devices  19.9 us (3%)
  between operations  16.7 us (2%)
    reduce_scatter x6, waiting for transfers between devices, reduced(): part = lax.psum_scatter(value, 'dp', scatter_dimension=axis, tiled=True)  111 us
    psum x2, waiting for transfers between devices, reduced(): return lax.psum(part.astype(BF16), 'section').astype(F32)  88.4 us
    all_gather x4, blocking collectives, gather(): return lax.all_gather(value.astype(BF16), 'dp', axis=axis, tiled=True)  83.1 us
    conv_general_dilated x2, matrix products, conv_weight_grad(): lax.conv_general_dilated(padded[None], d_hidden[None], (1, 1), ((0, 0), (...  44.8 us
    psum x1, blocking collectives, on_device(): gain_grad, bias_grad = lax.psum((grads[3], grads[4]), ('section', 'dp'))  40.9 us
    psum x2, blocking collectives, block_forward(): lax.psum(jnp.stack([jnp.sum(mask * hidden, 0), jnp.sum(mask * hidden * hi...  30.1 us
    psum x2, blocking collectives, block_backward(): sums = gain[layer] * lax.psum(jnp.stack([bias_sum, gain_sum]), 'dp')  28.2 us
    unnamed x188, local copies, waits for them, and re-layouts  15.8 us
  transfers between devices with their start and end apart: 18, of which 4 were waited for; matrix products, arithmetic and copies ran while one was open for 30% of the time, Pallas kernels for 0%

profile of v1, /device:TPU:0, one launch (start us, length us, event | category | flops | bytes accessed | tf_op | source)
XLA Modules:
  0.0 671.1 jit_solution(6705946956987874592)
XLA Ops:
  19.6 34.6 %all-gather.5 = bf16[1,3,128,512]{3,2,1,0:T(8,128)(2,1)} all-gather(bf16[1,3,16,512]{3,2,1,0:T(8,128)(2,1)S(1)} %get-tuple-element.75), channel_id=7, replica_groups=mesh['section'=4,'dp'=8] {'dp'}, dimensions={2}, use_global_device_ids=true | all-gather | bytes 442368 | tf_op jit(solution)/shard_map/all_gather | solution.py:122
  54.2 17.0 %all-gather.3 = bf16[1,3,128,512]{3,2,1,0:T(8,128)(2,1)} all-gather(bf16[1,3,16,512]{3,2,1,0:T(8,128)(2,1)S(1)} %get-tuple-element.74), channel_id=5, replica_groups=mesh['section'=4,'dp'=8] {'dp'}, dimensions={2}, use_global_device_ids=true | all-gather | bytes 442368 | tf_op jit(solution)/shard_map/all_gather | solution.py:122
  71.2 15.5 %all-gather.2 = bf16[1,3,512,128]{3,2,1,0:T(8,128)(2,1)} all-gather(bf16[1,3,64,128]{3,2,1,0:T(8,128)(2,1)S(1)} %get-tuple-element.73), channel_id=4, replica_groups=mesh['section'=4,'dp'=8] {'dp'}, dimensions={2}, use_global_device_ids=true | all-gather | bytes 442368 | tf_op jit(solution)/shard_map/all_gather | solution.py:122
  86.7 15.9 %all-gather.4 = bf16[1,3,512,128]{3,2,1,0:T(8,128)(2,1)S(1)} all-gather(bf16[1,3,64,128]{3,2,1,0:T(8,128)(2,1)S(1)} %get-tuple-element.72), channel_id=6, replica_groups=mesh['section'=4,'dp'=8] {'dp'}, dimensions={2}, use_global_device_ids=true | all-gather | bytes 442368 | tf_op jit(solution)/shard_map/all_gather | solution.py:122
  108.7 10.3 %psum.92 = s32[1]{0:T(128)} all-reduce(s32[1]{0:T(128)} %bitcast.16), channel_id=1, replica_groups=mesh['section'=4,'dp'=8] {'dp'}, use_global_device_ids=true, to_apply=%region_3.4 | all-reduce | flops 1 | bytes 8 | tf_op jit(solution)/shard_map/psum | solution.py:158
  119.0 8.2 %copy.143 = f32[3,1,2,192,2,512]{5,4,3,2,0,1:T(2,128)} copy(f32[3,1,2,192,2,512]{5,3,0,4,2,1:T(8,128)} %pad_maximum_fusion) | data formatting | bytes 9437184 | tf_op jit(solution)/shard_map/stack | solution.py:98
  127.2 7.4 %reshape.1040 = f32[3,768,512]{2,1,0:T(8,128)} reshape(f32[3,1,2,192,2,512]{5,4,3,2,0,1:T(2,128)} %copy.143) | data formatting | bytes 9437184 | tf_op jit(solution)/shard_map/reshape | solution.py:98
  140.1 6.2 fusion.113
  149.5 14.5 %psum.91 = f32[2,512]{1,0:T(2,128)} all-reduce(f32[2,512]{1,0:T(2,128)} %pad_maximum_fusion.7), channel_id=1, replica_groups=mesh['section'=4,'dp'=8] {'dp'}, use_global_device_ids=true, to_apply=%region_2.3 | all-reduce | flops 1024 | bytes 8192 | tf_op jit(solution)/shard_map/psum | solution.py:132
  164.8 3.4 broadcast_multiply_fusion
  182.6 6.2 fusion.110
  191.8 15.6 %psum.93 = f32[2,512]{1,0:T(2,128)} all-reduce(f32[2,512]{1,0:T(2,128)S(1)} %pad_maximum_fusion.8), channel_id=1, replica_groups=mesh['section'=4,'dp'=8] {'dp'}, use_global_device_ids=true, to_apply=%region_6.7 | all-reduce | flops 1024 | bytes 8192 | tf_op jit(solution)/shard_map/psum | solution.py:132
  209.9 5.5 add_convert_fusion
  216.4 5.6 multiply_reduce_fusion
  226.2 6.1 fusion.183
  236.2 4.0 subtract_multiply_fusion
  256.5 13.8 %psum.94 = f32[2,512]{1,0:T(2,128)S(1)} all-reduce(f32[2,512]{1,0:T(2,128)S(1)} %pad_maximum_fusion.4), channel_id=1, replica_groups=mesh['section'=4,'dp'=8] {'dp'}, use_global_device_ids=true, to_apply=%region_11.12 | all-reduce | flops 1024 | bytes 8192 | tf_op jit(solution)/shard_map/psum | solution.py:148
  270.4 3.6 fusion.182
  274.1 3.5 fusion.62
  279.8 3.8 collective-permute-start.4
  290.2 22.4 %fusion.8 = f32[3,3,512,512]{3,2,1,0:T(8,128)} fusion(bf16[1,4,384,512]{3,2,1,0:T(8,128)(2,1)S(1)} %copy-done.28, bf16[1,2,384,512]{3,2,1,0:T(8,128)(2,1)S(1)} %fusion.85), kind=kOutput, calls=%fused_computation.19 | convolution fusion | flops 3617587200 | bytes 11796480 | tf_op jit(solution)/shard_map/conv_general_dilated | solution.py:49
  321.7 4.0 select_convert_fusion
  332.0 14.4 %psum.95 = f32[2,512]{1,0:T(2,128)S(1)} all-reduce(f32[2,512]{1,0:T(2,128)S(1)} %get-tuple-element.85), channel_id=1, replica_groups=mesh['section'=4,'dp'=8] {'dp'}, use_global_device_ids=true, to_apply=%region_15.16 | all-reduce | flops 1024 | bytes 8192 | tf_op jit(solution)/shard_map/psum | solution.py:148
  348.5 22.4 %fusion.10 = f32[3,3,512,512]{3,2,1,0:T(8,128)} fusion(bf16[1,4,384,512]{3,2,1,0:T(8,128)(2,1)S(1)} %copy-done.26, bf16[1,2,384,512]{3,2,1,0:T(8,128)(2,1)S(1)} %bitcast.302), kind=kOutput, calls=%fused_computation.21 | convolution fusion | flops 3617587200 | bytes 11796480 | tf_op jit(solution)/shard_map/conv_general_dilated | solution.py:49
  370.9 6.8 %reshape.1039 = f32[3,1,2,192,2,512]{5,4,3,2,0,1:T(2,128)} reshape(f32[3,768,512]{2,1,0:T(8,128)} %get-tuple-element.46) | data formatting | bytes 9437184 | tf_op jit(solution)/shard_map/reshape | solution.py:80
  382.3 7.5 %fusion.187 = (f32[3,1,1,192,1,512]{5,4,3,2,0,1:T(1,128)S(1)}, f32[3,1,1,192,1,512]{5,4,3,2,0,1:T(1,128)S(1)}, f32[3,1,1,192,1,512]{5,4,3,2,0,1:T(1,128)S(1)}, f32[3,1,1,192,1,512]{5,4,3,2,0,1:T(1,128)S(1)}) fusion(f32[3,1,2,192,2,512]{5,4,3,2,0,1:T(2,128)} %reshape.1039), kind=kLoop, calls=%fused_computation.286 | loop fusion | bytes 9437184 | tf_op jit(solution)/shard_map/slice | solution.py:84
  392.0 40.9 %all-reduce = (f32[2,512]{1,0:T(2,128)}, f32[2,512]{1,0:T(2,128)}) all-reduce(f32[2,512]{1,0:T(2,128)S(1)} %copy-done.69, f32[2,512]{1,0:T(2,128)S(1)} %copy-done.68), channel_id=1, replica_groups=mesh['section'=4,'dp'=8] {'section','dp'}, use_global_device_ids=true, to_apply=%region_28.29 | all-reduce | flops 2048 | bytes 16384 | tf_op jit(solution)/shard_map/psum | solution.py:207
  444.2 13.3 %reduce-scatter.9.cloned.1.call-done = f32[576,512]{1,0:T(8,128)} async-done(((f32[4608,512]{1,0:T(8,128)}), f32[576,512]{1,0:T(8,128)}) %reduce-scatter.9.cloned.1.call-update) | async-done | bytes 1179664 | tf_op jit(solution)/shard_map/reduce_scatter | solution.py:201
  459.7 98.0 %reduce-scatter.7.cloned.1.call-done = f32[576,512]{1,0:T(8,128)} async-done(((f32[4608,512]{1,0:T(8,128)}), f32[576,512]{1,0:T(8,128)}) %reduce-scatter.7.cloned.1.call-update) | async-done | bytes 1179664 | tf_op jit(solution)/shard_map/reduce_scatter | solution.py:201
  560.0 6.3 fusion.105
  569.8 32.9 %all-reduce.6.cloned.1.call-done = (bf16[1,3,64,128]{3,2,1,0:T(8,128)(2,1)}, bf16[1,3,64,128]{3,2,1,0:T(8,128)(2,1)}, bf16[1,3,16,512]{3,2,1,0:T(8,128)(2,1)}, bf16[1,3,16,512]{3,2,1,0:T(8,128)(2,1)}) async-done(((bf16[1,3,64,128]{3,2,1,0:T(8,128)(2,1)}, bf16[1,3,64,128]{3,2,1,0:T(8,128)(2,1)}, bf16[1,3,16,512]{3,2,1,0:T(8,128)(2,1)}, bf16[1,3,16,512]{3,2,1,0:T(8,128)(2,1)}), ...) | async-done | bytes 196624 | tf_op jit(solution)/shard_map/psum | solution.py:202
  605.8 55.5 %all-reduce.8.cloned.1.call-done = (bf16[1,576,512]{2,1,0:T(8,128)(2,1)}, bf16[1,576,512]{2,1,0:T(8,128)(2,1)}) async-done(((bf16[1,576,512]{2,1,0:T(8,128)(2,1)}, bf16[1,576,512]{2,1,0:T(8,128)(2,1)}), (bf16[1,576,512]{2,1,0:T(8,128)(2,1)}, bf16[1,576,512]{2,1,0:T(8,128)(2,1)})) %all-reduce.8.cloned.1.call-update) | async-done | bytes 1179664 | tf_op jit(solution)/shard_map/psum | solution.py:202
  (335 shorter events, 129.2 us)
Async XLA Ops:
  7.2 132.6 %all-gather.9.cloned.1.call-start = ((), (), s32[]{:S(2)}) async-start(), calls=%async_computation.12 | async-start | bytes 5308416 | tf_op jit(solution)/shard_map/all_gather | solution.py:122
  10.2 172.1 %all-gather.11.cloned.1.call-start = ((), (), s32[]{:S(2)}) async-start(), calls=%async_computation.13 | async-start | bytes 5308416 | tf_op jit(solution)/shard_map/all_gather | solution.py:122
  10.9 426.9 %reduce-scatter.13.cloned.1.call-start = ((), (), s32[]{:S(2)}) async-start(), calls=%async_computation.9 | async-start | bytes 884736 | tf_op jit(solution)/shard_map/reduce_scatter | solution.py:201
  13.7 89.0 %copy-start.78 = (f32[2,512]{1,0:T(2,128)S(1)}, f32[2,512]{1,0:T(2,128)}, u32[]{:S(2)}) copy-start(f32[2,512]{1,0:T(2,128)} %param.16) | copy-start | bytes 12292
  13.7 89.6 %copy-start.79 = (f32[2,512]{1,0:T(2,128)S(1)}, f32[2,512]{1,0:T(2,128)}, u32[]{:S(2)}) copy-start(f32[2,512]{1,0:T(2,128)} %param.15) | copy-start | bytes 12292
  13.7 122.5 %collective-permute-start.1 = (bf16[1,384,512]{2,1,0:T(8,128)(2,1)S(1)}, bf16[1,384,512]{2,1,0:T(8,128)(2,1)S(1)}, u32[]{:S(2)}, u32[]{:S(2)}) collective-permute-start(bf16[1,384,512]{2,1,0:T(8,128)(2,1)S(1)} %get-tuple-element.71), channel_id=1, source_target_pairs={{1,0},{2,1},{3,2},{4,3},{5,4},{6,5},{7,6},{9,8},{10,9},{11,10},{12... | collective-permute-start | bytes 1179656 | tf_op jit(solution)/shard_map/ppermute | solution.py:20
  15.0 121.2 %collective-permute-start = (bf16[1,384,512]{2,1,0:T(8,128)(2,1)S(1)}, bf16[1,384,512]{2,1,0:T(8,128)(2,1)S(1)}, u32[]{:S(2)}, u32[]{:S(2)}) collective-permute-start(bf16[1,384,512]{2,1,0:T(8,128)(2,1)S(1)} %get-tuple-element.70), channel_id=1, source_target_pairs={{0,1},{1,2},{2,3},{3,4},{4,5},{5,6},{6,7},{8,9},{9,10},{10,11},{11... | collective-permute-start | bytes 1179656 | tf_op jit(solution)/shard_map/ppermute | solution.py:19
  18.8 85.9 %copy-start.70 = (pred[192]{0:T(512)(128)(4,1)}, pred[192]{0:T(512)(128)(4,1)S(1)}, u32[]{:S(2)}) copy-start(pred[192]{0:T(512)(128)(4,1)S(1)} %get-tuple-element.17) | copy-start | bytes 580
  18.8 85.9 %copy-start.72 = (pred[192]{0:T(512)(128)(4,1)}, pred[192]{0:T(512)(128)(4,1)S(1)}, u32[]{:S(2)}) copy-start(pred[192]{0:T(512)(128)(4,1)S(1)} %get-tuple-element.18) | copy-start | bytes 580
  18.8 85.9 %copy-start.74 = (pred[192]{0:T(512)(128)(4,1)}, pred[192]{0:T(512)(128)(4,1)S(1)}, u32[]{:S(2)}) copy-start(pred[192]{0:T(512)(128)(4,1)S(1)} %get-tuple-element.19) | copy-start | bytes 580
  18.9 85.9 %copy-start.76 = (pred[192]{0:T(512)(128)(4,1)}, pred[192]{0:T(512)(128)(4,1)S(1)}, u32[]{:S(2)}) copy-start(pred[192]{0:T(512)(128)(4,1)S(1)} %get-tuple-element.20) | copy-start | bytes 580
  19.5 266.1 %copy-start.37 = (f32[2,384]{1,0:T(2,128)}, f32[2,384]{1,0:T(2,128)S(1)}, u32[]{:S(2)}) copy-start(f32[2,384]{1,0:T(2,128)S(1)} %fusion.180) | copy-start | bytes 9220
  102.7 112.8 %copy-start.16 = (bf16[1,3,512,128]{3,2,1,0:T(8,128)(2,1)}, bf16[1,3,512,128]{3,2,1,0:T(8,128)(2,1)S(1)}, u32[]{:S(2)}) copy-start(bf16[1,3,512,128]{3,2,1,0:T(8,128)(2,1)S(1)} %all-gather.4) | copy-start | bytes 1179652
  103.3 74.6 %copy-start.51 = (f32[1,512]{1,0:T(1,128)}, f32[1,512]{1,0:T(1,128)S(1)}, u32[]{:S(2)}) copy-start(f32[1,512]{1,0:T(1,128)S(1)} %get-tuple-element.81) | copy-start | bytes 6148
  103.3 182.3 %copy-start.42 = (f32[1,512]{1,0:T(1,128)}, f32[1,512]{1,0:T(1,128)S(1)}, u32[]{:S(2)}) copy-start(f32[1,512]{1,0:T(1,128)S(1)} %get-tuple-element.80) | copy-start | bytes 6148
  136.0 138.1 %copy-start.39 = (f32[768]{0:T(1024)}, f32[768]{0:T(1024)S(1)}, u32[]{:S(2)}) copy-start(f32[768]{0:T(1024)S(1)} %fusion.167) | copy-start | bytes 9220
  169.9 8.8 %collective-permute-start.3 = (bf16[1,384,512]{2,1,0:T(8,128)(2,1)S(1)}, bf16[1,384,512]{2,1,0:T(8,128)(2,1)S(1)}, u32[]{:S(2)}, u32[]{:S(2)}) collective-permute-start(bf16[1,384,512]{2,1,0:T(8,128)(2,1)S(1)} %get-tuple-element.69), channel_id=1, source_target_pairs={{1,0},{2,1},{3,2},{4,3},{5,4},{6,5},{7,6},{9,8},{10,9},{11,10},{12... | collective-permute-start | bytes 1179656 | tf_op jit(solution)/shard_map/ppermute | solution.py:20
  171.3 7.4 %collective-permute-start.2 = (bf16[1,384,512]{2,1,0:T(8,128)(2,1)S(1)}, bf16[1,384,512]{2,1,0:T(8,128)(2,1)S(1)}, u32[]{:S(2)}, u32[]{:S(2)}) collective-permute-start(bf16[1,384,512]{2,1,0:T(8,128)(2,1)S(1)} %get-tuple-element.68), channel_id=1, source_target_pairs={{0,1},{1,2},{2,3},{3,4},{4,5},{5,6},{6,7},{8,9},{9,10},{10,11},{11... | collective-permute-start | bytes 1179656 | tf_op jit(solution)/shard_map/ppermute | solution.py:19
  208.2 77.4 %copy-start.44 = (f32[1,512]{1,0:T(1,128)}, f32[1,512]{1,0:T(1,128)S(1)}, u32[]{:S(2)}) copy-start(f32[1,512]{1,0:T(1,128)S(1)} %get-tuple-element.37) | copy-start | bytes 6148
  226.1 213.2 %reduce-scatter.11.cloned.1.call-start = ((), (), s32[]{:S(2)}) async-start(), calls=%async_computation.8 | async-start | bytes 884736 | tf_op jit(solution)/shard_map/reduce_scatter | solution.py:201
  232.3 41.7 %copy-start.2 = (f32[768,512]{1,0:T(8,128)}, f32[768,512]{1,0:T(8,128)S(1)}, u32[]{:S(2)}) copy-start(f32[768,512]{1,0:T(8,128)S(1)} %get-tuple-element.7) | copy-start | bytes 4718596
  240.2 200.7 %reduce-scatter.17.cloned.1.call-start = ((), (), s32[]{:S(2)}) async-start(), calls=%async_computation.11 | async-start | bytes 884736 | tf_op jit(solution)/shard_map/reduce_scatter | solution.py:201
  274.0 168.4 %reduce-scatter.15.cloned.1.call-start = ((), (), s32[]{:S(2)}) async-start(), calls=%async_computation.10 | async-start | bytes 884736 | tf_op jit(solution)/shard_map/reduce_scatter | solution.py:201
  278.5 39.3 %collective-permute-start.5 = (bf16[1,384,512]{2,1,0:T(8,128)(2,1)}, bf16[1,384,512]{2,1,0:T(8,128)(2,1)}, u32[]{:S(2)}, u32[]{:S(2)}) collective-permute-start(bf16[1,384,512]{2,1,0:T(8,128)(2,1)} %get-tuple-element.67), channel_id=1, source_target_pairs={{1,0},{2,1},{3,2},{4,3},{5,4},{6,5},{7,6},{9,8},{10,9},{11,10},{12... | collective-permute-start | bytes 1179656 | tf_op jit(solution)/shard_map/ppermute | solution.py:20
  279.8 38.0 %collective-permute-start.4 = (bf16[1,384,512]{2,1,0:T(8,128)(2,1)}, bf16[1,384,512]{2,1,0:T(8,128)(2,1)}, u32[]{:S(2)}, u32[]{:S(2)}) collective-permute-start(bf16[1,384,512]{2,1,0:T(8,128)(2,1)} %get-tuple-element.66), channel_id=1, source_target_pairs={{0,1},{1,2},{2,3},{3,4},{4,5},{5,6},{6,7},{8,9},{9,10},{10,11},{11... | collective-permute-start | bytes 1179656 | tf_op jit(solution)/shard_map/ppermute | solution.py:19
  290.1 167.4 %reduce-scatter.9.cloned.1.call-start = ((), (), s32[]{:S(2)}) async-start(), calls=%async_computation.7 | async-start | bytes 10616832 | tf_op jit(solution)/shard_map/reduce_scatter | solution.py:201
  312.7 245.0 %reduce-scatter.7.cloned.1.call-start = ((), (), s32[]{:S(2)}) async-start(), calls=%async_computation.6 | async-start | bytes 10616832 | tf_op jit(solution)/shard_map/reduce_scatter | solution.py:201
  370.8 231.9 %all-reduce.6.cloned.1.call-start = ((), (), s32[]{:S(2)}) async-start(), calls=%async_computation.14 | async-start | bytes 393216 | tf_op jit(solution)/shard_map/psum | solution.py:202
  377.7 55.2 %collective-permute-start.7 = (bf16[1,384,512]{2,1,0:T(8,128)(2,1)S(1)}, bf16[1,384,512]{2,1,0:T(8,128)(2,1)S(1)}, u32[]{:S(2)}, u32[]{:S(2)}) collective-permute-start(bf16[1,384,512]{2,1,0:T(8,128)(2,1)S(1)} %get-tuple-element.65), channel_id=1, source_target_pairs={{1,0},{2,1},{3,2},{4,3},{5,4},{6,5},{7,6},{9,8},{10,9},{11,10},{12... | collective-permute-start | bytes 1179656 | tf_op jit(solution)/shard_map/ppermute | solution.py:20
  379.0 54.5 %collective-permute-start.6 = (bf16[1,384,512]{2,1,0:T(8,128)(2,1)S(1)}, bf16[1,384,512]{2,1,0:T(8,128)(2,1)S(1)}, u32[]{:S(2)}, u32[]{:S(2)}) collective-permute-start(bf16[1,384,512]{2,1,0:T(8,128)(2,1)S(1)} %get-tuple-element.64), channel_id=1, source_target_pairs={{0,1},{1,2},{2,3},{3,4},{4,5},{5,6},{6,7},{8,9},{9,10},{10,11},{11... | collective-permute-start | bytes 1179656 | tf_op jit(solution)/shard_map/ppermute | solution.py:19
  443.9 217.3 %all-reduce.8.cloned.1.call-start = ((), (), s32[]{:S(2)}) async-start(), calls=%async_computation.15 | async-start | bytes 2359296 | tf_op jit(solution)/shard_map/psum | solution.py:202
  459.7 100.3 %copy-start.83 = (pred[8,49]{0,1:T(8,128)(4,1)S(1)}, pred[8,49]{0,1:T(8,128)(4,1)}, u32[]{:S(2)}) copy-start(pred[8,49]{0,1:T(8,128)(4,1)} %constant.64) | copy-start | bytes 1180
  (77 other events, 332.9 us)
Sparse Core Ops, SparseCore 0:
  10.3 61.0 all-gather.8
  73.6 56.7 all-gather.10
  226.3 29.7 reduce-scatter.12
  258.3 29.8 reduce-scatter.10
  290.3 29.7 reduce-scatter.16
  322.3 29.9 reduce-scatter.14
  354.6 102.8 reduce-scatter.8
  459.8 97.8 reduce-scatter.6
  561.4 41.3 all-reduce.5
  606.6 54.6 all-reduce.7

commit v2 on v1

--- a/solution.py
+++ b/solution.py
@@ -1,11 +1,17 @@
+import functools
+import types
+
 import jax
 import jax.numpy as jnp
 from jax import lax
+from jax.experimental import pallas as pl
+from jax.experimental.pallas import tpu as pltpu
 from jax.sharding import PartitionSpec as P
 
 EPS = 1e-05
 BF16 = jnp.bfloat16
 F32 = jnp.float32
+VMEM_BYTES = 62 * 1024 * 1024
 
 
 def gelu_back(point, upstream):
@@ -216,6 +222,1009 @@
     )
 
 
+GELU_C = 0.7978845608028654
+GELU_K = 0.044715
+MESH = pl.DeviceIdType.MESH
+
+
+def gelu_pair(x):
+    square = x * x
+    t = jnp.tanh(GELU_C * x * (1.0 + GELU_K * square))
+    half = 0.5 * (1.0 + t)
+    slope = half + 0.5 * x * (1.0 - t * t) * (GELU_C * (1.0 + 3.0 * GELU_K * square))
+    return x * half, slope
+
+
+def dot(a, b):
+    return jnp.dot(a, b, preferred_element_type=F32)
+
+
+def dot_nt(a, b):
+    return lax.dot_general(a, b, (((1,), (1,)), ((), ())), preferred_element_type=F32)
+
+
+def dot_tn(a, b):
+    return lax.dot_general(a, b, (((0,), (0,)), ((), ())), preferred_element_type=F32)
+
+
+def step_kernel(
+    dims,
+    counts,
+    pick_ref,
+    gain,
+    bias,
+    images,
+    conv_w,
+    squeeze_w,
+    expand_w,
+    cotangent,
+    out_task,
+    out_image,
+    out_conv,
+    out_squeeze,
+    out_expand,
+    out_gain,
+    out_bias,
+    *scratch,
+):
+    r = types.SimpleNamespace(**jax.tree.unflatten(dims.tree, scratch))
+    n_dp, cols, pixels, width, tasks, bottle = (
+        dims.n_dp,
+        dims.cols,
+        dims.pixels,
+        dims.width,
+        dims.tasks,
+        dims.bottle,
+    )
+    n_z = n_dp // 2
+    windows = cols // 2
+    lanes = 128
+    n_lane = width // lanes
+    shard_rows = dims.shard_rows
+    s = lax.axis_index("section")
+    d = lax.axis_index("dp")
+    z, c = d // 2, d % 2
+    sib = 2 * z + 1 - c
+    plane = [s + 1 - 2 * (s % 2), (s + 2) % 4, 3 - s]
+
+    def rem(a, b):
+        return lax.rem(a, b)
+
+    def z_at(step):
+        return rem(z + step, n_z)
+
+    def remote(src, dst, send, recv, device):
+        return pltpu.make_async_remote_copy(
+            src_ref=src,
+            dst_ref=dst,
+            send_sem=send,
+            recv_sem=recv,
+            device_id=device,
+            device_id_type=MESH,
+        )
+
+    def al(v, m):
+        return pl.multiple_of(v, m)
+
+    barrier = pltpu.get_barrier_semaphore()
+    for step in range(1, n_dp):
+        pl.semaphore_signal(
+            barrier, inc=1, device_id=(s, rem(d + step, n_dp)), device_id_type=MESH
+        )
+    for p in plane:
+        pl.semaphore_signal(barrier, inc=1, device_id=(p, d), device_id_type=MESH)
+
+    def load(i, src, dst):
+        return pltpu.make_async_copy(src, dst, r.load.at[i])
+
+    staging = [r.h1, r.slope0]
+    conv_rows = shard_rows[0]
+
+    def conv_load(layer, j):
+        lane = slice(j * lanes, (j + 1) * lanes)
+        return load(
+            5 + layer * n_lane + j,
+            conv_w.at[layer, :, lane],
+            staging[layer].at[j, 0:conv_rows],
+        )
+
+    loads = [
+        load(1, squeeze_w, r.sst),
+        load(2, expand_w, r.est),
+        load(3, images.at[s], r.xin),
+        load(4, cotangent.at[s], r.cin),
+    ]
+    for j in range(n_lane):
+        conv_load(0, j).start()
+    for item in loads[:2]:
+        item.start()
+    for j in range(n_lane):
+        conv_load(1, j).start()
+    for item in loads[2:]:
+        item.start()
+
+    full = [r.w0, r.gp, r.w1]
+
+    def shard(kind, buf, which):
+        rows = shard_rows[kind]
+        return buf.at[pl.ds(al(which * rows, 16), rows)]
+
+    def quarter(kind, buf, which, q):
+        rows = shard_rows[kind]
+        return buf.at[pl.ds(al(which * rows + q * (rows // 4), 16), rows // 4)]
+
+    def ag_z_copy(kind, step, owner):
+        view = quarter(kind, full[kind], owner, s)
+        return remote(
+            view,
+            view,
+            r.ag_zs.at[kind, step - 1],
+            r.ag_zr.at[kind, step - 1],
+            (s, 2 * z_at(step) + c),
+        )
+
+    def ag_p_copy(kind, step, p, q):
+        owner = 2 * z_at(n_z - step) + c
+        view = quarter(kind, full[kind], owner, q)
+        i = (step - 1) * 3 + p
+        return remote(view, view, r.ag_ps.at[kind, i], r.ag_pr.at[kind, i], (plane[p], d))
+
+    def ag_s_copy(kind, step, core):
+        view = shard(kind, full[kind], 2 * z_at(n_z - step if step else 0) + core)
+        return remote(view, view, r.ag_ss.at[kind, step], r.ag_sr.at[kind, step], (s, sib))
+
+    def ag_start(kind):
+        for step in range(1, n_z):
+            ag_z_copy(kind, step, d).start()
+        ag_s_copy(kind, 0, c).start()
+
+    def ag_z(kind, step):
+        owner = 2 * z_at(n_z - step) + c
+        ag_z_copy(kind, step, owner).wait_recv()
+        for p in range(3):
+            ag_p_copy(kind, step, p, s).start()
+
+    def ag_p(kind, step):
+        for p in range(3):
+            ag_p_copy(kind, step, p, plane[p]).wait_recv()
+        ag_s_copy(kind, step, c).start()
+
+    def ag_sib(kind):
+        for step in range(n_z):
+            ag_s_copy(kind, step, 1 - c).wait_recv()
+
+    def ag_end(kind):
+        for step in range(1, n_z):
+            ag_z_copy(kind, step, d).wait_send()
+            for p in range(3):
+                ag_p_copy(kind, step, p, s).wait_send()
+        for step in range(n_z):
+            ag_s_copy(kind, step, c).wait_send()
+
+    def cast_conv(layer, buf):
+        for j in range(n_lane):
+            conv_load(layer, j).wait()
+
+        def body(j, _):
+            buf[pl.ds(al(d * conv_rows, 16), conv_rows), pl.ds(al(j * lanes, lanes), lanes)] = (
+                staging[layer][j, 0:conv_rows, :].astype(BF16)
+            )
+            return 0
+
+        lax.fori_loop(0, n_lane, body, 0)
+
+    g_rows = shard_rows[1]
+    e_rows = n_ex = bottle // n_dp
+    s_rows = width // n_dp
+    n_sub = s_rows // e_rows
+
+    def ex_row(which, l, t):
+        return al(which * g_rows + (l * tasks + t) * e_rows, 16)
+
+    def sq_row(which, l, t):
+        return al(which * g_rows + (2 * tasks + l * tasks + t) * e_rows, 16)
+
+    cast_conv(0, r.w0)
+    pl.semaphore_wait(barrier, n_dp - 1 + 3)
+    ag_start(0)
+    loads[0].wait()
+    loads[1].wait()
+    for l in range(2):
+        for t in range(tasks):
+            r.gp[pl.ds(ex_row(d, l, t), e_rows), :] = r.est[l, t].astype(BF16)
+            for k in range(n_sub):
+                r.gp[pl.ds(sq_row(d, l, t), e_rows), k * lanes : (k + 1) * lanes] = r.sst[
+                    l, t, k * e_rows : (k + 1) * e_rows, :
+                ].astype(BF16)
+    ag_start(1)
+    cast_conv(1, r.w1)
+    ag_start(2)
+
+    count = counts[s, 0]
+    pick_tile = pick_ref[...]
+    slot_pick = (
+        (pick_tile // 2) * cols
+        + 2 * lax.broadcasted_iota(jnp.int32, (windows, lanes), 0)
+        + pick_tile % 2
+    )
+    r.mp[...] = jnp.where(slot_pick < count, 1.0, 0.0).astype(F32)
+
+    def lane_at(j, base=0):
+        return pl.ds(al(base + j * lanes, lanes), lanes)
+
+    def valid_rows(start, rows):
+        return (lax.broadcasted_iota(jnp.int32, (rows, lanes), 0) + start) < count
+
+    def shift_in(value_of, buf, block):
+        def body(j, _):
+            v = value_of(j)
+            at = lax.broadcasted_iota(jnp.int32, (cols, lanes), 0)
+            before = jnp.where(at == 0, 0.0, pltpu.roll(v, 1, 0))
+            after = jnp.where(at == cols - 1, 0.0, pltpu.roll(v, cols - 1, 0))
+            rows = pl.ds(block * cols, cols)
+            buf[rows, lane_at(j)] = before.astype(BF16)
+            buf[rows, lane_at(j, width)] = v.astype(BF16)
+            buf[rows, lane_at(j, 2 * width)] = after.astype(BF16)
+            return 0
+
+        lax.fori_loop(0, n_lane, body, 0)
+
+    @pl.when(d == 0)
+    def _():
+        r.halo[:, 0] = jnp.zeros_like(r.halo[:, 0])
+
+    @pl.when(d == n_dp - 1)
+    def _():
+        r.halo[:, 1] = jnp.zeros_like(r.halo[:, 1])
+
+    def halo_down(e, buf):
+        return remote(
+            buf.at[2 * cols : 3 * cols, width : 2 * width],
+            r.halo.at[e, 0],
+            r.halo_s.at[e, 0],
+            r.halo_r.at[e, 0],
+            (s, rem(d + 1, n_dp)),
+        )
+
+    def halo_up(e, buf):
+        return remote(
+            buf.at[cols : 2 * cols, width : 2 * width],
+            r.halo.at[e, 1],
+            r.halo_s.at[e, 1],
+            r.halo_r.at[e, 1],
+            (s, rem(d + n_dp - 1, n_dp)),
+        )
+
+    def halo_start(e, buf):
+        @pl.when(d < n_dp - 1)
+        def _():
+            halo_down(e, buf).start()
+
+        @pl.when(d > 0)
+        def _():
+            halo_up(e, buf).start()
+
+    def halo_finish(e, buf):
+        @pl.when(d > 0)
+        def _():
+            halo_down(e, buf).wait_recv()
+
+        @pl.when(d < n_dp - 1)
+        def _():
+            halo_up(e, buf).wait_recv()
+
+        shift_in(lambda j: r.halo[e, 0, :, lane_at(j)].astype(F32), buf, 0)
+        shift_in(lambda j: r.halo[e, 1, :, lane_at(j)].astype(F32), buf, 3)
+
+    def halo_sent(e, buf):
+        @pl.when(d < n_dp - 1)
+        def _():
+            halo_down(e, buf).wait_send()
+
+        @pl.when(d > 0)
+        def _():
+            halo_up(e, buf).wait_send()
+
+    def ex_copy(k, step, owner):
+        return remote(
+            r.ex_out.at[k],
+            r.ex_in.at[k, owner],
+            r.ex_s.at[k, step - 1],
+            r.ex_r.at[k, step - 1],
+            (s, rem(d + step, n_dp)),
+        )
+
+    def ex_start(k):
+        for step in range(1, n_dp):
+            ex_copy(k, step, d).start()
+        r.ex_in[k, d] = r.ex_out[k]
+
+    def ex_finish(k):
+        for step in range(1, n_dp):
+            ex_copy(k, step, rem(d + n_dp - step, n_dp)).wait_recv()
+        total = r.ex_in[k, 0]
+        for i in range(1, n_dp):
+            total = total + r.ex_in[k, i]
+        return total
+
+    def conv_forward(xc, w, h):
+        span = 3 * width
+        half = width // 2
+        for n in range(2):
+            acc = None
+            for a in range(3):
+                term = dot(
+                    xc[a * cols : a * cols + pixels, :],
+                    w[a * span : (a + 1) * span, n * half : (n + 1) * half],
+                )
+                acc = term if acc is None else acc + term
+            for j in range(n_lane // 2):
+                h[n * (n_lane // 2) + j] = acc[:, j * lanes : (j + 1) * lanes]
+
+    def conv_back(dc, w):
+        acc = None
+        for a in range(3):
+            for b in range(3):
+                term = dot_nt(
+                    dc[(2 - a) * cols : (2 - a) * cols + pixels, (2 - b) * width : (3 - b) * width],
+                    w[(3 * a + b) * width : (3 * a + b + 1) * width, :],
+                )
+                acc = term if acc is None else acc + term
+        for j in range(n_lane):
+            r.fbuf[j] = acc[:, j * lanes : (j + 1) * lanes]
+
+    quarter_rows = pixels // 4
+
+    def stats(h, k):
+        def body(j, _):
+            first = jnp.zeros((1, lanes), F32)
+            second = jnp.zeros((1, lanes), F32)
+            for i in range(4):
+                v = h[j, i * quarter_rows : (i + 1) * quarter_rows, :]
+                kept = jnp.where(valid_rows(i * quarter_rows, quarter_rows), v, 0.0)
+                first = first + jnp.sum(kept, 0, keepdims=True)
+                second = second + jnp.sum(kept * v, 0, keepdims=True)
+            r.ex_out[k, 0:1, lane_at(j)] = first
+            r.ex_out[k, 1:2, lane_at(j)] = second
+            return 0
+
+        r.ex_out[k] = jnp.broadcast_to(count.astype(F32), (8, width))
+        lax.fori_loop(0, n_lane, body, 0)
+
+    def norm_of(sums, layer):
+        total = sums[2:3, :]
+        centre = sums[0:1, :] / total
+        inverse = lax.rsqrt(sums[1:2, :] / total - centre * centre + EPS)
+        r.norm[layer, 0:1, :] = centre
+        r.norm[layer, 1:2, :] = inverse
+        r.norm[layer, 2:3, :] = gain[layer : layer + 1, :] * inverse
+        r.norm[layer, 3:4, :] = 1.0 / total
+
+    def corner_rows(k):
+        return pl.ds((k // 2) * cols + k % 2, windows, stride=2)
+
+    def picked(ref, j):
+        out = None
+        which = pick_ref[...]
+        for k in range(4):
+            part = jnp.where(which == k, ref[j, corner_rows(k), :], 0.0)
+            out = part if out is None else out + part
+        return out
+
+    loads[2].wait()
+
+    def image_row(i):
+        def value(j):
+            v = r.xin[i * cols : (i + 1) * cols, lane_at(j)].astype(F32)
+            return jnp.where(valid_rows(i * cols, cols), v, 0.0)
+
+        return value
+
+    shift_in(image_row(0), r.xc0, 1)
+    shift_in(image_row(1), r.xc0, 2)
+    halo_start(0, r.xc0)
+    for step in range(1, n_z):
+        ag_z(0, step)
+    halo_finish(0, r.xc0)
+    for step in range(1, n_z):
+        ag_z(1, step)
+    for step in range(1, n_z):
+        ag_p(0, step)
+        ag_z(2, step)
+    ag_sib(0)
+
+    conv_forward(r.xc0, r.w0, r.h0)
+    stats(r.h0, 0)
+    ex_start(0)
+    for step in range(1, n_z):
+        ag_p(1, step)
+    norm_of(ex_finish(0), 0)
+
+    def block_0(j, _):
+        lane = lane_at(j)
+        for i in range(4):
+            rows = slice(i * quarter_rows, (i + 1) * quarter_rows)
+            normed = (r.h0[j, rows, :] - r.norm[0, 0:1, lane]) * r.norm[
+                0, 2:3, lane
+            ] + bias[0:1, lane]
+            g, slope = gelu_pair(normed)
+            ok = valid_rows(i * quarter_rows, quarter_rows)
+            r.fbuf[j, rows, :] = jnp.where(ok, g, 0.0).astype(BF16).astype(F32)
+            r.slope0[j, rows, :] = jnp.where(ok, slope, 0.0)
+        f1p = picked(r.fbuf, j)
+        r.f1p[:, lane] = f1p
+        r.f1b[:, lane] = f1p.astype(BF16)
+        return 0
+
+    lax.fori_loop(0, n_lane, block_0, 0)
+    shift_in(lambda j: r.fbuf[j, 0:cols, :], r.xc1, 1)
+    shift_in(lambda j: r.fbuf[j, cols : 2 * cols, :], r.xc1, 2)
+    halo_start(1, r.xc1)
+    ag_sib(1)
+
+    def unpack(i, _):
+        for l in range(2):
+            for t in range(tasks):
+                r.ex_w[l, t, pl.ds(al(i * e_rows, 16), e_rows), :] = r.gp[
+                    pl.ds(ex_row(i, l, t), e_rows), :
+                ]
+                for k in range(n_sub):
+                    r.sq_w[
+                        l,
+                        pl.ds(al(i * s_rows + k * e_rows, 16), e_rows),
+                        t * bottle : (t + 1) * bottle,
+                    ] = r.gp[pl.ds(sq_row(i, l, t), e_rows), k * lanes : (k + 1) * lanes]
+        return 0
+
+    lax.fori_loop(0, n_dp, unpack, 0)
+    mask_pick = jnp.concatenate([r.mp[...]] * n_lane, axis=1)
+    g, slope = gelu_pair(dot(r.f1b[...], r.sq_w[0]))
+    r.excited0[...] = g.astype(BF16)
+    r.eslope0[...] = slope
+
+    def task_lane(t):
+        return pl.ds(al(t * bottle, lanes), bottle)
+
+    def gate_0(t, _):
+        value = jax.nn.sigmoid(dot(r.excited0[:, task_lane(t)], r.ex_w[0, t]))
+        r.gate0[t] = value
+        r.t1[t] = (mask_pick * value * r.f1p[...]).astype(BF16)
+        return 0
+
+    lax.fori_loop(0, tasks, gate_0, 0)
+    halo_finish(1, r.xc1)
+    for step in range(1, n_z):
+        ag_p(2, step)
+    ag_sib(2)
+
+    conv_forward(r.xc1, r.w1, r.h1)
+    stats(r.h1, 1)
+    ex_start(1)
+    for kind in range(3):
+        ag_end(kind)
+    norm_of(ex_finish(1), 1)
+
+    def block_1(j, _):
+        lane = lane_at(j)
+        off = picked(r.h1, j) - r.norm[1, 0:1, lane]
+        g, slope = gelu_pair(off * r.norm[1, 2:3, lane] + bias[1:2, lane])
+        r.f2p[:, lane] = (r.mp[...] * g).astype(BF16).astype(F32)
+        r.slope1[:, lane] = r.mp[...] * slope
+        r.centred1[:, lane] = off * r.norm[1, 1:2, lane]
+        return 0
+
+    lax.fori_loop(0, n_lane, block_1, 0)
+    loads[3].wait()
+    r.df2[...] = jnp.zeros_like(r.df2)
+
+    def pack_grads(l, t, grad_squeeze, grad_expand):
+        r.gs_st[...] = grad_squeeze
+        r.ge_st[...] = grad_expand
+
+        def body(i, _):
+            r.gp[pl.ds(ex_row(i, l, t), e_rows), :] = r.ge_st[
+                pl.ds(al(i * e_rows, 16), e_rows), :
+            ].astype(BF16)
+            for k in range(n_sub):
+                r.gp[pl.ds(sq_row(i, l, t), e_rows), k * lanes : (k + 1) * lanes] = r.gs_st[
+                    pl.ds(al(i * s_rows + k * e_rows, 16), e_rows), :
+                ].astype(BF16)
+            return 0
+
+        lax.fori_loop(0, n_dp, body, 0)
+
+    def gate_1(t, _):
+        w_s = r.sq_w[1, :, task_lane(t)]
+        w_e = r.ex_w[1, t]
+        f2p = r.f2p[...]
+        source = (f2p + r.t1[t].astype(F32)).astype(BF16)
+        g, slope = gelu_pair(dot(source, w_s))
+        excited = g.astype(BF16)
+        value = jax.nn.sigmoid(dot(excited, w_e))
+        field = mask_pick * f2p
+        d_task = r.cin[t].astype(F32)
+        r.cin[t] = (value * field).astype(BF16)
+        d_expanded = (d_task * field * value * (1.0 - value)).astype(BF16)
+        d_squeezed = (slope * dot_nt(d_expanded, w_e)).astype(BF16)
+        d_source = dot_nt(d_squeezed, w_s)
+        r.t1[t] = d_source.astype(BF16)
+        r.df2[...] += d_source + mask_pick * d_task * value
+        pack_grads(1, t, dot_tn(source, d_squeezed), dot_tn(excited, d_expanded))
+        return 0
+
+    lax.fori_loop(0, tasks, gate_1, 0)
+    task_store = pltpu.make_async_copy(r.cin, out_task.at[0], r.store.at[0])
+    task_store.start()
+
+    def back_1(j, _):
+        lane = lane_at(j)
+        d_norm = r.slope1[:, lane] * r.df2[:, lane].astype(BF16).astype(F32)
+        r.df2[:, lane] = d_norm
+        r.ex_out[2, 0:1, lane] = jnp.sum(d_norm, 0, keepdims=True)
+        r.ex_out[2, 1:2, lane] = jnp.sum(d_norm * r.centred1[:, lane], 0, keepdims=True)
+        return 0
+
+    r.ex_out[2] = jnp.zeros((8, width), F32)
+    lax.fori_loop(0, n_lane, back_1, 0)
+    ex_start(2)
+
+    r.df1[...] = jnp.zeros_like(r.df1)
+
+    def gate_0_back(t, _):
+        w_s = r.sq_w[0, :, task_lane(t)]
+        w_e = r.ex_w[0, t]
+        value = r.gate0[t]
+        d_task = r.t1[t].astype(F32)
+        excited = r.excited0[:, task_lane(t)]
+        d_expanded = (d_task * (mask_pick * r.f1p[...]) * value * (1.0 - value)).astype(BF16)
+        d_squeezed = (r.eslope0[:, task_lane(t)] * dot_nt(d_expanded, w_e)).astype(BF16)
+        r.df1[...] += dot_nt(d_squeezed, w_s) + mask_pick * d_task * value
+        pack_grads(0, t, dot_tn(r.f1b[...], d_squeezed), dot_tn(excited, d_expanded))
+        return 0
+
+    lax.fori_loop(0, tasks, gate_0_back, 0)
+
+    r.sums[...] = jnp.zeros_like(r.sums)
+
+    def back_terms(k, layer):
+        sums = ex_finish(k)
+        r.sums[2 * layer : 2 * layer + 2, :] = sums[0:2, :]
+        scale = gain[layer : layer + 1, :] * r.norm[layer, 3:4, :] * r.norm[layer, 1:2, :]
+        r.norm[layer, 4:5, :] = scale * sums[0:1, :]
+        r.norm[layer, 5:6, :] = scale * r.norm[layer, 1:2, :] * sums[1:2, :]
+
+    back_terms(2, 1)
+
+    def hidden_grad_1(j, _):
+        lane = lane_at(j)
+        norm = r.norm
+        for k in range(4):
+            at = corner_rows(k)
+            spread = jnp.where(pick_ref[...] == k, r.df2[:, lane] * norm[1, 2:3, lane], 0.0)
+            value = spread - (
+                norm[1, 4:5, lane] + (r.h1[j, at, :] - norm[1, 0:1, lane]) * norm[1, 5:6, lane]
+            )
+            slot = (k // 2) * cols + k % 2 + 2 * lax.broadcasted_iota(
+                jnp.int32, (windows, lanes), 0
+            )
+            r.fbuf[j, at, :] = jnp.where(slot < count, value, 0.0)
+        return 0
+
+    lax.fori_loop(0, n_lane, hidden_grad_1, 0)
+    shift_in(lambda j: r.fbuf[j, 0:cols, :], r.dc, 1)
+    shift_in(lambda j: r.fbuf[j, cols : 2 * cols, :], r.dc, 2)
+    halo_start(2, r.dc)
+
+    grads = [r.w1, r.gp, r.g1]
+
+    def pair_of(k):
+        return z_at(1 + k)
+
+    def rs_a_copy(kind, k, core):
+        return remote(
+            shard(kind, grads[kind], 2 * pair_of(k) + core),
+            r.ra[kind].at[k],
+            r.rs_as.at[kind, k],
+            r.rs_ar.at[kind, k],
+            (s, sib),
+        )
+
+    def rs_b_copy(kind, k, p):
+        return remote(
+            quarter(kind, grads[kind], 2 * pair_of(k) + c, plane[p]),
+            r.rb[kind].at[p, k],
+            r.rs_bs.at[kind, k, p],
+            r.rs_br.at[kind, k, p],
+            (plane[p], d),
+        )
+
+    def rs_c_copy(kind, k):
+        return remote(
+            r.qs[kind].at[k],
+            r.rc[kind].at[k],
+            r.rs_cs.at[kind, k],
+            r.rs_cr.at[kind, k],
+            (s, 2 * pair_of(k) + c),
+        )
+
+    def rs_d_copy(kind, p, q):
+        rows = shard_rows[kind] // 4
+        view = r.td[kind].at[pl.ds(al(q * rows, 16), rows)]
+        return remote(view, view, r.rs_ds.at[kind, p], r.rs_dr.at[kind, p], (plane[p], d))
+
+    def conv_weight(kind, xc, k):
+        tile = 2 * shard_rows[kind] // 3
+        per = 3 * width // tile
+
+        def body(i, _):
+            g = pair_of(k) * 3 + i
+            a = g // per
+            term = dot_tn(
+                xc[pl.ds(al(a * cols, 16), pixels), pl.ds(al((g % per) * tile, lanes), tile)],
+                r.dc[cols : 3 * cols, width : 2 * width],
+            )
+            grads[kind][pl.ds(al(g * tile, 16), tile), :] = term.astype(BF16)
+            return 0
+
+        lax.fori_loop(0, 3, body, 0)
+
+    def rs_a(kind, k):
+        rs_a_copy(kind, k, 1 - c).start()
+
+    def rs_b(kind, k):
+        rs_a_copy(kind, k, c).wait_recv()
+        rows = shard_rows[kind]
+        tile = rows // 4
+        start = (2 * pair_of(k) + c) * rows
+
+        def body(i, _):
+            at = pl.ds(al(start + i * tile, 16), tile)
+            grads[kind][at, :] = (
+                grads[kind][at, :].astype(F32)
+                + r.ra[kind][k, pl.ds(al(i * tile, 16), tile), :].astype(F32)
+            ).astype(BF16)
+            return 0
+
+        lax.fori_loop(0, 4, body, 0)
+        for p in range(3):
+            rs_b_copy(kind, k, p).start()
+
+    def rs_c(kind, k):
+        for p in range(3):
+            rs_b_copy(kind, k, p).wait_recv()
+        rows = shard_rows[kind] // 4
+        at = pl.ds(al((2 * pair_of(k) + c) * shard_rows[kind] + s * rows, 16), rows)
+        total = grads[kind][at, :].astype(F32)
+        for p in range(3):
+            total = total + r.rb[kind][p, k].astype(F32)
+        if k < n_z - 1:
+            r.qs[kind][k] = total.astype(BF16)
+            rs_c_copy(kind, k).start()
+        else:
+            r.qf[kind][...] = total
+
+    def rs_d(kind):
+        total = r.qf[kind][...]
+        for k in range(n_z - 1):
+            rs_c_copy(kind, k).wait_recv()
+            total = total + r.rc[kind][k].astype(F32)
+        rows = shard_rows[kind] // 4
+        r.td[kind][pl.ds(al(s * rows, 16), rows), :] = total.astype(BF16)
+        for p in range(3):
+            rs_d_copy(kind, p, s).start()
+
+    def rs_e(kind):
+        for p in range(3):
+            rs_d_copy(kind, p, plane[p]).wait_recv()
+
+    def rs_end(kind):
+        for k in range(n_z):
+            rs_a_copy(kind, k, 1 - c).wait_send()
+            for p in range(3):
+                rs_b_copy(kind, k, p).wait_send()
+            if k < n_z - 1:
+                rs_c_copy(kind, k).wait_send()
+        for p in range(3):
+            rs_d_copy(kind, p, s).wait_send()
+
+    for k in range(n_z):
+        conv_weight(2, r.xc1, k)
+        rs_a(2, k)
+        if k > 0:
+            rs_b(2, k - 1)
+    rs_b(2, n_z - 1)
+    for k in range(n_z):
+        rs_a(1, k)
+
+    halo_finish(2, r.dc)
+    conv_back(r.dc, r.w1)
+    halo_sent(2, r.dc)
+    for k in range(n_z):
+        rs_b(1, k)
+
+    def back_0(j, _):
+        lane = lane_at(j)
+        norm = r.norm
+        first = jnp.zeros((1, lanes), F32)
+        second = jnp.zeros((1, lanes), F32)
+        for k in range(4):
+            at = corner_rows(k)
+            d_field = r.fbuf[j, at, :].astype(BF16).astype(F32) + jnp.where(
+                pick_ref[...] == k, r.df1[:, lane], 0.0
+            )
+            d_norm = r.slope0[j, at, :] * d_field.astype(BF16).astype(F32)
+            r.fbuf[j, at, :] = d_norm
+            centred = (r.h0[j, at, :] - norm[0, 0:1, lane]) * norm[0, 1:2, lane]
+            first = first + jnp.sum(d_norm, 0, keepdims=True)
+            second = second + jnp.sum(d_norm * centred, 0, keepdims=True)
+        r.ex_out[3, 0:1, lane] = first
+        r.ex_out[3, 1:2, lane] = second
+        return 0
+
+    r.ex_out[3] = jnp.zeros((8, width), F32)
+    lax.fori_loop(0, n_lane, back_0, 0)
+    ex_start(3)
+    for k in range(n_z):
+        rs_c(2, k)
+    back_terms(3, 0)
+
+    def sums_copy(p, q):
+        return remote(
+            r.sums,
+            r.sums_in.at[q],
+            r.sums_s.at[p],
+            r.sums_r.at[p],
+            (plane[p], d),
+        )
+
+    for p in range(3):
+        sums_copy(p, s).start()
+    r.sums_in[s] = r.sums[...]
+
+    def hidden_grad_0(row):
+        def value(j):
+            lane = lane_at(j)
+            norm = r.norm
+            rows = slice(row * cols, (row + 1) * cols)
+            out = r.fbuf[j, rows, :] * norm[0, 2:3, lane] - (
+                norm[0, 4:5, lane] + (r.h0[j, rows, :] - norm[0, 0:1, lane]) * norm[0, 5:6, lane]
+            )
+            return jnp.where(valid_rows(row * cols, cols), out, 0.0)
+
+        return value
+
+    shift_in(hidden_grad_0(0), r.dc, 1)
+    shift_in(hidden_grad_0(1), r.dc, 2)
+    halo_start(3, r.dc)
+    for k in range(n_z):
+        conv_weight(0, r.xc0, k)
+        rs_a(0, k)
+        if k > 0:
+            rs_b(0, k - 1)
+    rs_b(0, n_z - 1)
+    for k in range(n_z):
+        rs_c(1, k)
+    rs_d(2)
+    rs_d(1)
+
+    halo_finish(3, r.dc)
+    conv_back(r.dc, r.w0)
+
+    def image_out(j, _):
+        lane = lane_at(j)
+        for i in range(4):
+            rows = slice(i * quarter_rows, (i + 1) * quarter_rows)
+            r.xin[rows, lane] = jnp.where(
+                valid_rows(i * quarter_rows, quarter_rows), r.fbuf[j, rows, :], 0.0
+            ).astype(BF16)
+        return 0
+
+    lax.fori_loop(0, n_lane, image_out, 0)
+    image_store = pltpu.make_async_copy(r.xin, out_image.at[0], r.store.at[1])
+    image_store.start()
+
+    for k in range(n_z):
+        rs_c(0, k)
+
+    def conv_out(kind, layer, i):
+        rs_e(kind)
+        copies = []
+        for j in range(n_lane):
+            lane = slice(j * lanes, (j + 1) * lanes)
+            staging[layer][j, 0:conv_rows, :] = r.td[kind][:, lane].astype(F32)
+            copies.append(
+                pltpu.make_async_copy(
+                    staging[layer].at[j, 0:conv_rows],
+                    out_conv.at[layer, :, lane],
+                    r.store.at[i + j],
+                )
+            )
+            copies[-1].start()
+        return copies
+
+    conv_store_1 = conv_out(2, 1, 4)
+    rs_e(1)
+    for l in range(2):
+        for t in range(tasks):
+            at = (l * tasks + t) * e_rows
+            r.est[l, t] = r.td[1][at : at + e_rows, :].astype(F32)
+            at = at + 2 * tasks * e_rows
+            for k in range(n_sub):
+                r.sst[l, t, k * e_rows : (k + 1) * e_rows, :] = r.td[1][
+                    at : at + e_rows, k * lanes : (k + 1) * lanes
+                ].astype(F32)
+    squeeze_store = pltpu.make_async_copy(r.sst, out_squeeze, r.store.at[2])
+    expand_store = pltpu.make_async_copy(r.est, out_expand, r.store.at[3])
+    squeeze_store.start()
+    expand_store.start()
+    for p in range(3):
+        sums_copy(p, plane[p]).wait_recv()
+    total = r.sums_in[0]
+    for i in range(1, 4):
+        total = total + r.sums_in[i]
+    for l in range(2):
+        out_bias[l : l + 1, :] = total[2 * l : 2 * l + 1, :]
+        out_gain[l : l + 1, :] = total[2 * l + 1 : 2 * l + 2, :]
+    rs_d(0)
+    conv_store_0 = conv_out(0, 0, 4 + n_lane)
+    for kind in range(3):
+        rs_end(kind)
+    for p in range(3):
+        sums_copy(p, s).wait_send()
+    for k in range(4):
+        for step in range(1, n_dp):
+            ex_copy(k, step, d).wait_send()
+    halo_sent(0, r.xc0)
+    halo_sent(1, r.xc1)
+    halo_sent(3, r.dc)
+    for copy in (
+        task_store,
+        image_store,
+        squeeze_store,
+        expand_store,
+        *conv_store_1,
+        *conv_store_0,
+    ):
+        copy.wait()
+
+
+def fused(images, counts, pool_index, conv_w, squeeze_w, expand_w, gain, bias, cotangent):
+    n_dp = lax.axis_size("dp")
+    here = lax.axis_index("section")
+    micro, pixels, width = images.shape
+    tasks, bottle = squeeze_w.shape[1], squeeze_w.shape[3]
+    cols = 2 * pool_index.shape[2]
+    windows = cols // 2
+    own_pick = lax.dynamic_index_in_dim(pool_index, here, 0, keepdims=False)
+    pick = jnp.broadcast_to(own_pick.reshape(windows, 1), (windows, 128))
+    conv_rows = conv_w.shape[1]
+    gate_rows = 4 * tasks * expand_w.shape[2]
+    shard_rows = (conv_rows, gate_rows, conv_rows)
+    n_z = n_dp // 2
+    vm = pltpu.VMEM
+    dma = pltpu.SemaphoreType.DMA
+    scratch = dict(
+        load=dma((5 + 2 * (width // 128),)),
+        store=dma((4 + 2 * (width // 128),)),
+        sst=vm(squeeze_w.shape, F32),
+        est=vm(expand_w.shape, F32),
+        xin=vm((pixels, width), BF16),
+        cin=vm((tasks, windows, width), BF16),
+        w0=vm((n_dp * conv_rows, width), BF16),
+        gp=vm((n_dp * gate_rows, width), BF16),
+        w1=vm((n_dp * conv_rows, width), BF16),
+        g1=vm((n_dp * conv_rows, width), BF16),
+        sq_w=vm((2, width, tasks * bottle), BF16),
+        ex_w=vm((2, tasks, bottle, width), BF16),
+        ag_zs=dma((3, n_z - 1)),
+        ag_zr=dma((3, n_z - 1)),
+        ag_ps=dma((3, 3 * (n_z - 1))),
+        ag_pr=dma((3, 3 * (n_z - 1))),
+        ag_ss=dma((3, n_z)),
+        ag_sr=dma((3, n_z)),
+        mp=vm((windows, 128), F32),
+        halo=vm((4, 2, cols, width), BF16),
+        halo_s=dma((4, 2)),
+        halo_r=dma((4, 2)),
+        ex_out=vm((4, 8, width), F32),
+        ex_in=vm((4, n_dp, 8, width), F32),
+        ex_s=dma((4, n_dp - 1)),
+        ex_r=dma((4, n_dp - 1)),
+        norm=vm((2, 8, width), F32),
+        xc0=vm((4 * cols, 3 * width), BF16),
+        xc1=vm((4 * cols, 3 * width), BF16),
+        dc=vm((4 * cols, 3 * width), BF16),
+        h0=vm((width // 128, pixels, 128), F32),
+        h1=vm((width // 128, pixels, 128), F32),
+        slope0=vm((width // 128, pixels, 128), F32),
+        fbuf=vm((width // 128, pixels, 128), F32),
+        f1p=vm((windows, width), F32),
+        f1b=vm((windows, width), BF16),
+        excited0=vm((windows, tasks * bottle), BF16),
+        eslope0=vm((windows, tasks * bottle), F32),
+        gate0=vm((tasks, windows, width), F32),
+        t1=vm((tasks, windows, width), BF16),
+        f2p=vm((windows, width), F32),
+        slope1=vm((windows, width), F32),
+        centred1=vm((windows, width), F32),
+        df2=vm((windows, width), F32),
+        df1=vm((windows, width), F32),
+        gs_st=vm((width, bottle), F32),
+        ge_st=vm((bottle, width), F32),
+        sums=vm((8, width), F32),
+        sums_in=vm((4, 8, width), F32),
+        sums_s=dma((3,)),
+        sums_r=dma((3,)),
+        rs_as=dma((3, n_z)),
+        rs_ar=dma((3, n_z)),
+        rs_bs=dma((3, n_z, 3)),
+        rs_br=dma((3, n_z, 3)),
+        rs_cs=dma((3, n_z - 1)),
+        rs_cr=dma((3, n_z - 1)),
+        rs_ds=dma((3, 3)),
+        rs_dr=dma((3, 3)),
+    )
+    quarters = [rows // 4 for rows in shard_rows]
+    scratch.update(
+        ra=[vm((n_z, rows, width), BF16) for rows in shard_rows],
+        rb=[vm((3, n_z, rows, width), BF16) for rows in quarters],
+        qs=[vm((n_z - 1, rows, width), BF16) for rows in quarters],
+        qf=[vm((rows, width), F32) for rows in quarters],
+        rc=[vm((n_z - 1, rows, width), BF16) for rows in quarters],
+        td=[vm((rows, width), BF16) for rows in shard_rows],
+    )
+    buffers, tree = jax.tree.flatten(scratch, is_leaf=lambda v: not isinstance(v, (dict, list)))
+    dims = types.SimpleNamespace(
+        tree=tree,
+        n_dp=n_dp,
+        cols=cols,
+        pixels=pixels,
+        width=width,
+        tasks=tasks,
+        bottle=bottle,
+        shard_rows=shard_rows,
+    )
+    any_spec = pl.BlockSpec(memory_space=pl.ANY)
+    vmem_spec = pl.BlockSpec(memory_space=pltpu.VMEM)
+    smem_spec = pl.BlockSpec(memory_space=pltpu.SMEM)
+    return pl.pallas_call(
+        functools.partial(step_kernel, dims),
+        out_shape=(
+            jax.ShapeDtypeStruct((1, tasks, windows, width), BF16),
+            jax.ShapeDtypeStruct((1, pixels, width), BF16),
+            jax.ShapeDtypeStruct(conv_w.shape, F32),
+            jax.ShapeDtypeStruct(squeeze_w.shape, F32),
+            jax.ShapeDtypeStruct(expand_w.shape, F32),
+            jax.ShapeDtypeStruct(gain.shape, F32),
+            jax.ShapeDtypeStruct(bias.shape, F32),
+        ),
+        in_specs=[smem_spec, vmem_spec, vmem_spec, vmem_spec] + [any_spec] * 5,
+        out_specs=(any_spec,) * 5 + (vmem_spec,) * 2,
+        scratch_shapes=tuple(buffers),
+        compiler_params=pltpu.CompilerParams(
+            collective_id=0, has_side_effects=True, vmem_limit_bytes=VMEM_BYTES
+        ),
+    )(counts, pick, gain, bias, images, conv_w, squeeze_w, expand_w, cotangent)
+
+
+def fits_kernel(mesh, args):
+    images, counts, pool_index, conv_w, squeeze_w, expand_w = args[:6]
+    sections, n_dp = mesh.shape["section"], mesh.shape["dp"]
+    conv_rows = conv_w.shape[1] // n_dp
+    e_rows = expand_w.shape[2] // n_dp
+    return (
+        sections == 4
+        and images.shape[0] == sections
+        and n_dp % 2 == 0
+        and pool_index.shape[1] == n_dp
+        and conv_rows % 64 == 0
+        and e_rows == 16
+        and squeeze_w.shape[2] // n_dp == 4 * e_rows
+        and squeeze_w.shape[3] == 128
+        and images.shape[2] == 4 * 128
+    )
+
+
 def solution(mesh):
     placed = (
         P(None, "dp", None),
@@ -228,8 +1237,12 @@
         P(),
         P(None, None, "dp", None),
     )
-    return jax.shard_map(
-        on_device,
+    def run(*args):
+        return mapped(fused if fits_kernel(mesh, args) else on_device)(*args)
+
+    def mapped(body):
+        return jax.shard_map(
+        body,
         mesh=mesh,
         in_specs=placed,
         out_specs=(
@@ -243,3 +1256,5 @@
         ),
         check_vma=False,
     )
+
+    return run

time: 680 us -> 182 us (0.27); the launches traced: 671 us -> 182 us
  waiting for transfers between devices: 201 us -> 0 us
  blocking collectives: 193 us -> 0 us
  Pallas kernels: 0 us -> 171 us
  matrix products: 101 us -> 0 us
  other arithmetic: 66.1 us -> 0 us
  local copies, waits for them, and re-layouts: 73.9 us -> 10.8 us
  starting transfers between devices: 19.9 us -> 0 us
  between operations: 16.7 us -> 0.68 us
    pallas_call x0 -> x1, Pallas kernels: none -> 171 us  [fused(): pl.pallas_call(functools.partial(step_kernel, dims), out_shape=(jax.Shape...]
    reduce_scatter x6 -> x0, waiting for transfers between devices: 111 us -> none  [reduced(): part = lax.psum_scatter(value, 'dp', scatter_dimension=axis, tiled=True)]
    psum x6 -> x0, blocking collectives: 110 us -> none  [the longest x1 40.9 us: on_device(): gain_grad, bias_grad = lax.psum((grads[3], grads[4]), ('section', 'dp'))]
    psum x2 -> x0, waiting for transfers between devices: 88.4 us -> none  [reduced(): return lax.psum(part.astype(BF16), 'section').astype(F32)]
    all_gather x4 -> x0, blocking collectives: 83.1 us -> none  [gather(): return lax.all_gather(value.astype(BF16), 'dp', axis=axis, tiled=True)]
    conv_general_dilated x6 -> x0, matrix products: 67.4 us -> none  [the longest x2 44.8 us: conv_weight_grad(): lax.conv_general_dilated(padded[None], d_hidden[None], (1, 1), ((0, 0), (...]
    dot_general x12 -> x0, matrix products: 33.9 us -> none  [the longest x2 11.1 us: gate_forward(): jnp.einsum('tpb,tbc->tpc', excited, w_expand, preferred_element_type=F32)]
    another operation x18 -> x0, other arithmetic: 22.8 us -> none  [the longest x3 7.19 us: on_device(): conv_grad = jnp.stack([reduced(g, 0) for g in grads[0]])]
  transfers between devices with their start and end apart: 18 -> 0, of which waited for: 4 -> 0; matrix products, arithmetic and copies ran while one was open for 30% -> 0% of each run, Pallas kernels for 0% -> 0%
where the time goes in v2:
time: 182 us
  Pallas kernels  171 us (94%)
  local copies, waits for them, and re-layouts  10.8 us (6%)
    pallas_call x1, Pallas kernels, fused(): pl.pallas_call(functools.partial(step_kernel, dims), out_shape=(jax.Shape...  171 us
    unnamed x20, local copies, waits for them, and re-layouts  10.1 us

profile of v2, /device:TPU:0, one launch (start us, length us, event | category | flops | bytes accessed | tf_op | source)
XLA Modules:
  0.0 182.1 jit_solution(7608093133736853930)
XLA Ops:
  0.6 0.0 copy-start
  0.7 0.7 copy-done
  1.3 1.3 copy.16.counts
  2.6 0.7 broadcast_in_dim.8.pick_ref
  3.4 170.6 %shard_map.144 = (bf16[1,3,192,512]{3,2,1,0:T(8,128)(2,1)}, bf16[1,768,512]{2,1,0:T(8,128)(2,1)}, f32[2,576,512]{2,1,0:T(8,128)}, f32[2,3,64,128]{3,2,1,0:T(8,12...) custom-call(s32[4,1]{1,0:T(4,128)} %copy.16.counts, s32[192,128]{1,0:T(8,128)} %broadcast_in_dim.8.pick_ref, ...), custom_call_target="tpu_custom_call" | custom-call | tf_op jit(solution)/shard_map/pallas_call | solution.py:1190
  174.0 0.0 copy-start.1
  174.0 2.1 %copy.24 = bf16[1,3,192,512]{3,2,1,0:T(8,128)(2,1)} copy(bf16[1,3,192,512]{3,2,1,0:T(8,128)(2,1)} %get-tuple-element.14) | data formatting | bytes 1179648
  176.1 2.1 %copy.25 = bf16[1,768,512]{2,1,0:T(8,128)(2,1)} copy(bf16[1,768,512]{2,1,0:T(8,128)(2,1)} %get-tuple-element.15) | data formatting | bytes 1572864
  178.1 0.0 copy-done.1
  178.1 0.0 copy-start.3
  178.1 0.0 copy-start.2
  178.1 0.0 copy-start.5
  178.1 0.0 copy-start.4
  178.1 1.4 copy.26
  179.5 0.0 copy-done.3
  179.6 0.7 copy.27
  180.2 0.0 copy-done.2
  180.2 0.7 copy.28
  180.9 0.0 copy-done.5
  180.9 0.6 copy.29
  181.5 0.0 copy-done.4
  181.5 0.6 copy.30
  (1 shorter events, 0.0 us)
Async XLA Ops:
  0.6 0.7 copy-start
  174.0 4.1 %copy-start.1 = (f32[2,576,512]{2,1,0:T(8,128)S(1)}, f32[2,576,512]{2,1,0:T(8,128)}, u32[]{:S(2)}) copy-start(f32[2,576,512]{2,1,0:T(8,128)} %get-tuple-element.16) | copy-start | bytes 7077892
  178.1 1.4 copy-start.3
  178.1 2.1 %copy-start.2 = (f32[2,3,16,512]{3,2,1,0:T(8,128)S(1)}, f32[2,3,16,512]{3,2,1,0:T(8,128)}, u32[]{:S(2)}) copy-start(f32[2,3,16,512]{3,2,1,0:T(8,128)} %get-tuple-element.18) | copy-start | bytes 589828
  178.1 2.8 %copy-start.5 = (f32[2,512]{1,0:T(2,128)S(1)}, f32[2,512]{1,0:T(2,128)}, u32[]{:S(2)}) copy-start(f32[2,512]{1,0:T(2,128)} %get-tuple-element.19) | copy-start | bytes 12292
  178.1 3.4 %copy-start.4 = (f32[2,512]{1,0:T(2,128)S(1)}, f32[2,512]{1,0:T(2,128)}, u32[]{:S(2)}) copy-start(f32[2,512]{1,0:T(2,128)} %get-tuple-element.20) | copy-start | bytes 12292

commit v3 on v2

--- a/solution.py
+++ b/solution.py
@@ -250,7 +250,7 @@
 def step_kernel(
     dims,
     counts,
-    pick_ref,
+    picks,
     gain,
     bias,
     images,
@@ -260,13 +260,14 @@
     cotangent,
     out_task,
     out_image,
-    out_conv,
-    out_squeeze,
-    out_expand,
+    out_reduced_0,
+    out_reduced_1,
+    out_reduced_2,
     out_gain,
     out_bias,
     *scratch,
 ):
+    out_reduced = (out_reduced_0, out_reduced_1, out_reduced_2)
     r = types.SimpleNamespace(**jax.tree.unflatten(dims.tree, scratch))
     n_dp, cols, pixels, width, tasks, bottle = (
         dims.n_dp,
@@ -334,14 +335,12 @@
         load(3, images.at[s], r.xin),
         load(4, cotangent.at[s], r.cin),
     ]
-    for j in range(n_lane):
-        conv_load(0, j).start()
-    for item in loads[:2]:
-        item.start()
-    for j in range(n_lane):
-        conv_load(1, j).start()
-    for item in loads[2:]:
-        item.start()
+    loads[2].start()
+    for layer in range(2):
+        for j in range(n_lane):
+            conv_load(layer, j).start()
+    for i in (0, 1, 3):
+        loads[i].start()
 
     full = [r.w0, r.gp, r.w1]
 
@@ -353,53 +352,129 @@
         rows = shard_rows[kind]
         return buf.at[pl.ds(al(which * rows + q * (rows // 4), 16), rows // 4)]
 
-    def ag_z_copy(kind, step, owner):
-        view = quarter(kind, full[kind], owner, s)
+
+    def z_of(way, hop):
+        return z_at(n_z - hop if way == 0 else hop)
+
+    def has(way, hop):
+        return z >= hop if way == 0 else z < n_z - hop
+
+    def hop_id(way, hop):
+        return (hop - 1) * 2 + way
+
+    def ag_z_copy(kind, way, hop, owner):
+        view = quarter(kind, full[kind], 2 * owner + c, s)
+        i = hop_id(way, hop)
         return remote(
             view,
             view,
-            r.ag_zs.at[kind, step - 1],
-            r.ag_zr.at[kind, step - 1],
-            (s, 2 * z_at(step) + c),
-        )
-
-    def ag_p_copy(kind, step, p, q):
-        owner = 2 * z_at(n_z - step) + c
-        view = quarter(kind, full[kind], owner, q)
-        i = (step - 1) * 3 + p
-        return remote(view, view, r.ag_ps.at[kind, i], r.ag_pr.at[kind, i], (plane[p], d))
-
-    def ag_s_copy(kind, step, core):
-        view = shard(kind, full[kind], 2 * z_at(n_z - step if step else 0) + core)
-        return remote(view, view, r.ag_ss.at[kind, step], r.ag_sr.at[kind, step], (s, sib))
+            r.ag_zs.at[kind, i],
+            r.ag_zr.at[kind, i],
+            (s, 2 * z_at(1 if way == 0 else n_z - 1) + c),
+        )
+
+    def ag_pass(kind, way, hop, do):
+        here_has = has(way, hop - 1) if hop > 1 else True
+        there = z < n_z - 1 if way == 0 else z > 0
+        owner = z_of(way, hop - 1)
+
+        @pl.when(jnp.logical_and(here_has, there))
+        def _():
+            do(ag_z_copy(kind, way, hop, owner))
+
+    halves = [slice(0, width // 2), slice(width // 2, width)]
+
+    def ag_p_copy(kind, way, hop, leg, q):
+        view = quarter(kind, full[kind], 2 * z_of(way, hop) + c, q)
+        if leg >= 2:
+            view = view.at[:, halves[leg - 2]]
+        to = plane[(0, 1, 1, 0)[leg]]
+        i = hop_id(way, hop) * 4 + leg
+        return remote(view, view, r.ag_ps.at[kind, i], r.ag_pr.at[kind, i], (to, d))
+
+    def ag_own_copy(kind, core):
+        view = shard(kind, full[kind], 2 * z + core)
+        return remote(view, view, r.ag_os.at[kind], r.ag_or.at[kind], (s, sib))
+
+    def ag_s_copy(kind, way, hop, q, i, core):
+        view = quarter(kind, full[kind], 2 * z_of(way, hop) + core, q)
+        i = hop_id(way, hop) * 4 + i
+        return remote(view, view, r.ag_ss.at[kind, i], r.ag_sr.at[kind, i], (s, sib))
+
+    others = [s] + plane
 
     def ag_start(kind):
-        for step in range(1, n_z):
-            ag_z_copy(kind, step, d).start()
-        ag_s_copy(kind, 0, c).start()
-
-    def ag_z(kind, step):
-        owner = 2 * z_at(n_z - step) + c
-        ag_z_copy(kind, step, owner).wait_recv()
-        for p in range(3):
-            ag_p_copy(kind, step, p, s).start()
-
-    def ag_p(kind, step):
-        for p in range(3):
-            ag_p_copy(kind, step, p, plane[p]).wait_recv()
-        ag_s_copy(kind, step, c).start()
+        for way in range(2):
+            ag_pass(kind, way, 1, lambda copy: copy.start())
+        ag_own_copy(kind, c).start()
+
+    def for_hop(hop, do):
+        for way in range(2):
+
+            @pl.when(has(way, hop))
+            def _():
+                do(way)
+
+    def ag_z(kind, hop):
+        def do(way):
+            ag_z_copy(kind, way, hop, z_of(way, hop)).wait_recv()
+            if hop < n_z - 1:
+                ag_pass(kind, way, hop + 1, lambda copy: copy.start())
+            if kind != 1:
+                for leg in range(2):
+                    ag_p_copy(kind, way, hop, leg, s).start()
+            ag_s_copy(kind, way, hop, s, 0, c).start()
+
+        for_hop(hop, do)
+
+    def ag_l(kind, hop):
+        def do(way):
+            for leg in range(2):
+                ag_p_copy(kind, way, hop, leg, s).start()
+
+        for_hop(hop, do)
+
+    def ag_r(kind, hop):
+        def do(way):
+            for leg in range(2):
+                ag_p_copy(kind, way, hop, leg, plane[leg]).wait_recv()
+                ag_p_copy(kind, way, hop, 2 + leg, plane[leg]).start()
+                ag_s_copy(kind, way, hop, plane[leg], 1 + leg, c).start()
+
+        for_hop(hop, do)
+
+    def ag_p(kind, hop):
+        def do(way):
+            for leg in range(2):
+                ag_p_copy(kind, way, hop, 2 + leg, plane[2]).wait_recv()
+            ag_s_copy(kind, way, hop, plane[2], 3, c).start()
+
+        for_hop(hop, do)
 
     def ag_sib(kind):
-        for step in range(n_z):
-            ag_s_copy(kind, step, 1 - c).wait_recv()
+        ag_own_copy(kind, 1 - c).wait_recv()
+        for hop in range(1, n_z):
+
+            def do(way):
+                for i in range(4):
+                    ag_s_copy(kind, way, hop, others[i], i, 1 - c).wait_recv()
+
+            for_hop(hop, do)
 
     def ag_end(kind):
-        for step in range(1, n_z):
-            ag_z_copy(kind, step, d).wait_send()
-            for p in range(3):
-                ag_p_copy(kind, step, p, s).wait_send()
-        for step in range(n_z):
-            ag_s_copy(kind, step, c).wait_send()
+        ag_own_copy(kind, c).wait_send()
+        for hop in range(1, n_z):
+
+            def do(way):
+                for leg in range(2):
+                    ag_p_copy(kind, way, hop, leg, s).wait_send()
+                    ag_p_copy(kind, way, hop, 2 + leg, plane[leg]).wait_send()
+                for i in range(4):
+                    ag_s_copy(kind, way, hop, others[i], i, c).wait_send()
+
+            for way in range(2):
+                ag_pass(kind, way, hop, lambda copy: copy.wait_send())
+            for_hop(hop, do)
 
     def cast_conv(layer, buf):
         for j in range(n_lane):
@@ -424,24 +499,14 @@
     def sq_row(which, l, t):
         return al(which * g_rows + (2 * tasks + l * tasks + t) * e_rows, 16)
 
-    cast_conv(0, r.w0)
-    pl.semaphore_wait(barrier, n_dp - 1 + 3)
-    ag_start(0)
-    loads[0].wait()
-    loads[1].wait()
-    for l in range(2):
-        for t in range(tasks):
-            r.gp[pl.ds(ex_row(d, l, t), e_rows), :] = r.est[l, t].astype(BF16)
-            for k in range(n_sub):
-                r.gp[pl.ds(sq_row(d, l, t), e_rows), k * lanes : (k + 1) * lanes] = r.sst[
-                    l, t, k * e_rows : (k + 1) * e_rows, :
-                ].astype(BF16)
-    ag_start(1)
-    cast_conv(1, r.w1)
-    ag_start(2)
-
-    count = counts[s, 0]
-    pick_tile = pick_ref[...]
+    count = counts[s]
+    wide = 2 * lanes
+    pick_row = jnp.concatenate(
+        [picks[s].astype(F32), jnp.zeros((1, wide - windows), F32)], axis=1
+    )
+    pick_tile = jnp.broadcast_to(pick_row, (lanes, wide)).T[:windows, :].astype(jnp.int32)
+    pick_ref = r.pick
+    pick_ref[...] = pick_tile
     slot_pick = (
         (pick_tile // 2) * cols
         + 2 * lax.broadcasted_iota(jnp.int32, (windows, lanes), 0)
@@ -480,7 +545,7 @@
     def halo_down(e, buf):
         return remote(
             buf.at[2 * cols : 3 * cols, width : 2 * width],
-            r.halo.at[e, 0],
+            r.halo.at[e % 2, 0],
             r.halo_s.at[e, 0],
             r.halo_r.at[e, 0],
             (s, rem(d + 1, n_dp)),
@@ -489,7 +554,7 @@
     def halo_up(e, buf):
         return remote(
             buf.at[cols : 2 * cols, width : 2 * width],
-            r.halo.at[e, 1],
+            r.halo.at[e % 2, 1],
             r.halo_s.at[e, 1],
             r.halo_r.at[e, 1],
             (s, rem(d + n_dp - 1, n_dp)),
@@ -513,8 +578,8 @@
         def _():
             halo_up(e, buf).wait_recv()
 
-        shift_in(lambda j: r.halo[e, 0, :, lane_at(j)].astype(F32), buf, 0)
-        shift_in(lambda j: r.halo[e, 1, :, lane_at(j)].astype(F32), buf, 3)
+        shift_in(lambda j: r.halo[e % 2, 0, :, lane_at(j)].astype(F32), buf, 0)
+        shift_in(lambda j: r.halo[e % 2, 1, :, lane_at(j)].astype(F32), buf, 3)
 
     def halo_sent(e, buf):
         @pl.when(d < n_dp - 1)
@@ -545,33 +610,41 @@
         total = r.ex_in[k, 0]
         for i in range(1, n_dp):
             total = total + r.ex_in[k, i]
-        return total
-
-    def conv_forward(xc, w, h):
+        return [
+            jnp.concatenate([total[i * n_lane + j : i * n_lane + j + 1] for j in range(n_lane)], 1)
+            for i in range(2)
+        ]
+
+    def ex_put(k, i, j, value):
+        r.ex_out[k, pl.ds(i * n_lane + j, 1), :] = value
+
+    def conv_forward(xc, w, h, row):
         span = 3 * width
-        half = width // 2
-        for n in range(2):
-            acc = None
-            for a in range(3):
-                term = dot(
-                    xc[a * cols : a * cols + pixels, :],
-                    w[a * span : (a + 1) * span, n * half : (n + 1) * half],
-                )
-                acc = term if acc is None else acc + term
-            for j in range(n_lane // 2):
-                h[n * (n_lane // 2) + j] = acc[:, j * lanes : (j + 1) * lanes]
-
-    def conv_back(dc, w):
         acc = None
         for a in range(3):
+            term = dot(
+                xc[(a + row) * cols : (a + row + 1) * cols, :], w[a * span : (a + 1) * span, :]
+            )
+            acc = term if acc is None else acc + term
+        for j in range(n_lane):
+            h[j, row * cols : (row + 1) * cols, :] = acc[:, j * lanes : (j + 1) * lanes]
+
+    def conv_back(dc, w, row, part):
+        acc = None
+        for a in range(3):
+            block = 2 - a + row
+            if (block in (0, 3)) != (part == 1):
+                continue
             for b in range(3):
                 term = dot_nt(
-                    dc[(2 - a) * cols : (2 - a) * cols + pixels, (2 - b) * width : (3 - b) * width],
+                    dc[block * cols : (block + 1) * cols, (2 - b) * width : (3 - b) * width],
                     w[(3 * a + b) * width : (3 * a + b + 1) * width, :],
                 )
                 acc = term if acc is None else acc + term
         for j in range(n_lane):
-            r.fbuf[j] = acc[:, j * lanes : (j + 1) * lanes]
+            at = (j, slice(row * cols, (row + 1) * cols), slice(None))
+            piece = acc[:, j * lanes : (j + 1) * lanes]
+            r.fbuf[at] = piece if part == 0 else r.fbuf[at] + piece
 
     quarter_rows = pixels // 4
 
@@ -584,17 +657,16 @@
                 kept = jnp.where(valid_rows(i * quarter_rows, quarter_rows), v, 0.0)
                 first = first + jnp.sum(kept, 0, keepdims=True)
                 second = second + jnp.sum(kept * v, 0, keepdims=True)
-            r.ex_out[k, 0:1, lane_at(j)] = first
-            r.ex_out[k, 1:2, lane_at(j)] = second
+            ex_put(k, 0, j, first)
+            ex_put(k, 1, j, second)
             return 0
 
-        r.ex_out[k] = jnp.broadcast_to(count.astype(F32), (8, width))
         lax.fori_loop(0, n_lane, body, 0)
 
     def norm_of(sums, layer):
-        total = sums[2:3, :]
-        centre = sums[0:1, :] / total
-        inverse = lax.rsqrt(sums[1:2, :] / total - centre * centre + EPS)
+        total = r.total[0:1, :]
+        centre = sums[0] / total
+        inverse = lax.rsqrt(sums[1] / total - centre * centre + EPS)
         r.norm[layer, 0:1, :] = centre
         r.norm[layer, 1:2, :] = inverse
         r.norm[layer, 2:3, :] = gain[layer : layer + 1, :] * inverse
@@ -622,22 +694,44 @@
 
     shift_in(image_row(0), r.xc0, 1)
     shift_in(image_row(1), r.xc0, 2)
+    cast_conv(0, r.w0)
+    pl.semaphore_wait(barrier, n_dp - 1 + 3)
+    ag_start(0)
+    r.ex_out[4] = jnp.broadcast_to(count.astype(F32), (8, lanes))
+    ex_start(4)
+    loads[0].wait()
+    loads[1].wait()
+    for l in range(2):
+        for t in range(tasks):
+            r.gp[pl.ds(ex_row(d, l, t), e_rows), :] = r.est[l, t].astype(BF16)
+            for k in range(n_sub):
+                r.gp[pl.ds(sq_row(d, l, t), e_rows), k * lanes : (k + 1) * lanes] = r.sst[
+                    l, t, k * e_rows : (k + 1) * e_rows, :
+                ].astype(BF16)
+    cast_conv(1, r.w1)
+    ag_z(0, 1)
+    ag_z(0, 2)
     halo_start(0, r.xc0)
-    for step in range(1, n_z):
-        ag_z(0, step)
+    ag_r(0, 1)
+    ag_z(0, 3)
+    ag_start(2)
+    ag_r(0, 2)
+    ag_p(0, 1)
+    ag_r(0, 3)
+    ag_p(0, 2)
     halo_finish(0, r.xc0)
-    for step in range(1, n_z):
-        ag_z(1, step)
-    for step in range(1, n_z):
-        ag_p(0, step)
-        ag_z(2, step)
+    ag_z(2, 1)
+    ag_start(1)
+    ag_p(0, 3)
+    r.total[...] = jnp.concatenate([ex_finish(4)[0]] * 8, axis=0)
     ag_sib(0)
-
-    conv_forward(r.xc0, r.w0, r.h0)
+    conv_forward(r.xc0, r.w0, r.h0, 0)
+    conv_forward(r.xc0, r.w0, r.h0, 1)
     stats(r.h0, 0)
     ex_start(0)
-    for step in range(1, n_z):
-        ag_p(1, step)
+    halo_sent(0, r.xc0)
+    ag_z(2, 2)
+    ag_r(2, 1)
     norm_of(ex_finish(0), 0)
 
     def block_0(j, _):
@@ -660,6 +754,25 @@
     shift_in(lambda j: r.fbuf[j, 0:cols, :], r.xc1, 1)
     shift_in(lambda j: r.fbuf[j, cols : 2 * cols, :], r.xc1, 2)
     halo_start(1, r.xc1)
+    ag_z(2, 3)
+    ag_r(2, 2)
+    ag_p(2, 1)
+    ag_r(2, 3)
+    ag_p(2, 2)
+    for hop in range(1, n_z):
+        ag_z(1, hop)
+        ag_l(1, hop)
+    halo_finish(1, r.xc1)
+    ag_p(2, 3)
+    ag_sib(2)
+    conv_forward(r.xc1, r.w1, r.h1, 0)
+    for hop in range(1, n_z):
+        ag_r(1, hop)
+    conv_forward(r.xc1, r.w1, r.h1, 1)
+    stats(r.h1, 1)
+    ex_start(1)
+    for hop in range(1, n_z):
+        ag_p(1, hop)
     ag_sib(1)
 
     def unpack(i, _):
@@ -692,17 +805,10 @@
         return 0
 
     lax.fori_loop(0, tasks, gate_0, 0)
-    halo_finish(1, r.xc1)
-    for step in range(1, n_z):
-        ag_p(2, step)
-    ag_sib(2)
-
-    conv_forward(r.xc1, r.w1, r.h1)
-    stats(r.h1, 1)
-    ex_start(1)
+    norm_of(ex_finish(1), 1)
+
     for kind in range(3):
         ag_end(kind)
-    norm_of(ex_finish(1), 1)
 
     def block_1(j, _):
         lane = lane_at(j)
@@ -714,24 +820,170 @@
         return 0
 
     lax.fori_loop(0, n_lane, block_1, 0)
+    grads = [r.w1, r.gp, r.g1]
+
+    def pair_of(k):
+        return z_at(1 + k)
+
+    def rs_a_copy(kind, k, core):
+        return remote(
+            shard(kind, grads[kind], 2 * pair_of(k) + core),
+            r.ra[kind].at[k],
+            r.rs_as.at[kind, k],
+            r.rs_ar.at[kind, k],
+            (s, sib),
+        )
+
+    def rs_b_copy(kind, k, way):
+        o = 2 * pair_of(k) + c
+        half = (0, 0, 1, 1, 0, 1)[way]
+        to = plane[(0, 0, 1, 1, 1, 0)[way]]
+        q = to if way in (0, 2, 4, 5) else plane[2]
+        return remote(
+            quarter(kind, grads[kind], o, q).at[:, halves[half]],
+            r.rb[kind].at[k, way],
+            r.rs_bs.at[kind, k, way],
+            r.rs_br.at[kind, k, way],
+            (to, d),
+        )
+
+    def rs_c_copy(kind, k):
+        return remote(
+            r.qs[kind].at[k],
+            r.rc[kind].at[k],
+            r.rs_cs.at[kind, k],
+            r.rs_cr.at[kind, k],
+            (s, 2 * pair_of(k) + c),
+        )
+
+    def rs_d_copy(kind, leg, q):
+        rows = shard_rows[kind] // 4
+        view = r.td[kind].at[pl.ds(al(q * rows, 16), rows)]
+        if leg >= 2:
+            view = view.at[:, halves[leg - 2]]
+        to = plane[(0, 1, 1, 0)[leg]]
+        return remote(view, view, r.rs_ds.at[kind, leg], r.rs_dr.at[kind, leg], (to, d))
+
+    def conv_weight(kind, xc, k):
+        tile = 2 * shard_rows[kind] // 3
+        per = 3 * width // tile
+
+        for i in range(3):
+            g = pair_of(k) * 3 + i
+            a = g // per
+            term = dot_tn(
+                xc[pl.ds(al(a * cols, 16), pixels), pl.ds(al((g % per) * tile, lanes), tile)],
+                r.dc[cols : 3 * cols, width : 2 * width],
+            )
+            grads[kind][pl.ds(al(g * tile, 16), tile), :] = term.astype(BF16)
+
+    def rs_a(kind, k):
+        rs_a_copy(kind, k, 1 - c).start()
+
+    def rs_b(kind, k):
+        rs_a_copy(kind, k, c).wait_recv()
+        rows = shard_rows[kind]
+        tile = rows // 4
+        start = (2 * pair_of(k) + c) * rows
+
+        def body(i, _):
+            at = pl.ds(al(start + i * tile, 16), tile)
+            grads[kind][at, :] = (
+                grads[kind][at, :].astype(F32)
+                + r.ra[kind][k, pl.ds(al(i * tile, 16), tile), :].astype(F32)
+            ).astype(BF16)
+            return 0
+
+        lax.fori_loop(0, 4, body, 0)
+        for way in range(4):
+            rs_b_copy(kind, k, way).start()
+
+    def quarter_at(kind, k, q):
+        rows = shard_rows[kind]
+        return pl.ds(al((2 * pair_of(k) + c) * rows + q * (rows // 4), 16), rows // 4)
+
+    def rs_r(kind, k):
+        for half in range(2):
+            rs_b_copy(kind, k, 2 * half).wait_recv()
+            rs_b_copy(kind, k, 2 * half + 1).wait_recv()
+            at = quarter_at(kind, k, plane[1 - half])
+            grads[kind][at, halves[half]] = (
+                grads[kind][at, halves[half]].astype(F32)
+                + r.rb[kind][k, 2 * half + 1].astype(F32)
+            ).astype(BF16)
+            rs_b_copy(kind, k, 4 + half).start()
+
+    def rs_c(kind, k):
+        at = quarter_at(kind, k, s)
+        parts = []
+        for half in range(2):
+            rs_b_copy(kind, k, 4 + half).wait_recv()
+            parts.append(
+                grads[kind][at, halves[half]].astype(F32)
+                + r.rb[kind][k, 2 * half].astype(F32)
+                + r.rb[kind][k, 4 + half].astype(F32)
+            )
+        total = jnp.concatenate(parts, axis=1)
+        if k < n_z - 1:
+            r.qs[kind][k] = total.astype(BF16)
+            rs_c_copy(kind, k).start()
+        else:
+            r.qf[kind][...] = total
+
+    def rs_d(kind):
+        total = r.qf[kind][...]
+        for k in range(n_z - 1):
+            rs_c_copy(kind, k).wait_recv()
+            total = total + r.rc[kind][k].astype(F32)
+        rows = shard_rows[kind] // 4
+        r.td[kind][pl.ds(al(s * rows, 16), rows), :] = total.astype(BF16)
+        for leg in range(2):
+            rs_d_copy(kind, leg, s).start()
+
+    def rs_dr(kind):
+        for leg in range(2):
+            rs_d_copy(kind, leg, plane[leg]).wait_recv()
+            rs_d_copy(kind, 2 + leg, plane[leg]).start()
+
+    def rs_e(kind):
+        for leg in range(2):
+            rs_d_copy(kind, 2 + leg, plane[2]).wait_recv()
+
+    def rs_end(kind):
+        for k in range(n_z):
+            rs_a_copy(kind, k, 1 - c).wait_send()
+            for way in range(6):
+                rs_b_copy(kind, k, way).wait_send()
+            if k < n_z - 1:
+                rs_c_copy(kind, k).wait_send()
+        for leg in range(2):
+            rs_d_copy(kind, leg, s).wait_send()
+            rs_d_copy(kind, 2 + leg, plane[leg]).wait_send()
+
     loads[3].wait()
     r.df2[...] = jnp.zeros_like(r.df2)
 
     def pack_grads(l, t, grad_squeeze, grad_expand):
-        r.gs_st[...] = grad_squeeze
-        r.ge_st[...] = grad_expand
+        r.fbuf[0, 0:width, :] = grad_squeeze
+        for j in range(n_lane):
+            r.fbuf[1, j * bottle : (j + 1) * bottle, :] = grad_expand[:, j * lanes : (j + 1) * lanes]
 
         def body(i, _):
-            r.gp[pl.ds(ex_row(i, l, t), e_rows), :] = r.ge_st[
-                pl.ds(al(i * e_rows, 16), e_rows), :
-            ].astype(BF16)
+            for j in range(n_lane):
+                lane = slice(j * lanes, (j + 1) * lanes)
+                r.gp[pl.ds(ex_row(i, l, t), e_rows), lane] = r.fbuf[
+                    1, pl.ds(al(j * bottle + i * e_rows, 16), e_rows), :
+                ].astype(BF16)
             for k in range(n_sub):
-                r.gp[pl.ds(sq_row(i, l, t), e_rows), k * lanes : (k + 1) * lanes] = r.gs_st[
-                    pl.ds(al(i * s_rows + k * e_rows, 16), e_rows), :
+                r.gp[pl.ds(sq_row(i, l, t), e_rows), k * lanes : (k + 1) * lanes] = r.fbuf[
+                    0, pl.ds(al(i * s_rows + k * e_rows, 16), e_rows), :
                 ].astype(BF16)
             return 0
 
         lax.fori_loop(0, n_dp, body, 0)
+
+    def kept(i):
+        return pl.ds(al(i * windows, 16), windows)
 
     def gate_1(t, _):
         w_s = r.sq_w[1, :, task_lane(t)]
@@ -749,7 +1001,19 @@
         d_source = dot_nt(d_squeezed, w_s)
         r.t1[t] = d_source.astype(BF16)
         r.df2[...] += d_source + mask_pick * d_task * value
-        pack_grads(1, t, dot_tn(source, d_squeezed), dot_tn(excited, d_expanded))
+        r.g1[kept(t), :] = source
+        r.g1[kept(tasks + t), :] = d_expanded
+        r.g1[kept(2 * tasks), task_lane(t)] = excited
+        r.g1[kept(2 * tasks + 1), task_lane(t)] = d_squeezed
+        return 0
+
+    def gate_1_weight(t, _):
+        pack_grads(
+            1,
+            t,
+            dot_tn(r.g1[kept(t), :], r.g1[kept(2 * tasks + 1), task_lane(t)]),
+            dot_tn(r.g1[kept(2 * tasks), task_lane(t)], r.g1[kept(tasks + t), :]),
+        )
         return 0
 
     lax.fori_loop(0, tasks, gate_1, 0)
@@ -760,11 +1024,10 @@
         lane = lane_at(j)
         d_norm = r.slope1[:, lane] * r.df2[:, lane].astype(BF16).astype(F32)
         r.df2[:, lane] = d_norm
-        r.ex_out[2, 0:1, lane] = jnp.sum(d_norm, 0, keepdims=True)
-        r.ex_out[2, 1:2, lane] = jnp.sum(d_norm * r.centred1[:, lane], 0, keepdims=True)
+        ex_put(2, 0, j, jnp.sum(d_norm, 0, keepdims=True))
+        ex_put(2, 1, j, jnp.sum(d_norm * r.centred1[:, lane], 0, keepdims=True))
         return 0
 
-    r.ex_out[2] = jnp.zeros((8, width), F32)
     lax.fori_loop(0, n_lane, back_1, 0)
     ex_start(2)
 
@@ -783,16 +1046,20 @@
         return 0
 
     lax.fori_loop(0, tasks, gate_0_back, 0)
+    lax.fori_loop(0, tasks, gate_1_weight, 0)
 
     r.sums[...] = jnp.zeros_like(r.sums)
 
     def back_terms(k, layer):
         sums = ex_finish(k)
-        r.sums[2 * layer : 2 * layer + 2, :] = sums[0:2, :]
+        r.sums[2 * layer : 2 * layer + 1, :] = sums[0]
+        r.sums[2 * layer + 1 : 2 * layer + 2, :] = sums[1]
         scale = gain[layer : layer + 1, :] * r.norm[layer, 3:4, :] * r.norm[layer, 1:2, :]
-        r.norm[layer, 4:5, :] = scale * sums[0:1, :]
-        r.norm[layer, 5:6, :] = scale * r.norm[layer, 1:2, :] * sums[1:2, :]
-
+        r.norm[layer, 4:5, :] = scale * sums[0]
+        r.norm[layer, 5:6, :] = scale * r.norm[layer, 1:2, :] * sums[1]
+
+    for k in range(n_z):
+        rs_a(1, k)
     back_terms(2, 1)
 
     def hidden_grad_1(j, _):
@@ -815,133 +1082,21 @@
     shift_in(lambda j: r.fbuf[j, cols : 2 * cols, :], r.dc, 2)
     halo_start(2, r.dc)
 
-    grads = [r.w1, r.gp, r.g1]
-
-    def pair_of(k):
-        return z_at(1 + k)
-
-    def rs_a_copy(kind, k, core):
-        return remote(
-            shard(kind, grads[kind], 2 * pair_of(k) + core),
-            r.ra[kind].at[k],
-            r.rs_as.at[kind, k],
-            r.rs_ar.at[kind, k],
-            (s, sib),
-        )
-
-    def rs_b_copy(kind, k, p):
-        return remote(
-            quarter(kind, grads[kind], 2 * pair_of(k) + c, plane[p]),
-            r.rb[kind].at[p, k],
-            r.rs_bs.at[kind, k, p],
-            r.rs_br.at[kind, k, p],
-            (plane[p], d),
-        )
-
-    def rs_c_copy(kind, k):
-        return remote(
-            r.qs[kind].at[k],
-            r.rc[kind].at[k],
-            r.rs_cs.at[kind, k],
-            r.rs_cr.at[kind, k],
-            (s, 2 * pair_of(k) + c),
-        )
-
-    def rs_d_copy(kind, p, q):
-        rows = shard_rows[kind] // 4
-        view = r.td[kind].at[pl.ds(al(q * rows, 16), rows)]
-        return remote(view, view, r.rs_ds.at[kind, p], r.rs_dr.at[kind, p], (plane[p], d))
-
-    def conv_weight(kind, xc, k):
-        tile = 2 * shard_rows[kind] // 3
-        per = 3 * width // tile
-
-        def body(i, _):
-            g = pair_of(k) * 3 + i
-            a = g // per
-            term = dot_tn(
-                xc[pl.ds(al(a * cols, 16), pixels), pl.ds(al((g % per) * tile, lanes), tile)],
-                r.dc[cols : 3 * cols, width : 2 * width],
-            )
-            grads[kind][pl.ds(al(g * tile, 16), tile), :] = term.astype(BF16)
-            return 0
-
-        lax.fori_loop(0, 3, body, 0)
-
-    def rs_a(kind, k):
-        rs_a_copy(kind, k, 1 - c).start()
-
-    def rs_b(kind, k):
-        rs_a_copy(kind, k, c).wait_recv()
-        rows = shard_rows[kind]
-        tile = rows // 4
-        start = (2 * pair_of(k) + c) * rows
-
-        def body(i, _):
-            at = pl.ds(al(start + i * tile, 16), tile)
-            grads[kind][at, :] = (
-                grads[kind][at, :].astype(F32)
-                + r.ra[kind][k, pl.ds(al(i * tile, 16), tile), :].astype(F32)
-            ).astype(BF16)
-            return 0
-
-        lax.fori_loop(0, 4, body, 0)
-        for p in range(3):
-            rs_b_copy(kind, k, p).start()
-
-    def rs_c(kind, k):
-        for p in range(3):
-            rs_b_copy(kind, k, p).wait_recv()
-        rows = shard_rows[kind] // 4
-        at = pl.ds(al((2 * pair_of(k) + c) * shard_rows[kind] + s * rows, 16), rows)
-        total = grads[kind][at, :].astype(F32)
-        for p in range(3):
-            total = total + r.rb[kind][p, k].astype(F32)
-        if k < n_z - 1:
-            r.qs[kind][k] = total.astype(BF16)
-            rs_c_copy(kind, k).start()
-        else:
-            r.qf[kind][...] = total
-
-    def rs_d(kind):
-        total = r.qf[kind][...]
-        for k in range(n_z - 1):
-            rs_c_copy(kind, k).wait_recv()
-            total = total + r.rc[kind][k].astype(F32)
-        rows = shard_rows[kind] // 4
-        r.td[kind][pl.ds(al(s * rows, 16), rows), :] = total.astype(BF16)
-        for p in range(3):
-            rs_d_copy(kind, p, s).start()
-
-    def rs_e(kind):
-        for p in range(3):
-            rs_d_copy(kind, p, plane[p]).wait_recv()
-
-    def rs_end(kind):
-        for k in range(n_z):
-            rs_a_copy(kind, k, 1 - c).wait_send()
-            for p in range(3):
-                rs_b_copy(kind, k, p).wait_send()
-            if k < n_z - 1:
-                rs_c_copy(kind, k).wait_send()
-        for p in range(3):
-            rs_d_copy(kind, p, s).wait_send()
-
-    for k in range(n_z):
-        conv_weight(2, r.xc1, k)
-        rs_a(2, k)
-        if k > 0:
-            rs_b(2, k - 1)
-    rs_b(2, n_z - 1)
-    for k in range(n_z):
-        rs_a(1, k)
-
-    halo_finish(2, r.dc)
-    conv_back(r.dc, r.w1)
-    halo_sent(2, r.dc)
     for k in range(n_z):
         rs_b(1, k)
-
+    conv_weight(2, r.xc1, 0)
+    rs_a(2, 0)
+    conv_back(r.dc, r.w1, 0, 0)
+    conv_back(r.dc, r.w1, 1, 0)
+    rs_b(2, 0)
+    conv_weight(2, r.xc1, 1)
+    rs_a(2, 1)
+    halo_finish(2, r.dc)
+    conv_back(r.dc, r.w1, 0, 1)
+    conv_back(r.dc, r.w1, 1, 1)
+    for k in range(n_z):
+        rs_r(1, k)
+    rs_b(2, 1)
     def back_0(j, _):
         lane = lane_at(j)
         norm = r.norm
@@ -957,15 +1112,17 @@
             centred = (r.h0[j, at, :] - norm[0, 0:1, lane]) * norm[0, 1:2, lane]
             first = first + jnp.sum(d_norm, 0, keepdims=True)
             second = second + jnp.sum(d_norm * centred, 0, keepdims=True)
-        r.ex_out[3, 0:1, lane] = first
-        r.ex_out[3, 1:2, lane] = second
+        ex_put(3, 0, j, first)
+        ex_put(3, 1, j, second)
         return 0
 
-    r.ex_out[3] = jnp.zeros((8, width), F32)
     lax.fori_loop(0, n_lane, back_0, 0)
     ex_start(3)
-    for k in range(n_z):
-        rs_c(2, k)
+    conv_weight(2, r.xc1, 2)
+    rs_a(2, 2)
+    conv_weight(2, r.xc1, 3)
+    rs_a(2, 3)
+    halo_sent(2, r.dc)
     back_terms(3, 0)
 
     def sums_copy(p, q):
@@ -996,20 +1153,34 @@
     shift_in(hidden_grad_0(0), r.dc, 1)
     shift_in(hidden_grad_0(1), r.dc, 2)
     halo_start(3, r.dc)
-    for k in range(n_z):
-        conv_weight(0, r.xc0, k)
-        rs_a(0, k)
-        if k > 0:
-            rs_b(0, k - 1)
-    rs_b(0, n_z - 1)
+    rs_b(2, 2)
+    rs_r(2, 0)
+    conv_weight(0, r.xc0, 0)
+    rs_a(0, 0)
+    rs_b(2, 3)
     for k in range(n_z):
         rs_c(1, k)
-    rs_d(2)
-    rs_d(1)
-
+    rs_r(2, 1)
+    conv_weight(0, r.xc0, 1)
+    rs_a(0, 1)
+    rs_c(2, 0)
+    rs_b(0, 0)
+    conv_weight(0, r.xc0, 2)
+    rs_a(0, 2)
+    conv_weight(0, r.xc0, 3)
+    rs_a(0, 3)
+    rs_r(2, 2)
+    rs_b(0, 1)
+    conv_back(r.dc, r.w0, 0, 0)
+    conv_back(r.dc, r.w0, 1, 0)
+    rs_c(2, 1)
+    rs_r(2, 3)
+    rs_b(0, 2)
     halo_finish(3, r.dc)
-    conv_back(r.dc, r.w0)
-
+    conv_back(r.dc, r.w0, 0, 1)
+    conv_back(r.dc, r.w0, 1, 1)
+    rs_b(0, 3)
+    rs_c(2, 2)
     def image_out(j, _):
         lane = lane_at(j)
         for i in range(4):
@@ -1022,41 +1193,31 @@
     lax.fori_loop(0, n_lane, image_out, 0)
     image_store = pltpu.make_async_copy(r.xin, out_image.at[0], r.store.at[1])
     image_store.start()
-
-    for k in range(n_z):
-        rs_c(0, k)
-
-    def conv_out(kind, layer, i):
+    rs_r(0, 0)
+    rs_c(2, 3)
+    rs_r(0, 1)
+    rs_c(0, 0)
+    rs_r(0, 2)
+    rs_c(0, 1)
+    rs_r(0, 3)
+    rs_d(1)
+    rs_d(2)
+    rs_c(0, 2)
+    rs_c(0, 3)
+    rs_dr(1)
+    rs_dr(2)
+    rs_d(0)
+    stores = [task_store, image_store]
+
+    def reduced_out(kind):
         rs_e(kind)
-        copies = []
-        for j in range(n_lane):
-            lane = slice(j * lanes, (j + 1) * lanes)
-            staging[layer][j, 0:conv_rows, :] = r.td[kind][:, lane].astype(F32)
-            copies.append(
-                pltpu.make_async_copy(
-                    staging[layer].at[j, 0:conv_rows],
-                    out_conv.at[layer, :, lane],
-                    r.store.at[i + j],
-                )
-            )
-            copies[-1].start()
-        return copies
-
-    conv_store_1 = conv_out(2, 1, 4)
-    rs_e(1)
-    for l in range(2):
-        for t in range(tasks):
-            at = (l * tasks + t) * e_rows
-            r.est[l, t] = r.td[1][at : at + e_rows, :].astype(F32)
-            at = at + 2 * tasks * e_rows
-            for k in range(n_sub):
-                r.sst[l, t, k * e_rows : (k + 1) * e_rows, :] = r.td[1][
-                    at : at + e_rows, k * lanes : (k + 1) * lanes
-                ].astype(F32)
-    squeeze_store = pltpu.make_async_copy(r.sst, out_squeeze, r.store.at[2])
-    expand_store = pltpu.make_async_copy(r.est, out_expand, r.store.at[3])
-    squeeze_store.start()
-    expand_store.start()
+        stores.append(
+            pltpu.make_async_copy(r.td[kind], out_reduced[kind], r.store.at[2 + kind])
+        )
+        stores[-1].start()
+
+    reduced_out(1)
+    reduced_out(2)
     for p in range(3):
         sums_copy(p, plane[p]).wait_recv()
     total = r.sums_in[0]
@@ -1065,38 +1226,101 @@
     for l in range(2):
         out_bias[l : l + 1, :] = total[2 * l : 2 * l + 1, :]
         out_gain[l : l + 1, :] = total[2 * l + 1 : 2 * l + 2, :]
-    rs_d(0)
-    conv_store_0 = conv_out(0, 0, 4 + n_lane)
-    for kind in range(3):
+    for kind in range(1, 3):
         rs_end(kind)
     for p in range(3):
         sums_copy(p, s).wait_send()
-    for k in range(4):
+    for k in range(5):
         for step in range(1, n_dp):
             ex_copy(k, step, d).wait_send()
-    halo_sent(0, r.xc0)
+    halo_sent(3, r.dc)
     halo_sent(1, r.xc1)
-    halo_sent(3, r.dc)
-    for copy in (
-        task_store,
-        image_store,
-        squeeze_store,
-        expand_store,
-        *conv_store_1,
-        *conv_store_0,
-    ):
+    rs_dr(0)
+    reduced_out(0)
+    rs_end(0)
+    for copy in stores:
+        copy.wait()
+
+
+def finish_kernel(
+    dims,
+    task,
+    image,
+    reduced_0,
+    reduced_1,
+    reduced_2,
+    gain,
+    bias,
+    out_task,
+    out_image,
+    out_conv,
+    out_squeeze,
+    out_expand,
+    out_gain,
+    out_bias,
+    task_in,
+    image_in,
+    conv_in,
+    conv_wide,
+    gate_in,
+    squeeze_wide,
+    expand_wide,
+    sem_in,
+    sem_out,
+):
+    lanes = 128
+    e_rows = dims.bottle // dims.n_dp
+    ins = [
+        pltpu.make_async_copy(reduced_0, conv_in.at[0], sem_in.at[0]),
+        pltpu.make_async_copy(reduced_2, conv_in.at[1], sem_in.at[1]),
+        pltpu.make_async_copy(reduced_1, gate_in, sem_in.at[2]),
+        pltpu.make_async_copy(task, task_in, sem_in.at[3]),
+        pltpu.make_async_copy(image, image_in, sem_in.at[4]),
+    ]
+    for copy in ins:
+        copy.start()
+    outs = [
+        pltpu.make_async_copy(task_in, out_task, sem_out.at[0]),
+        pltpu.make_async_copy(image_in, out_image, sem_out.at[1]),
+    ]
+    out_gain[...] = gain[...]
+    out_bias[...] = bias[...]
+    for layer in range(2):
+        ins[layer].wait()
+        conv_wide[layer] = conv_in[layer].astype(F32)
+        outs.append(
+            pltpu.make_async_copy(
+                conv_wide.at[layer], out_conv.at[layer], sem_out.at[2 + layer]
+            )
+        )
+        outs[-1].start()
+    for i in range(2):
+        ins[3 + i].wait()
+        outs[i].start()
+    ins[2].wait()
+    for l in range(2):
+        for t in range(dims.tasks):
+            at = (l * dims.tasks + t) * e_rows
+            expand_wide[l, t] = gate_in[at : at + e_rows, :].astype(F32)
+            at = at + 2 * dims.tasks * e_rows
+            for k in range(dims.width // dims.n_dp // e_rows):
+                squeeze_wide[l, t, k * e_rows : (k + 1) * e_rows, :] = gate_in[
+                    at : at + e_rows, k * lanes : (k + 1) * lanes
+                ].astype(F32)
+    outs.append(pltpu.make_async_copy(squeeze_wide, out_squeeze, sem_out.at[4]))
+    outs.append(pltpu.make_async_copy(expand_wide, out_expand, sem_out.at[5]))
+    outs[-2].start()
+    outs[-1].start()
+    for copy in outs:
         copy.wait()
 
 
 def fused(images, counts, pool_index, conv_w, squeeze_w, expand_w, gain, bias, cotangent):
     n_dp = lax.axis_size("dp")
-    here = lax.axis_index("section")
     micro, pixels, width = images.shape
     tasks, bottle = squeeze_w.shape[1], squeeze_w.shape[3]
     cols = 2 * pool_index.shape[2]
     windows = cols // 2
-    own_pick = lax.dynamic_index_in_dim(pool_index, here, 0, keepdims=False)
-    pick = jnp.broadcast_to(own_pick.reshape(windows, 1), (windows, 128))
     conv_rows = conv_w.shape[1]
     gate_rows = 4 * tasks * expand_w.shape[2]
     shard_rows = (conv_rows, gate_rows, conv_rows)
@@ -1105,7 +1329,7 @@
     dma = pltpu.SemaphoreType.DMA
     scratch = dict(
         load=dma((5 + 2 * (width // 128),)),
-        store=dma((4 + 2 * (width // 128),)),
+        store=dma((5,)),
         sst=vm(squeeze_w.shape, F32),
         est=vm(expand_w.shape, F32),
         xin=vm((pixels, width), BF16),
@@ -1116,20 +1340,24 @@
         g1=vm((n_dp * conv_rows, width), BF16),
         sq_w=vm((2, width, tasks * bottle), BF16),
         ex_w=vm((2, tasks, bottle, width), BF16),
-        ag_zs=dma((3, n_z - 1)),
-        ag_zr=dma((3, n_z - 1)),
-        ag_ps=dma((3, 3 * (n_z - 1))),
-        ag_pr=dma((3, 3 * (n_z - 1))),
-        ag_ss=dma((3, n_z)),
-        ag_sr=dma((3, n_z)),
+        ag_zs=dma((3, 2 * (n_z - 1))),
+        ag_zr=dma((3, 2 * (n_z - 1))),
+        ag_ps=dma((3, 8 * (n_z - 1))),
+        ag_pr=dma((3, 8 * (n_z - 1))),
+        ag_ss=dma((3, 8 * (n_z - 1))),
+        ag_sr=dma((3, 8 * (n_z - 1))),
+        ag_os=dma((3,)),
+        ag_or=dma((3,)),
         mp=vm((windows, 128), F32),
-        halo=vm((4, 2, cols, width), BF16),
+        pick=vm((windows, 128), jnp.int32),
+        halo=vm((2, 2, cols, width), BF16),
         halo_s=dma((4, 2)),
         halo_r=dma((4, 2)),
-        ex_out=vm((4, 8, width), F32),
-        ex_in=vm((4, n_dp, 8, width), F32),
-        ex_s=dma((4, n_dp - 1)),
-        ex_r=dma((4, n_dp - 1)),
+        ex_out=vm((5, 8, 128), F32),
+        ex_in=vm((5, n_dp, 8, 128), F32),
+        total=vm((8, width), F32),
+        ex_s=dma((5, n_dp - 1)),
+        ex_r=dma((5, n_dp - 1)),
         norm=vm((2, 8, width), F32),
         xc0=vm((4 * cols, 3 * width), BF16),
         xc1=vm((4 * cols, 3 * width), BF16),
@@ -1149,25 +1377,23 @@
         centred1=vm((windows, width), F32),
         df2=vm((windows, width), F32),
         df1=vm((windows, width), F32),
-        gs_st=vm((width, bottle), F32),
-        ge_st=vm((bottle, width), F32),
         sums=vm((8, width), F32),
         sums_in=vm((4, 8, width), F32),
         sums_s=dma((3,)),
         sums_r=dma((3,)),
         rs_as=dma((3, n_z)),
         rs_ar=dma((3, n_z)),
-        rs_bs=dma((3, n_z, 3)),
-        rs_br=dma((3, n_z, 3)),
+        rs_bs=dma((3, n_z, 6)),
+        rs_br=dma((3, n_z, 6)),
         rs_cs=dma((3, n_z - 1)),
         rs_cr=dma((3, n_z - 1)),
-        rs_ds=dma((3, 3)),
-        rs_dr=dma((3, 3)),
+        rs_ds=dma((3, 4)),
+        rs_dr=dma((3, 4)),
     )
     quarters = [rows // 4 for rows in shard_rows]
     scratch.update(
         ra=[vm((n_z, rows, width), BF16) for rows in shard_rows],
-        rb=[vm((3, n_z, rows, width), BF16) for rows in quarters],
+        rb=[vm((n_z, 6, rows, width // 2), BF16) for rows in quarters],
         qs=[vm((n_z - 1, rows, width), BF16) for rows in quarters],
         qf=[vm((rows, width), F32) for rows in quarters],
         rc=[vm((n_z - 1, rows, width), BF16) for rows in quarters],
@@ -1187,8 +1413,24 @@
     any_spec = pl.BlockSpec(memory_space=pl.ANY)
     vmem_spec = pl.BlockSpec(memory_space=pltpu.VMEM)
     smem_spec = pl.BlockSpec(memory_space=pltpu.SMEM)
+    results = pl.pallas_call(
+        functools.partial(step_kernel, dims),
+        out_shape=(
+            jax.ShapeDtypeStruct((1, tasks, windows, width), BF16),
+            jax.ShapeDtypeStruct((1, pixels, width), BF16),
+            *[jax.ShapeDtypeStruct((rows, width), BF16) for rows in shard_rows],
+            jax.ShapeDtypeStruct(gain.shape, F32),
+            jax.ShapeDtypeStruct(bias.shape, F32),
+        ),
+        in_specs=[smem_spec, vmem_spec, vmem_spec, vmem_spec] + [any_spec] * 5,
+        out_specs=(any_spec,) * 5 + (vmem_spec,) * 2,
+        scratch_shapes=tuple(buffers),
+        compiler_params=pltpu.CompilerParams(
+            collective_id=0, has_side_effects=True, vmem_limit_bytes=VMEM_BYTES
+        ),
+    )(counts.reshape(micro), pool_index, gain, bias, images, conv_w, squeeze_w, expand_w, cotangent)
     return pl.pallas_call(
-        functools.partial(step_kernel, dims),
+        functools.partial(finish_kernel, dims),
         out_shape=(
             jax.ShapeDtypeStruct((1, tasks, windows, width), BF16),
             jax.ShapeDtypeStruct((1, pixels, width), BF16),
@@ -1198,13 +1440,21 @@
             jax.ShapeDtypeStruct(gain.shape, F32),
             jax.ShapeDtypeStruct(bias.shape, F32),
         ),
-        in_specs=[smem_spec, vmem_spec, vmem_spec, vmem_spec] + [any_spec] * 5,
+        in_specs=[any_spec] * 5 + [vmem_spec] * 2,
         out_specs=(any_spec,) * 5 + (vmem_spec,) * 2,
-        scratch_shapes=tuple(buffers),
-        compiler_params=pltpu.CompilerParams(
-            collective_id=0, has_side_effects=True, vmem_limit_bytes=VMEM_BYTES
+        scratch_shapes=(
+            vm((1, tasks, windows, width), BF16),
+            vm((1, pixels, width), BF16),
+            vm(conv_w.shape, BF16),
+            vm(conv_w.shape, F32),
+            vm((gate_rows, width), BF16),
+            vm(squeeze_w.shape, F32),
+            vm(expand_w.shape, F32),
+            dma((5,)),
+            dma((6,)),
         ),
-    )(counts, pick, gain, bias, images, conv_w, squeeze_w, expand_w, cotangent)
+        compiler_params=pltpu.CompilerParams(vmem_limit_bytes=VMEM_BYTES),
+    )(*results)
 
 
 def fits_kernel(mesh, args):

time: 182 us -> 147 us (0.81)
  Pallas kernels: 171 us -> 145 us
  local copies, waits for them, and re-layouts: 10.8 us -> 0 us
    pallas_call x1, Pallas kernels: 171 us -> 141 us  [fused(): pl.pallas_call(functools.partial(step_kernel, dims), out_shape=(jax.Shape...]
    unnamed x20 -> x0, local copies, waits for them, and re-layouts: 10.1 us -> none
    pallas_call x0 -> x1, Pallas kernels: none -> 4.49 us  [fused(): pl.pallas_call(functools.partial(finish_kernel, dims), out_shape=(jax.Sha...]
where the time goes in v3:
time: 147 us; the launch traced here: 146 us
  Pallas kernels  145 us (99%)
    pallas_call x1, Pallas kernels, fused(): pl.pallas_call(functools.partial(step_kernel, dims), out_shape=(jax.Shape...  141 us
    pallas_call x1, Pallas kernels, fused(): pl.pallas_call(functools.partial(finish_kernel, dims), out_shape=(jax.Sha...  4.49 us

profile of v3, /device:TPU:0, one launch (start us, length us, event | category | flops | bytes accessed | tf_op | source)
XLA Modules:
  0.0 146.2 jit_solution(9086533950457817186)
XLA Ops:
  0.6 140.9 %shard_map.144 = (bf16[1,3,192,512]{3,2,1,0:T(8,128)(2,1)}, bf16[1,768,512]{2,1,0:T(8,128)(2,1)}, bf16[576,512]{1,0:T(8,128)(2,1)}, bf16[192,512]{1,0:T(8,128)(2...) custom-call(s32[4]{0:T(128)} %bitcast.1, s32[4,1,192]{2,1,0:T(1,128)} %picks.1, f32[2,512]{1,0:T(2,128)} %gain.1, ...), custom_call_target="tpu_custom_call" | custom-call | tf_op jit(solution)/shard_map/pallas_call | solution.py:1416
  141.5 4.5 %shard_map.145 = (bf16[1,3,192,512]{3,2,1,0:T(8,128)(2,1)}, bf16[1,768,512]{2,1,0:T(8,128)(2,1)}, f32[2,576,512]{2,1,0:T(8,128)}, f32[2,3,64,128]{3,2,1,0:T(8,12...) custom-call(bf16[1,3,192,512]{3,2,1,0:T(8,128)(2,1)} %get-tuple-element.14.task, ...), custom_call_target="tpu_custom_call" | custom-call | tf_op jit(solution)/shard_map/pallas_call | solution.py:1432

commit v4 on v3

--- a/solution.py
+++ b/solution.py
@@ -352,25 +352,33 @@
         rows = shard_rows[kind]
         return buf.at[pl.ds(al(which * rows + q * (rows // 4), 16), rows // 4)]
 
-
     def z_of(way, hop):
         return z_at(n_z - hop if way == 0 else hop)
 
     def has(way, hop):
         return z >= hop if way == 0 else z < n_z - hop
 
-    def hop_id(way, hop):
-        return (hop - 1) * 2 + way
+    def slot_of(way, hop):
+        return n_z - 1 - hop if way == 0 else hop - 1
 
     def ag_z_copy(kind, way, hop, owner):
         view = quarter(kind, full[kind], 2 * owner + c, s)
-        i = hop_id(way, hop)
         return remote(
             view,
             view,
-            r.ag_zs.at[kind, i],
-            r.ag_zr.at[kind, i],
+            r.ag_zs.at[kind, (hop - 1) * 2 + way],
+            r.ag_zr.at[kind, slot_of(way, hop)],
             (s, 2 * z_at(1 if way == 0 else n_z - 1) + c),
+        )
+
+    def gate_z_copy(step, owner):
+        view = quarter(1, full[1], 2 * owner + c, s)
+        return remote(
+            view,
+            view,
+            r.ag_zs.at[1, step - 1],
+            r.ag_zr.at[1, step - 1],
+            (s, 2 * z_at(step) + c),
         )
 
     def ag_pass(kind, way, hop, do):
@@ -384,97 +392,102 @@
 
     halves = [slice(0, width // 2), slice(width // 2, width)]
 
-    def ag_p_copy(kind, way, hop, leg, q):
-        view = quarter(kind, full[kind], 2 * z_of(way, hop) + c, q)
+    def ag_p_copy(kind, slot, owner, leg, q):
+        view = quarter(kind, full[kind], 2 * owner + c, q)
         if leg >= 2:
             view = view.at[:, halves[leg - 2]]
         to = plane[(0, 1, 1, 0)[leg]]
-        i = hop_id(way, hop) * 4 + leg
+        i = slot * 4 + leg
         return remote(view, view, r.ag_ps.at[kind, i], r.ag_pr.at[kind, i], (to, d))
 
     def ag_own_copy(kind, core):
         view = shard(kind, full[kind], 2 * z + core)
         return remote(view, view, r.ag_os.at[kind], r.ag_or.at[kind], (s, sib))
 
-    def ag_s_copy(kind, way, hop, q, i, core):
-        view = quarter(kind, full[kind], 2 * z_of(way, hop) + core, q)
-        i = hop_id(way, hop) * 4 + i
+    def ag_s_copy(kind, slot, owner, i, core):
+        view = quarter(kind, full[kind], 2 * owner + core, others[i])
+        i = slot * 4 + i
         return remote(view, view, r.ag_ss.at[kind, i], r.ag_sr.at[kind, i], (s, sib))
 
     others = [s] + plane
 
     def ag_start(kind):
-        for way in range(2):
-            ag_pass(kind, way, 1, lambda copy: copy.start())
+        if kind == 1:
+            for step in range(1, n_z):
+                gate_z_copy(step, z).start()
+        else:
+            for way in range(2):
+                ag_pass(kind, way, 1, lambda copy: copy.start())
         ag_own_copy(kind, c).start()
 
-    def for_hop(hop, do):
+    def for_hop(kind, hop, do):
+        if kind == 1:
+            do(hop - 1, z_at(n_z - hop), None)
+            return
         for way in range(2):
 
             @pl.when(has(way, hop))
             def _():
-                do(way)
+                do(slot_of(way, hop), z_of(way, hop), way)
 
     def ag_z(kind, hop):
-        def do(way):
-            ag_z_copy(kind, way, hop, z_of(way, hop)).wait_recv()
-            if hop < n_z - 1:
-                ag_pass(kind, way, hop + 1, lambda copy: copy.start())
-            if kind != 1:
-                for leg in range(2):
-                    ag_p_copy(kind, way, hop, leg, s).start()
-            ag_s_copy(kind, way, hop, s, 0, c).start()
-
-        for_hop(hop, do)
-
-    def ag_l(kind, hop):
-        def do(way):
+        def do(slot, owner, way):
+            if kind == 1:
+                gate_z_copy(hop, owner).wait_recv()
+            else:
+                ag_z_copy(kind, way, hop, owner).wait_recv()
+                if hop < n_z - 1:
+                    ag_pass(kind, way, hop + 1, lambda copy: copy.start())
             for leg in range(2):
-                ag_p_copy(kind, way, hop, leg, s).start()
-
-        for_hop(hop, do)
+                ag_p_copy(kind, slot, owner, leg, s).start()
+            ag_s_copy(kind, slot, owner, 0, c).start()
+
+        for_hop(kind, hop, do)
 
     def ag_r(kind, hop):
-        def do(way):
+        def do(slot, owner, way):
             for leg in range(2):
-                ag_p_copy(kind, way, hop, leg, plane[leg]).wait_recv()
-                ag_p_copy(kind, way, hop, 2 + leg, plane[leg]).start()
-                ag_s_copy(kind, way, hop, plane[leg], 1 + leg, c).start()
-
-        for_hop(hop, do)
+                ag_p_copy(kind, slot, owner, leg, plane[leg]).wait_recv()
+                ag_p_copy(kind, slot, owner, 2 + leg, plane[leg]).start()
+                ag_s_copy(kind, slot, owner, 1 + leg, c).start()
+
+        for_hop(kind, hop, do)
 
     def ag_p(kind, hop):
-        def do(way):
+        def do(slot, owner, way):
             for leg in range(2):
-                ag_p_copy(kind, way, hop, 2 + leg, plane[2]).wait_recv()
-            ag_s_copy(kind, way, hop, plane[2], 3, c).start()
-
-        for_hop(hop, do)
+                ag_p_copy(kind, slot, owner, 2 + leg, plane[2]).wait_recv()
+            ag_s_copy(kind, slot, owner, 3, c).start()
+
+        for_hop(kind, hop, do)
 
     def ag_sib(kind):
         ag_own_copy(kind, 1 - c).wait_recv()
         for hop in range(1, n_z):
 
-            def do(way):
+            def do(slot, owner, way):
                 for i in range(4):
-                    ag_s_copy(kind, way, hop, others[i], i, 1 - c).wait_recv()
-
-            for_hop(hop, do)
+                    ag_s_copy(kind, slot, owner, i, 1 - c).wait_recv()
+
+            for_hop(kind, hop, do)
 
     def ag_end(kind):
         ag_own_copy(kind, c).wait_send()
         for hop in range(1, n_z):
 
-            def do(way):
+            def do(slot, owner, way):
                 for leg in range(2):
-                    ag_p_copy(kind, way, hop, leg, s).wait_send()
-                    ag_p_copy(kind, way, hop, 2 + leg, plane[leg]).wait_send()
+                    ag_p_copy(kind, slot, owner, leg, s).wait_send()
+                    ag_p_copy(kind, slot, owner, 2 + leg, plane[leg]).wait_send()
                 for i in range(4):
-                    ag_s_copy(kind, way, hop, others[i], i, c).wait_send()
-
-            for way in range(2):
-                ag_pass(kind, way, hop, lambda copy: copy.wait_send())
-            for_hop(hop, do)
+                    ag_s_copy(kind, slot, owner, i, c).wait_send()
+
+            if kind == 1:
+                gate_z_copy(hop, z).wait_send()
+            else:
+                for way in range(2):
+                    ag_pass(kind, way, hop, lambda copy: copy.wait_send())
+            for_hop(kind, hop, do)
 
     def cast_conv(layer, buf):
         for j in range(n_lane):
@@ -591,15 +604,22 @@
             halo_up(e, buf).wait_send()
 
     def ex_copy(k, step, owner):
+        turn = (k + 1) % 5 % 2
         return remote(
             r.ex_out.at[k],
             r.ex_in.at[k, owner],
-            r.ex_s.at[k, step - 1],
-            r.ex_r.at[k, step - 1],
+            r.ex_s.at[turn, step - 1],
+            r.ex_r.at[turn, step - 1],
             (s, rem(d + step, n_dp)),
         )
 
+    def ex_sent(k):
+        for step in range(1, n_dp):
+            ex_copy(k, step, d).wait_send()
+
     def ex_start(k):
+        if k in (1, 2, 3):
+            ex_sent((4, 0, 1)[k - 1])
         for step in range(1, n_dp):
             ex_copy(k, step, d).start()
         r.ex_in[k, d] = r.ex_out[k]
@@ -618,16 +638,22 @@
     def ex_put(k, i, j, value):
         r.ex_out[k, pl.ds(i * n_lane + j, 1), :] = value
 
-    def conv_forward(xc, w, h, row):
+    def conv_forward(xc, w, h, row, part):
         span = 3 * width
         acc = None
         for a in range(3):
-            term = dot(
-                xc[(a + row) * cols : (a + row + 1) * cols, :], w[a * span : (a + 1) * span, :]
-            )
+            block = a + row
+            if (block in (0, 3)) != (part == 1):
+                continue
+            term = dot(xc[block * cols : (block + 1) * cols, :], w[a * span : (a + 1) * span, :])
             acc = term if acc is None else acc + term
+        add_to(h, row, part, acc)
+
+    def add_to(out, row, part, acc):
         for j in range(n_lane):
-            h[j, row * cols : (row + 1) * cols, :] = acc[:, j * lanes : (j + 1) * lanes]
+            at = (j, slice(row * cols, (row + 1) * cols), slice(None))
+            piece = acc[:, j * lanes : (j + 1) * lanes]
+            out[at] = piece if part == 0 else out[at] + piece
 
     def conv_back(dc, w, row, part):
         acc = None
@@ -641,10 +667,7 @@
                     w[(3 * a + b) * width : (3 * a + b + 1) * width, :],
                 )
                 acc = term if acc is None else acc + term
-        for j in range(n_lane):
-            at = (j, slice(row * cols, (row + 1) * cols), slice(None))
-            piece = acc[:, j * lanes : (j + 1) * lanes]
-            r.fbuf[at] = piece if part == 0 else r.fbuf[at] + piece
+        add_to(r.fbuf, row, part, acc)
 
     quarter_rows = pixels // 4
 
@@ -711,27 +734,32 @@
     cast_conv(1, r.w1)
     ag_z(0, 1)
     ag_z(0, 2)
-    halo_start(0, r.xc0)
     ag_r(0, 1)
     ag_z(0, 3)
     ag_start(2)
     ag_r(0, 2)
     ag_p(0, 1)
     ag_r(0, 3)
+    ag_z(2, 1)
+    halo_start(0, r.xc0)
+    r.total[...] = jnp.concatenate([ex_finish(4)[0]] * 8, axis=0)
     ag_p(0, 2)
+    ag_p(0, 3)
+    ag_sib(0)
+    ag_z(2, 2)
+    conv_forward(r.xc0, r.w0, r.h0, 0, 0)
+    conv_forward(r.xc0, r.w0, r.h0, 1, 0)
+    ag_r(2, 1)
     halo_finish(0, r.xc0)
-    ag_z(2, 1)
-    ag_start(1)
-    ag_p(0, 3)
-    r.total[...] = jnp.concatenate([ex_finish(4)[0]] * 8, axis=0)
-    ag_sib(0)
-    conv_forward(r.xc0, r.w0, r.h0, 0)
-    conv_forward(r.xc0, r.w0, r.h0, 1)
+    conv_forward(r.xc0, r.w0, r.h0, 0, 1)
+    conv_forward(r.xc0, r.w0, r.h0, 1, 1)
     stats(r.h0, 0)
     ex_start(0)
     halo_sent(0, r.xc0)
-    ag_z(2, 2)
-    ag_r(2, 1)
+    ag_z(2, 3)
+    ag_start(1)
+    ag_r(2, 2)
+    ag_p(2, 1)
     norm_of(ex_finish(0), 0)
 
     def block_0(j, _):
@@ -754,21 +782,19 @@
     shift_in(lambda j: r.fbuf[j, 0:cols, :], r.xc1, 1)
     shift_in(lambda j: r.fbuf[j, cols : 2 * cols, :], r.xc1, 2)
     halo_start(1, r.xc1)
-    ag_z(2, 3)
-    ag_r(2, 2)
-    ag_p(2, 1)
     ag_r(2, 3)
     ag_p(2, 2)
-    for hop in range(1, n_z):
-        ag_z(1, hop)
-        ag_l(1, hop)
-    halo_finish(1, r.xc1)
+    for step in range(1, n_z):
+        ag_z(1, step)
     ag_p(2, 3)
     ag_sib(2)
-    conv_forward(r.xc1, r.w1, r.h1, 0)
-    for hop in range(1, n_z):
-        ag_r(1, hop)
-    conv_forward(r.xc1, r.w1, r.h1, 1)
+    conv_forward(r.xc1, r.w1, r.h1, 0, 0)
+    for step in range(1, n_z):
+        ag_r(1, step)
+    conv_forward(r.xc1, r.w1, r.h1, 1, 0)
+    halo_finish(1, r.xc1)
+    conv_forward(r.xc1, r.w1, r.h1, 0, 1)
+    conv_forward(r.xc1, r.w1, r.h1, 1, 1)
     stats(r.h1, 1)
     ex_start(1)
     for hop in range(1, n_z):
@@ -809,6 +835,8 @@
 
     for kind in range(3):
         ag_end(kind)
+    for p in plane:
+        pl.semaphore_signal(r.ready, inc=1, device_id=(p, d), device_id_type=MESH)
 
     def block_1(j, _):
         lane = lane_at(j)
@@ -823,7 +851,7 @@
     grads = [r.w1, r.gp, r.g1]
 
     def pair_of(k):
-        return z_at(1 + k)
+        return z_at((2, 1, 3, 0)[k])
 
     def rs_a_copy(kind, k, core):
         return remote(
@@ -833,6 +861,10 @@
             r.rs_ar.at[kind, k],
             (s, sib),
         )
+
+    def again(first, second, i):
+        per = 4 * (n_z - 1)
+        return (first if i < 3 * per else second).at[i // per % 3, i % per]
 
     def rs_b_copy(kind, k, way):
         o = 2 * pair_of(k) + c
@@ -842,8 +874,8 @@
         return remote(
             quarter(kind, grads[kind], o, q).at[:, halves[half]],
             r.rb[kind].at[k, way],
-            r.rs_bs.at[kind, k, way],
-            r.rs_br.at[kind, k, way],
+            again(r.ag_ps, r.ag_ss, (kind * n_z + k) * 6 + way),
+            again(r.ag_pr, r.ag_sr, (kind * n_z + k) * 6 + way),
             (to, d),
         )
 
@@ -858,10 +890,9 @@
 
     def rs_d_copy(kind, leg, q):
         rows = shard_rows[kind] // 4
-        view = r.td[kind].at[pl.ds(al(q * rows, 16), rows)]
-        if leg >= 2:
-            view = view.at[:, halves[leg - 2]]
-        to = plane[(0, 1, 1, 0)[leg]]
+        half = (0, 1, 1, 0, 0, 1)[leg]
+        to = plane[(0, 1, 0, 1, 1, 0)[leg]]
+        view = r.td[kind].at[pl.ds(al(q * rows, 16), rows), halves[half]]
         return remote(view, view, r.rs_ds.at[kind, leg], r.rs_dr.at[kind, leg], (to, d))
 
     def conv_weight(kind, xc, k):
@@ -937,17 +968,18 @@
             total = total + r.rc[kind][k].astype(F32)
         rows = shard_rows[kind] // 4
         r.td[kind][pl.ds(al(s * rows, 16), rows), :] = total.astype(BF16)
-        for leg in range(2):
+        for leg in range(4):
             rs_d_copy(kind, leg, s).start()
 
     def rs_dr(kind):
         for leg in range(2):
             rs_d_copy(kind, leg, plane[leg]).wait_recv()
-            rs_d_copy(kind, 2 + leg, plane[leg]).start()
+            rs_d_copy(kind, 4 + leg, plane[leg]).start()
 
     def rs_e(kind):
         for leg in range(2):
-            rs_d_copy(kind, 2 + leg, plane[2]).wait_recv()
+            rs_d_copy(kind, 2 + leg, plane[leg]).wait_recv()
+            rs_d_copy(kind, 4 + leg, plane[2]).wait_recv()
 
     def rs_end(kind):
         for k in range(n_z):
@@ -956,9 +988,10 @@
                 rs_b_copy(kind, k, way).wait_send()
             if k < n_z - 1:
                 rs_c_copy(kind, k).wait_send()
+        for leg in range(4):
+            rs_d_copy(kind, leg, s).wait_send()
         for leg in range(2):
-            rs_d_copy(kind, leg, s).wait_send()
-            rs_d_copy(kind, 2 + leg, plane[leg]).wait_send()
+            rs_d_copy(kind, 4 + leg, plane[leg]).wait_send()
 
     loads[3].wait()
     r.df2[...] = jnp.zeros_like(r.df2)
@@ -1082,21 +1115,21 @@
     shift_in(lambda j: r.fbuf[j, cols : 2 * cols, :], r.dc, 2)
     halo_start(2, r.dc)
 
+    pl.semaphore_wait(r.ready, 3)
     for k in range(n_z):
         rs_b(1, k)
-    conv_weight(2, r.xc1, 0)
-    rs_a(2, 0)
+    for k in range(2):
+        conv_weight(2, r.xc1, k)
+        rs_a(2, k)
     conv_back(r.dc, r.w1, 0, 0)
+    rs_b(2, 0)
     conv_back(r.dc, r.w1, 1, 0)
-    rs_b(2, 0)
-    conv_weight(2, r.xc1, 1)
-    rs_a(2, 1)
+    for k in range(n_z):
+        rs_r(1, k)
+    rs_b(2, 1)
     halo_finish(2, r.dc)
     conv_back(r.dc, r.w1, 0, 1)
     conv_back(r.dc, r.w1, 1, 1)
-    for k in range(n_z):
-        rs_r(1, k)
-    rs_b(2, 1)
     def back_0(j, _):
         lane = lane_at(j)
         norm = r.norm
@@ -1120,8 +1153,10 @@
     ex_start(3)
     conv_weight(2, r.xc1, 2)
     rs_a(2, 2)
+    rs_r(2, 0)
     conv_weight(2, r.xc1, 3)
     rs_a(2, 3)
+    rs_b(2, 2)
     halo_sent(2, r.dc)
     back_terms(3, 0)
 
@@ -1153,34 +1188,30 @@
     shift_in(hidden_grad_0(0), r.dc, 1)
     shift_in(hidden_grad_0(1), r.dc, 2)
     halo_start(3, r.dc)
-    rs_b(2, 2)
-    rs_r(2, 0)
     conv_weight(0, r.xc0, 0)
     rs_a(0, 0)
+    rs_r(2, 1)
     rs_b(2, 3)
     for k in range(n_z):
         rs_c(1, k)
-    rs_r(2, 1)
     conv_weight(0, r.xc0, 1)
     rs_a(0, 1)
     rs_c(2, 0)
-    rs_b(0, 0)
     conv_weight(0, r.xc0, 2)
     rs_a(0, 2)
+    rs_r(2, 2)
+    rs_b(0, 0)
     conv_weight(0, r.xc0, 3)
     rs_a(0, 3)
-    rs_r(2, 2)
+    rs_c(2, 1)
+    conv_back(r.dc, r.w0, 0, 0)
+    rs_r(2, 3)
     rs_b(0, 1)
-    conv_back(r.dc, r.w0, 0, 0)
     conv_back(r.dc, r.w0, 1, 0)
-    rs_c(2, 1)
-    rs_r(2, 3)
-    rs_b(0, 2)
+    rs_c(2, 2)
     halo_finish(3, r.dc)
     conv_back(r.dc, r.w0, 0, 1)
     conv_back(r.dc, r.w0, 1, 1)
-    rs_b(0, 3)
-    rs_c(2, 2)
     def image_out(j, _):
         lane = lane_at(j)
         for i in range(4):
@@ -1194,30 +1225,21 @@
     image_store = pltpu.make_async_copy(r.xin, out_image.at[0], r.store.at[1])
     image_store.start()
     rs_r(0, 0)
+    rs_b(0, 2)
     rs_c(2, 3)
     rs_r(0, 1)
     rs_c(0, 0)
+    rs_b(0, 3)
     rs_r(0, 2)
     rs_c(0, 1)
     rs_r(0, 3)
+    rs_c(0, 2)
     rs_d(1)
     rs_d(2)
-    rs_c(0, 2)
     rs_c(0, 3)
     rs_dr(1)
     rs_dr(2)
     rs_d(0)
-    stores = [task_store, image_store]
-
-    def reduced_out(kind):
-        rs_e(kind)
-        stores.append(
-            pltpu.make_async_copy(r.td[kind], out_reduced[kind], r.store.at[2 + kind])
-        )
-        stores[-1].start()
-
-    reduced_out(1)
-    reduced_out(2)
     for p in range(3):
         sums_copy(p, plane[p]).wait_recv()
     total = r.sums_in[0]
@@ -1226,16 +1248,26 @@
     for l in range(2):
         out_bias[l : l + 1, :] = total[2 * l : 2 * l + 1, :]
         out_gain[l : l + 1, :] = total[2 * l + 1 : 2 * l + 2, :]
-    for kind in range(1, 3):
-        rs_end(kind)
     for p in range(3):
         sums_copy(p, s).wait_send()
-    for k in range(5):
-        for step in range(1, n_dp):
-            ex_copy(k, step, d).wait_send()
+    ex_sent(2)
+    ex_sent(3)
     halo_sent(3, r.dc)
     halo_sent(1, r.xc1)
     rs_dr(0)
+    stores = [task_store, image_store]
+
+    def reduced_out(kind):
+        rs_e(kind)
+        stores.append(
+            pltpu.make_async_copy(r.td[kind], out_reduced[kind], r.store.at[2 + kind])
+        )
+        stores[-1].start()
+
+    reduced_out(1)
+    reduced_out(2)
+    for kind in range(1, 3):
+        rs_end(kind)
     reduced_out(0)
     rs_end(0)
     for copy in stores:
@@ -1341,11 +1373,11 @@
         sq_w=vm((2, width, tasks * bottle), BF16),
         ex_w=vm((2, tasks, bottle, width), BF16),
         ag_zs=dma((3, 2 * (n_z - 1))),
-        ag_zr=dma((3, 2 * (n_z - 1))),
-        ag_ps=dma((3, 8 * (n_z - 1))),
-        ag_pr=dma((3, 8 * (n_z - 1))),
-        ag_ss=dma((3, 8 * (n_z - 1))),
-        ag_sr=dma((3, 8 * (n_z - 1))),
+        ag_zr=dma((3, n_z - 1)),
+        ag_ps=dma((3, 4 * (n_z - 1))),
+        ag_pr=dma((3, 4 * (n_z - 1))),
+        ag_ss=dma((3, 4 * (n_z - 1))),
+        ag_sr=dma((3, 4 * (n_z - 1))),
         ag_os=dma((3,)),
         ag_or=dma((3,)),
         mp=vm((windows, 128), F32),
@@ -1356,8 +1388,8 @@
         ex_out=vm((5, 8, 128), F32),
         ex_in=vm((5, n_dp, 8, 128), F32),
         total=vm((8, width), F32),
-        ex_s=dma((5, n_dp - 1)),
-        ex_r=dma((5, n_dp - 1)),
+        ex_s=dma((2, n_dp - 1)),
+        ex_r=dma((2, n_dp - 1)),
         norm=vm((2, 8, width), F32),
         xc0=vm((4 * cols, 3 * width), BF16),
         xc1=vm((4 * cols, 3 * width), BF16),
@@ -1383,12 +1415,11 @@
         sums_r=dma((3,)),
         rs_as=dma((3, n_z)),
         rs_ar=dma((3, n_z)),
-        rs_bs=dma((3, n_z, 6)),
-        rs_br=dma((3, n_z, 6)),
+        ready=pltpu.SemaphoreType.REGULAR,
         rs_cs=dma((3, n_z - 1)),
         rs_cr=dma((3, n_z - 1)),
-        rs_ds=dma((3, 4)),
-        rs_dr=dma((3, 4)),
+        rs_ds=dma((3, 6)),
+        rs_dr=dma((3, 6)),
     )
     quarters = [rows // 4 for rows in shard_rows]
     scratch.update(

time: 147 us -> 137 us (0.932)
  Pallas kernels: 145 us -> 136 us
    pallas_call x1, Pallas kernels: 141 us -> 131 us  [fused(): pl.pallas_call(functools.partial(step_kernel, dims), out_shape=(jax.Shape...]
where the time goes in v4:
time: 137 us
  Pallas kernels  136 us (99%)
    pallas_call x1, Pallas kernels, fused(): pl.pallas_call(functools.partial(step_kernel, dims), out_shape=(jax.Shape...  131 us
    pallas_call x1, Pallas kernels, fused(): pl.pallas_call(functools.partial(finish_kernel, dims), out_shape=(jax.Sha...  4.49 us

profile of v4, /device:TPU:0, one launch (start us, length us, event | category | flops | bytes accessed | tf_op | source)
XLA Modules:
  0.0 136.7 jit_solution(8555044608291315429)
XLA Ops:
  0.6 131.4 %shard_map.144 = (bf16[1,3,192,512]{3,2,1,0:T(8,128)(2,1)}, bf16[1,768,512]{2,1,0:T(8,128)(2,1)}, bf16[576,512]{1,0:T(8,128)(2,1)}, bf16[192,512]{1,0:T(8,128)(2...) custom-call(s32[4]{0:T(128)} %bitcast.1, s32[4,1,192]{2,1,0:T(1,128)} %picks.1, f32[2,512]{1,0:T(2,128)} %gain.1, ...), custom_call_target="tpu_custom_call" | custom-call | tf_op jit(solution)/shard_map/pallas_call | solution.py:1447
  132.1 4.5 %shard_map.145 = (bf16[1,3,192,512]{3,2,1,0:T(8,128)(2,1)}, bf16[1,768,512]{2,1,0:T(8,128)(2,1)}, f32[2,576,512]{2,1,0:T(8,128)}, f32[2,3,64,128]{3,2,1,0:T(8,12...) custom-call(bf16[1,3,192,512]{3,2,1,0:T(8,128)(2,1)} %get-tuple-element.14.task, ...), custom_call_target="tpu_custom_call" | custom-call | tf_op jit(solution)/shard_map/pallas_call | solution.py:1463

commit v5 on v4

--- a/solution.py
+++ b/solution.py
@@ -11,7 +11,7 @@
 EPS = 1e-05
 BF16 = jnp.bfloat16
 F32 = jnp.float32
-VMEM_BYTES = 62 * 1024 * 1024
+VMEM_BYTES = 58 * 1024 * 1024
 
 
 def gelu_back(point, upstream):
@@ -227,12 +227,18 @@
 MESH = pl.DeviceIdType.MESH
 
 
+def gelu_tanh(x):
+    return jnp.tanh(GELU_C * x * (1.0 + GELU_K * (x * x)))
+
+
+def gelu_slope(x, t):
+    inner = GELU_C * (1.0 + 3.0 * GELU_K * (x * x))
+    return 0.5 * (1.0 + t) + 0.5 * x * (1.0 - t * t) * inner
+
+
 def gelu_pair(x):
-    square = x * x
-    t = jnp.tanh(GELU_C * x * (1.0 + GELU_K * square))
-    half = 0.5 * (1.0 + t)
-    slope = half + 0.5 * x * (1.0 - t * t) * (GELU_C * (1.0 + 3.0 * GELU_K * square))
-    return x * half, slope
+    t = gelu_tanh(x)
+    return 0.5 * x * (1.0 + t), gelu_slope(x, t)
 
 
 def dot(a, b):
@@ -329,17 +335,26 @@
             staging[layer].at[j, 0:conv_rows],
         )
 
+    cot_at = (2 * tasks + 2) * windows
+    image_at = cot_at + tasks * windows
     loads = [
         load(1, squeeze_w, r.sst),
         load(2, expand_w, r.est),
-        load(3, images.at[s], r.xin),
-        load(4, cotangent.at[s], r.cin),
+        load(3, images.at[s], r.g1.at[image_at : image_at + pixels]),
+        *[
+            load(
+                5 + 2 * n_lane + t,
+                cotangent.at[s, t],
+                r.g1.at[cot_at + t * windows : cot_at + (t + 1) * windows],
+            )
+            for t in range(tasks)
+        ],
     ]
     loads[2].start()
     for layer in range(2):
         for j in range(n_lane):
             conv_load(layer, j).start()
-    for i in (0, 1, 3):
+    for i in (0, 1, *range(3, 3 + tasks)):
         loads[i].start()
 
     full = [r.w0, r.gp, r.w1]
@@ -420,17 +435,19 @@
                 ag_pass(kind, way, 1, lambda copy: copy.start())
         ag_own_copy(kind, c).start()
 
-    def for_hop(kind, hop, do):
+    at_end = jnp.logical_or(z == 0, z == n_z - 1)
+
+    def for_hop(kind, hop, do, also=True):
         if kind == 1:
             do(hop - 1, z_at(n_z - hop), None)
             return
         for way in range(2):
 
-            @pl.when(has(way, hop))
+            @pl.when(jnp.logical_and(has(way, hop), also))
             def _():
                 do(slot_of(way, hop), z_of(way, hop), way)
 
-    def ag_z(kind, hop):
+    def ag_z(kind, hop, also=True):
         def do(slot, owner, way):
             if kind == 1:
                 gate_z_copy(hop, owner).wait_recv()
@@ -442,16 +459,16 @@
                 ag_p_copy(kind, slot, owner, leg, s).start()
             ag_s_copy(kind, slot, owner, 0, c).start()
 
-        for_hop(kind, hop, do)
-
-    def ag_r(kind, hop):
+        for_hop(kind, hop, do, also)
+
+    def ag_r(kind, hop, also=True):
         def do(slot, owner, way):
             for leg in range(2):
                 ag_p_copy(kind, slot, owner, leg, plane[leg]).wait_recv()
                 ag_p_copy(kind, slot, owner, 2 + leg, plane[leg]).start()
                 ag_s_copy(kind, slot, owner, 1 + leg, c).start()
 
-        for_hop(kind, hop, do)
+        for_hop(kind, hop, do, also)
 
     def ag_p(kind, hop):
         def do(slot, owner, way):
@@ -710,7 +727,7 @@
 
     def image_row(i):
         def value(j):
-            v = r.xin[i * cols : (i + 1) * cols, lane_at(j)].astype(F32)
+            v = r.g1[image_at + i * cols : image_at + (i + 1) * cols, lane_at(j)].astype(F32)
             return jnp.where(valid_rows(i * cols, cols), v, 0.0)
 
         return value
@@ -737,18 +754,18 @@
     ag_r(0, 1)
     ag_z(0, 3)
     ag_start(2)
+    halo_start(0, r.xc0)
     ag_r(0, 2)
     ag_p(0, 1)
     ag_r(0, 3)
     ag_z(2, 1)
-    halo_start(0, r.xc0)
     r.total[...] = jnp.concatenate([ex_finish(4)[0]] * 8, axis=0)
     ag_p(0, 2)
     ag_p(0, 3)
     ag_sib(0)
-    ag_z(2, 2)
     conv_forward(r.xc0, r.w0, r.h0, 0, 0)
     conv_forward(r.xc0, r.w0, r.h0, 1, 0)
+    ag_z(2, 2)
     ag_r(2, 1)
     halo_finish(0, r.xc0)
     conv_forward(r.xc0, r.w0, r.h0, 0, 1)
@@ -756,10 +773,9 @@
     stats(r.h0, 0)
     ex_start(0)
     halo_sent(0, r.xc0)
+    ag_start(1)
     ag_z(2, 3)
-    ag_start(1)
-    ag_r(2, 2)
-    ag_p(2, 1)
+    ag_r(2, 2, at_end)
     norm_of(ex_finish(0), 0)
 
     def block_0(j, _):
@@ -769,9 +785,22 @@
             normed = (r.h0[j, rows, :] - r.norm[0, 0:1, lane]) * r.norm[
                 0, 2:3, lane
             ] + bias[0:1, lane]
-            g, slope = gelu_pair(normed)
+            t = gelu_tanh(normed)
             ok = valid_rows(i * quarter_rows, quarter_rows)
+            g = 0.5 * normed * (1.0 + t)
             r.fbuf[j, rows, :] = jnp.where(ok, g, 0.0).astype(BF16).astype(F32)
+            r.slope0[j, rows, :] = t
+        return 0
+
+    def block_0_rest(j, _):
+        lane = lane_at(j)
+        for i in range(4):
+            rows = slice(i * quarter_rows, (i + 1) * quarter_rows)
+            normed = (r.h0[j, rows, :] - r.norm[0, 0:1, lane]) * r.norm[0, 2:3, lane] + bias[
+                0:1, lane
+            ]
+            slope = gelu_slope(normed, r.slope0[j, rows, :])
+            ok = valid_rows(i * quarter_rows, quarter_rows)
             r.slope0[j, rows, :] = jnp.where(ok, slope, 0.0)
         f1p = picked(r.fbuf, j)
         r.f1p[:, lane] = f1p
@@ -782,10 +811,13 @@
     shift_in(lambda j: r.fbuf[j, 0:cols, :], r.xc1, 1)
     shift_in(lambda j: r.fbuf[j, cols : 2 * cols, :], r.xc1, 2)
     halo_start(1, r.xc1)
+    ag_r(2, 2, jnp.logical_not(at_end))
+    ag_p(2, 1)
     ag_r(2, 3)
-    ag_p(2, 2)
     for step in range(1, n_z):
         ag_z(1, step)
+    lax.fori_loop(0, n_lane, block_0_rest, 0)
+    ag_p(2, 2)
     ag_p(2, 3)
     ag_sib(2)
     conv_forward(r.xc1, r.w1, r.h1, 0, 0)
@@ -830,7 +862,8 @@
         r.t1[t] = (mask_pick * value * r.f1p[...]).astype(BF16)
         return 0
 
-    lax.fori_loop(0, tasks, gate_0, 0)
+    for t in range(tasks):
+        gate_0(t, 0)
     norm_of(ex_finish(1), 1)
 
     for kind in range(3):
@@ -892,7 +925,7 @@
         rows = shard_rows[kind] // 4
         half = (0, 1, 1, 0, 0, 1)[leg]
         to = plane[(0, 1, 0, 1, 1, 0)[leg]]
-        view = r.td[kind].at[pl.ds(al(q * rows, 16), rows), halves[half]]
+        view = out_reduced[kind].at[pl.ds(al(q * rows, 16), rows), halves[half]]
         return remote(view, view, r.rs_ds.at[kind, leg], r.rs_dr.at[kind, leg], (to, d))
 
     def conv_weight(kind, xc, k):
@@ -967,7 +1000,7 @@
             rs_c_copy(kind, k).wait_recv()
             total = total + r.rc[kind][k].astype(F32)
         rows = shard_rows[kind] // 4
-        r.td[kind][pl.ds(al(s * rows, 16), rows), :] = total.astype(BF16)
+        out_reduced[kind][pl.ds(al(s * rows, 16), rows), :] = total.astype(BF16)
         for leg in range(4):
             rs_d_copy(kind, leg, s).start()
 
@@ -993,7 +1026,8 @@
         for leg in range(2):
             rs_d_copy(kind, 4 + leg, plane[leg]).wait_send()
 
-    loads[3].wait()
+    for item in loads[3:]:
+        item.wait()
     r.df2[...] = jnp.zeros_like(r.df2)
 
     def pack_grads(l, t, grad_squeeze, grad_expand):
@@ -1027,8 +1061,8 @@
         excited = g.astype(BF16)
         value = jax.nn.sigmoid(dot(excited, w_e))
         field = mask_pick * f2p
-        d_task = r.cin[t].astype(F32)
-        r.cin[t] = (value * field).astype(BF16)
+        d_task = r.g1[cot_at + t * windows : cot_at + (t + 1) * windows, :].astype(F32)
+        out_task[0, t] = (value * field).astype(BF16)
         d_expanded = (d_task * field * value * (1.0 - value)).astype(BF16)
         d_squeezed = (slope * dot_nt(d_expanded, w_e)).astype(BF16)
         d_source = dot_nt(d_squeezed, w_s)
@@ -1049,10 +1083,8 @@
         )
         return 0
 
-    lax.fori_loop(0, tasks, gate_1, 0)
-    task_store = pltpu.make_async_copy(r.cin, out_task.at[0], r.store.at[0])
-    task_store.start()
-
+    for t in range(tasks):
+        gate_1(t, 0)
     def back_1(j, _):
         lane = lane_at(j)
         d_norm = r.slope1[:, lane] * r.df2[:, lane].astype(BF16).astype(F32)
@@ -1078,8 +1110,10 @@
         pack_grads(0, t, dot_tn(r.f1b[...], d_squeezed), dot_tn(excited, d_expanded))
         return 0
 
-    lax.fori_loop(0, tasks, gate_0_back, 0)
-    lax.fori_loop(0, tasks, gate_1_weight, 0)
+    for t in range(tasks):
+        gate_0_back(t, 0)
+    for t in range(tasks):
+        gate_1_weight(t, 0)
 
     r.sums[...] = jnp.zeros_like(r.sums)
 
@@ -1216,14 +1250,12 @@
         lane = lane_at(j)
         for i in range(4):
             rows = slice(i * quarter_rows, (i + 1) * quarter_rows)
-            r.xin[rows, lane] = jnp.where(
+            out_image[0, rows, lane] = jnp.where(
                 valid_rows(i * quarter_rows, quarter_rows), r.fbuf[j, rows, :], 0.0
             ).astype(BF16)
         return 0
 
     lax.fori_loop(0, n_lane, image_out, 0)
-    image_store = pltpu.make_async_copy(r.xin, out_image.at[0], r.store.at[1])
-    image_store.start()
     rs_r(0, 0)
     rs_b(0, 2)
     rs_c(2, 3)
@@ -1255,23 +1287,9 @@
     halo_sent(3, r.dc)
     halo_sent(1, r.xc1)
     rs_dr(0)
-    stores = [task_store, image_store]
-
-    def reduced_out(kind):
+    for kind in (1, 2, 0):
         rs_e(kind)
-        stores.append(
-            pltpu.make_async_copy(r.td[kind], out_reduced[kind], r.store.at[2 + kind])
-        )
-        stores[-1].start()
-
-    reduced_out(1)
-    reduced_out(2)
-    for kind in range(1, 3):
         rs_end(kind)
-    reduced_out(0)
-    rs_end(0)
-    for copy in stores:
-        copy.wait()
 
 
 def finish_kernel(
@@ -1290,59 +1308,37 @@
     out_expand,
     out_gain,
     out_bias,
-    task_in,
-    image_in,
-    conv_in,
     conv_wide,
-    gate_in,
     squeeze_wide,
     expand_wide,
-    sem_in,
-    sem_out,
+    sem,
 ):
     lanes = 128
     e_rows = dims.bottle // dims.n_dp
-    ins = [
-        pltpu.make_async_copy(reduced_0, conv_in.at[0], sem_in.at[0]),
-        pltpu.make_async_copy(reduced_2, conv_in.at[1], sem_in.at[1]),
-        pltpu.make_async_copy(reduced_1, gate_in, sem_in.at[2]),
-        pltpu.make_async_copy(task, task_in, sem_in.at[3]),
-        pltpu.make_async_copy(image, image_in, sem_in.at[4]),
-    ]
-    for copy in ins:
-        copy.start()
-    outs = [
-        pltpu.make_async_copy(task_in, out_task, sem_out.at[0]),
-        pltpu.make_async_copy(image_in, out_image, sem_out.at[1]),
-    ]
-    out_gain[...] = gain[...]
-    out_bias[...] = bias[...]
-    for layer in range(2):
-        ins[layer].wait()
-        conv_wide[layer] = conv_in[layer].astype(F32)
-        outs.append(
-            pltpu.make_async_copy(
-                conv_wide.at[layer], out_conv.at[layer], sem_out.at[2 + layer]
-            )
-        )
+    outs = []
+
+    def store(src, dst):
+        outs.append(pltpu.make_async_copy(src, dst, sem.at[len(outs)]))
         outs[-1].start()
-    for i in range(2):
-        ins[3 + i].wait()
-        outs[i].start()
-    ins[2].wait()
+
+    store(task, out_task)
+    store(image, out_image)
+    for layer, reduced in enumerate((reduced_0, reduced_2)):
+        conv_wide[layer] = reduced[...].astype(F32)
+        store(conv_wide.at[layer], out_conv.at[layer])
     for l in range(2):
         for t in range(dims.tasks):
             at = (l * dims.tasks + t) * e_rows
-            expand_wide[l, t] = gate_in[at : at + e_rows, :].astype(F32)
+            expand_wide[l, t] = reduced_1[at : at + e_rows, :].astype(F32)
             at = at + 2 * dims.tasks * e_rows
             for k in range(dims.width // dims.n_dp // e_rows):
-                squeeze_wide[l, t, k * e_rows : (k + 1) * e_rows, :] = gate_in[
+                squeeze_wide[l, t, k * e_rows : (k + 1) * e_rows, :] = reduced_1[
                     at : at + e_rows, k * lanes : (k + 1) * lanes
                 ].astype(F32)
-    outs.append(pltpu.make_async_copy(squeeze_wide, out_squeeze, sem_out.at[4]))
-    outs.append(pltpu.make_async_copy(expand_wide, out_expand, sem_out.at[5]))
-    outs[-2].start()
-    outs[-1].start()
+    store(squeeze_wide, out_squeeze)
+    store(expand_wide, out_expand)
+    out_gain[...] = gain[...]
+    out_bias[...] = bias[...]
     for copy in outs:
         copy.wait()
 
@@ -1360,12 +1356,9 @@
     vm = pltpu.VMEM
     dma = pltpu.SemaphoreType.DMA
     scratch = dict(
-        load=dma((5 + 2 * (width // 128),)),
-        store=dma((5,)),
+        load=dma((5 + 2 * (width // 128) + tasks,)),
         sst=vm(squeeze_w.shape, F32),
         est=vm(expand_w.shape, F32),
-        xin=vm((pixels, width), BF16),
-        cin=vm((tasks, windows, width), BF16),
         w0=vm((n_dp * conv_rows, width), BF16),
         gp=vm((n_dp * gate_rows, width), BF16),
         w1=vm((n_dp * conv_rows, width), BF16),
@@ -1428,7 +1421,6 @@
         qs=[vm((n_z - 1, rows, width), BF16) for rows in quarters],
         qf=[vm((rows, width), F32) for rows in quarters],
         rc=[vm((n_z - 1, rows, width), BF16) for rows in quarters],
-        td=[vm((rows, width), BF16) for rows in shard_rows],
     )
     buffers, tree = jax.tree.flatten(scratch, is_leaf=lambda v: not isinstance(v, (dict, list)))
     dims = types.SimpleNamespace(
@@ -1447,19 +1439,20 @@
     results = pl.pallas_call(
         functools.partial(step_kernel, dims),
         out_shape=(
-            jax.ShapeDtypeStruct((1, tasks, windows, width), BF16),
-            jax.ShapeDtypeStruct((1, pixels, width), BF16),
-            *[jax.ShapeDtypeStruct((rows, width), BF16) for rows in shard_rows],
-            jax.ShapeDtypeStruct(gain.shape, F32),
-            jax.ShapeDtypeStruct(bias.shape, F32),
+            vm((1, tasks, windows, width), BF16),
+            vm((1, pixels, width), BF16),
+            *[vm((rows, width), BF16) for rows in shard_rows],
+            vm(gain.shape, F32),
+            vm(bias.shape, F32),
         ),
         in_specs=[smem_spec, vmem_spec, vmem_spec, vmem_spec] + [any_spec] * 5,
-        out_specs=(any_spec,) * 5 + (vmem_spec,) * 2,
+        out_specs=(vmem_spec,) * 7,
         scratch_shapes=tuple(buffers),
         compiler_params=pltpu.CompilerParams(
             collective_id=0, has_side_effects=True, vmem_limit_bytes=VMEM_BYTES
         ),
     )(counts.reshape(micro), pool_index, gain, bias, images, conv_w, squeeze_w, expand_w, cotangent)
+    results = [pltpu.with_memory_space_constraint(v, pltpu.VMEM) for v in results]
     return pl.pallas_call(
         functools.partial(finish_kernel, dims),
         out_shape=(
@@ -1471,20 +1464,15 @@
             jax.ShapeDtypeStruct(gain.shape, F32),
             jax.ShapeDtypeStruct(bias.shape, F32),
         ),
-        in_specs=[any_spec] * 5 + [vmem_spec] * 2,
+        in_specs=[vmem_spec] * 7,
         out_specs=(any_spec,) * 5 + (vmem_spec,) * 2,
         scratch_shapes=(
-            vm((1, tasks, windows, width), BF16),
-            vm((1, pixels, width), BF16),
-            vm(conv_w.shape, BF16),
             vm(conv_w.shape, F32),
-            vm((gate_rows, width), BF16),
             vm(squeeze_w.shape, F32),
             vm(expand_w.shape, F32),
-            dma((5,)),
             dma((6,)),
         ),
-        compiler_params=pltpu.CompilerParams(vmem_limit_bytes=VMEM_BYTES),
+        compiler_params=pltpu.CompilerParams(vmem_limit_bytes=16 * 1024 * 1024),
     )(*results)
 
 

time: 137 us -> 132 us (0.964)
  Pallas kernels: 136 us -> 131 us
    pallas_call x1, Pallas kernels: 131 us -> 128 us  [fused(): pl.pallas_call(functools.partial(step_kernel, dims), out_shape=(vm((1, ta...]
    pallas_call x1, Pallas kernels: 4.49 us -> 2.62 us  [fused(): pl.pallas_call(functools.partial(finish_kernel, dims), out_shape=(jax.Sha...]
where the time goes in v5:
time: 132 us
  Pallas kernels  131 us (99%)
    pallas_call x1, Pallas kernels, fused(): pl.pallas_call(functools.partial(step_kernel, dims), out_shape=(vm((1, ta...  128 us

profile of v5, /device:TPU:0, one launch (start us, length us, event | category | flops | bytes accessed | tf_op | source)
XLA Modules:
  0.0 131.6 jit_solution(15850632939202444824)
XLA Ops:
  0.6 128.1 %shard_map.144 = (bf16[1,3,192,512]{3,2,1,0:T(8,128)(2,1)S(1)}, bf16[1,768,512]{2,1,0:T(8,128)(2,1)S(1)}, bf16[576,512]{1,0:T(8,128)(2,1)S(1)}, bf16[192,512]{1,...) custom-call(s32[4]{0:T(128)} %bitcast.1, s32[4,1,192]{2,1,0:T(1,128)} %picks.1, ...), custom_call_target="tpu_custom_call" | custom-call | tf_op jit(solution)/shard_map/pallas_call | solution.py:1439
  128.8 2.6 %shard_map.145 = (bf16[1,3,192,512]{3,2,1,0:T(8,128)(2,1)}, bf16[1,768,512]{2,1,0:T(8,128)(2,1)}, f32[2,576,512]{2,1,0:T(8,128)}, f32[2,3,64,128]{3,2,1,0:T(8,12...) custom-call(bf16[1,3,192,512]{3,2,1,0:T(8,128)(2,1)S(1)} %get-tuple-element.14.task, ...), custom_call_target="tpu_custom_call" | custom-call | tf_op jit(solution)/shard_map/pallas_call | solution.py:1456

commit v6 on v5

--- a/solution.py
+++ b/solution.py
@@ -256,9 +256,9 @@
 def step_kernel(
     dims,
     counts,
-    picks,
-    gain,
-    bias,
+    picks_in,
+    gain_in,
+    bias_in,
     images,
     conv_w,
     squeeze_w,
@@ -350,10 +350,19 @@
             for t in range(tasks)
         ],
     ]
+    small_at = 5 + 2 * n_lane + tasks
+    picks, gain, bias = r.picks, r.gain, r.bias
+    small = [
+        load(small_at, picks_in, picks),
+        load(small_at + 1, gain_in, gain),
+        load(small_at + 2, bias_in, bias),
+    ]
     loads[2].start()
     for layer in range(2):
         for j in range(n_lane):
             conv_load(layer, j).start()
+    for item in small:
+        item.start()
     for i in (0, 1, *range(3, 3 + tasks)):
         loads[i].start()
 
@@ -408,11 +417,10 @@
     halves = [slice(0, width // 2), slice(width // 2, width)]
 
     def ag_p_copy(kind, slot, owner, leg, q):
-        view = quarter(kind, full[kind], 2 * owner + c, q)
-        if leg >= 2:
-            view = view.at[:, halves[leg - 2]]
-        to = plane[(0, 1, 1, 0)[leg]]
-        i = slot * 4 + leg
+        half = (0, 1, 0, 1, 0, 1)[leg]
+        view = quarter(kind, full[kind], 2 * owner + c, q).at[:, halves[half]]
+        to = plane[(0, 0, 1, 1, 1, 0)[leg]]
+        i = slot * 6 + leg
         return remote(view, view, r.ag_ps.at[kind, i], r.ag_pr.at[kind, i], (to, d))
 
     def ag_own_copy(kind, core):
@@ -447,7 +455,7 @@
             def _():
                 do(slot_of(way, hop), z_of(way, hop), way)
 
-    def ag_z(kind, hop, also=True):
+    def ag_z(kind, hop):
         def do(slot, owner, way):
             if kind == 1:
                 gate_z_copy(hop, owner).wait_recv()
@@ -455,25 +463,41 @@
                 ag_z_copy(kind, way, hop, owner).wait_recv()
                 if hop < n_z - 1:
                     ag_pass(kind, way, hop + 1, lambda copy: copy.start())
-            for leg in range(2):
+            for leg in (0, 3):
+                ag_p_copy(kind, slot, owner, leg, s).start()
+
+        for_hop(kind, hop, do)
+
+    def ag_y(kind, hop):
+        def do(slot, owner, way):
+            for leg in (0, 3):
+                ag_p_copy(kind, slot, owner, leg, s).wait_send()
+            for leg in (1, 2):
                 ag_p_copy(kind, slot, owner, leg, s).start()
             ag_s_copy(kind, slot, owner, 0, c).start()
 
-        for_hop(kind, hop, do, also)
+        for_hop(kind, hop, do)
 
     def ag_r(kind, hop, also=True):
         def do(slot, owner, way):
-            for leg in range(2):
-                ag_p_copy(kind, slot, owner, leg, plane[leg]).wait_recv()
-                ag_p_copy(kind, slot, owner, 2 + leg, plane[leg]).start()
-                ag_s_copy(kind, slot, owner, 1 + leg, c).start()
+            for h in range(2):
+                ag_p_copy(kind, slot, owner, 3 * h, plane[h]).wait_recv()
+                ag_p_copy(kind, slot, owner, 4 + h, plane[h]).start()
 
         for_hop(kind, hop, do, also)
+
+    def ag_q(kind, hop):
+        def do(slot, owner, way):
+            for axis in range(2):
+                ag_p_copy(kind, slot, owner, 1 + axis, plane[axis]).wait_recv()
+                ag_s_copy(kind, slot, owner, 1 + axis, c).start()
+
+        for_hop(kind, hop, do)
 
     def ag_p(kind, hop):
         def do(slot, owner, way):
-            for leg in range(2):
-                ag_p_copy(kind, slot, owner, 2 + leg, plane[2]).wait_recv()
+            for h in range(2):
+                ag_p_copy(kind, slot, owner, 4 + h, plane[2]).wait_recv()
             ag_s_copy(kind, slot, owner, 3, c).start()
 
         for_hop(kind, hop, do)
@@ -493,9 +517,10 @@
         for hop in range(1, n_z):
 
             def do(slot, owner, way):
-                for leg in range(2):
+                for leg in (1, 2):
                     ag_p_copy(kind, slot, owner, leg, s).wait_send()
-                    ag_p_copy(kind, slot, owner, 2 + leg, plane[leg]).wait_send()
+                for h in range(2):
+                    ag_p_copy(kind, slot, owner, 4 + h, plane[h]).wait_send()
                 for i in range(4):
                     ag_s_copy(kind, slot, owner, i, c).wait_send()
 
@@ -530,19 +555,7 @@
         return al(which * g_rows + (2 * tasks + l * tasks + t) * e_rows, 16)
 
     count = counts[s]
-    wide = 2 * lanes
-    pick_row = jnp.concatenate(
-        [picks[s].astype(F32), jnp.zeros((1, wide - windows), F32)], axis=1
-    )
-    pick_tile = jnp.broadcast_to(pick_row, (lanes, wide)).T[:windows, :].astype(jnp.int32)
     pick_ref = r.pick
-    pick_ref[...] = pick_tile
-    slot_pick = (
-        (pick_tile // 2) * cols
-        + 2 * lax.broadcasted_iota(jnp.int32, (windows, lanes), 0)
-        + pick_tile % 2
-    )
-    r.mp[...] = jnp.where(slot_pick < count, 1.0, 0.0).astype(F32)
 
     def lane_at(j, base=0):
         return pl.ds(al(base + j * lanes, lanes), lanes)
@@ -576,8 +589,8 @@
         return remote(
             buf.at[2 * cols : 3 * cols, width : 2 * width],
             r.halo.at[e % 2, 0],
-            r.halo_s.at[e, 0],
-            r.halo_r.at[e, 0],
+            r.halo_s.at[e % 2, 0],
+            r.halo_r.at[e % 2, 0],
             (s, rem(d + 1, n_dp)),
         )
 
@@ -585,8 +598,8 @@
         return remote(
             buf.at[cols : 2 * cols, width : 2 * width],
             r.halo.at[e % 2, 1],
-            r.halo_s.at[e, 1],
-            r.halo_r.at[e, 1],
+            r.halo_s.at[e % 2, 1],
+            r.halo_r.at[e % 2, 1],
             (s, rem(d + n_dp - 1, n_dp)),
         )
 
@@ -655,7 +668,7 @@
     def ex_put(k, i, j, value):
         r.ex_out[k, pl.ds(i * n_lane + j, 1), :] = value
 
-    def conv_forward(xc, w, h, row, part):
+    def conv_forward(xc, w, h, row, part, k=None):
         span = 3 * width
         acc = None
         for a in range(3):
@@ -664,13 +677,22 @@
                 continue
             term = dot(xc[block * cols : (block + 1) * cols, :], w[a * span : (a + 1) * span, :])
             acc = term if acc is None else acc + term
-        add_to(h, row, part, acc)
-
-    def add_to(out, row, part, acc):
+        add_to(h, row, part, acc, k)
+
+    def add_to(out, row, part, acc, k=None):
         for j in range(n_lane):
             at = (j, slice(row * cols, (row + 1) * cols), slice(None))
             piece = acc[:, j * lanes : (j + 1) * lanes]
-            out[at] = piece if part == 0 else out[at] + piece
+            if part == 1:
+                piece = out[at] + piece
+            out[at] = piece
+            if k is not None:
+                kept = jnp.where(valid_rows(row * cols, cols), piece, 0.0)
+                for i, value in enumerate((kept, kept * piece)):
+                    value = jnp.sum(value, 0, keepdims=True)
+                    if row == 1:
+                        value = value + r.ex_out[k, i * n_lane + j : i * n_lane + j + 1, :]
+                    ex_put(k, i, j, value)
 
     def conv_back(dc, w, row, part):
         acc = None
@@ -687,21 +709,6 @@
         add_to(r.fbuf, row, part, acc)
 
     quarter_rows = pixels // 4
-
-    def stats(h, k):
-        def body(j, _):
-            first = jnp.zeros((1, lanes), F32)
-            second = jnp.zeros((1, lanes), F32)
-            for i in range(4):
-                v = h[j, i * quarter_rows : (i + 1) * quarter_rows, :]
-                kept = jnp.where(valid_rows(i * quarter_rows, quarter_rows), v, 0.0)
-                first = first + jnp.sum(kept, 0, keepdims=True)
-                second = second + jnp.sum(kept * v, 0, keepdims=True)
-            ex_put(k, 0, j, first)
-            ex_put(k, 1, j, second)
-            return 0
-
-        lax.fori_loop(0, n_lane, body, 0)
 
     def norm_of(sums, layer):
         total = r.total[0:1, :]
@@ -750,17 +757,38 @@
                 ].astype(BF16)
     cast_conv(1, r.w1)
     ag_z(0, 1)
+    ag_y(0, 1)
+    for item in small:
+        item.wait()
+    wide = 2 * lanes
+    pick_row = jnp.concatenate(
+        [picks[s].astype(F32), jnp.zeros((1, wide - windows), F32)], axis=1
+    )
+    pick_tile = jnp.broadcast_to(pick_row, (lanes, wide)).T[:windows, :].astype(jnp.int32)
+    pick_ref[...] = pick_tile
+    slot_pick = (
+        (pick_tile // 2) * cols
+        + 2 * lax.broadcasted_iota(jnp.int32, (windows, lanes), 0)
+        + pick_tile % 2
+    )
+    r.mp[...] = jnp.where(slot_pick < count, 1.0, 0.0).astype(F32)
     ag_z(0, 2)
     ag_r(0, 1)
+    ag_y(0, 2)
     ag_z(0, 3)
     ag_start(2)
     halo_start(0, r.xc0)
+    ag_q(0, 1)
+    ag_y(0, 3)
     ag_r(0, 2)
     ag_p(0, 1)
     ag_r(0, 3)
+    ag_q(0, 2)
     ag_z(2, 1)
     r.total[...] = jnp.concatenate([ex_finish(4)[0]] * 8, axis=0)
     ag_p(0, 2)
+    ag_y(2, 1)
+    ag_q(0, 3)
     ag_p(0, 3)
     ag_sib(0)
     conv_forward(r.xc0, r.w0, r.h0, 0, 0)
@@ -768,13 +796,14 @@
     ag_z(2, 2)
     ag_r(2, 1)
     halo_finish(0, r.xc0)
-    conv_forward(r.xc0, r.w0, r.h0, 0, 1)
-    conv_forward(r.xc0, r.w0, r.h0, 1, 1)
-    stats(r.h0, 0)
+    ag_y(2, 2)
+    conv_forward(r.xc0, r.w0, r.h0, 0, 1, 0)
+    conv_forward(r.xc0, r.w0, r.h0, 1, 1, 0)
     ex_start(0)
     halo_sent(0, r.xc0)
     ag_start(1)
     ag_z(2, 3)
+    ag_q(2, 1)
     ag_r(2, 2, at_end)
     norm_of(ex_finish(0), 0)
 
@@ -811,13 +840,18 @@
     shift_in(lambda j: r.fbuf[j, 0:cols, :], r.xc1, 1)
     shift_in(lambda j: r.fbuf[j, cols : 2 * cols, :], r.xc1, 2)
     halo_start(1, r.xc1)
+    ag_y(2, 3)
     ag_r(2, 2, jnp.logical_not(at_end))
     ag_p(2, 1)
     ag_r(2, 3)
+    ag_q(2, 2)
     for step in range(1, n_z):
         ag_z(1, step)
     lax.fori_loop(0, n_lane, block_0_rest, 0)
+    ag_q(2, 3)
     ag_p(2, 2)
+    for step in range(1, n_z):
+        ag_y(1, step)
     ag_p(2, 3)
     ag_sib(2)
     conv_forward(r.xc1, r.w1, r.h1, 0, 0)
@@ -825,10 +859,11 @@
         ag_r(1, step)
     conv_forward(r.xc1, r.w1, r.h1, 1, 0)
     halo_finish(1, r.xc1)
-    conv_forward(r.xc1, r.w1, r.h1, 0, 1)
-    conv_forward(r.xc1, r.w1, r.h1, 1, 1)
-    stats(r.h1, 1)
+    conv_forward(r.xc1, r.w1, r.h1, 0, 1, 1)
+    conv_forward(r.xc1, r.w1, r.h1, 1, 1, 1)
     ex_start(1)
+    for step in range(1, n_z):
+        ag_q(1, step)
     for hop in range(1, n_z):
         ag_p(1, hop)
     ag_sib(1)
@@ -870,6 +905,7 @@
         ag_end(kind)
     for p in plane:
         pl.semaphore_signal(r.ready, inc=1, device_id=(p, d), device_id_type=MESH)
+    pl.semaphore_signal(r.ready, inc=1, device_id=(s, sib), device_id_type=MESH)
 
     def block_1(j, _):
         lane = lane_at(j)
@@ -890,14 +926,17 @@
         return remote(
             shard(kind, grads[kind], 2 * pair_of(k) + core),
             r.ra[kind].at[k],
-            r.rs_as.at[kind, k],
-            r.rs_ar.at[kind, k],
+            r.ag_zs.at[kind, k],
+            r.ag_zr.at[kind, k] if k < n_z - 1 else r.ag_or.at[kind],
             (s, sib),
         )
 
     def again(first, second, i):
-        per = 4 * (n_z - 1)
-        return (first if i < 3 * per else second).at[i // per % 3, i % per]
+        per = 6 * (n_z - 1)
+        if i < 3 * per:
+            return first.at[i // per, i % per]
+        i, per = i - 3 * per, 4 * (n_z - 1)
+        return second.at[i // per, i % per]
 
     def rs_b_copy(kind, k, way):
         o = 2 * pair_of(k) + c
@@ -921,12 +960,18 @@
             (s, 2 * pair_of(k) + c),
         )
 
+    def d_sem(kind, leg):
+        return (kind * n_z + leg // 4) * 6 + leg % 4
+
     def rs_d_copy(kind, leg, q):
         rows = shard_rows[kind] // 4
         half = (0, 1, 1, 0, 0, 1)[leg]
         to = plane[(0, 1, 0, 1, 1, 0)[leg]]
         view = out_reduced[kind].at[pl.ds(al(q * rows, 16), rows), halves[half]]
-        return remote(view, view, r.rs_ds.at[kind, leg], r.rs_dr.at[kind, leg], (to, d))
+        i = d_sem(kind, leg)
+        return remote(
+            view, view, again(r.ag_ps, r.ag_ss, i), again(r.ag_pr, r.ag_sr, i), (to, d)
+        )
 
     def conv_weight(kind, xc, k):
         tile = 2 * shard_rows[kind] // 3
@@ -1001,6 +1046,8 @@
             total = total + r.rc[kind][k].astype(F32)
         rows = shard_rows[kind] // 4
         out_reduced[kind][pl.ds(al(s * rows, 16), rows), :] = total.astype(BF16)
+        for leg in range(6):
+            rs_b_copy(kind, leg // 4, leg % 4).wait_send()
         for leg in range(4):
             rs_d_copy(kind, leg, s).start()
 
@@ -1017,7 +1064,7 @@
     def rs_end(kind):
         for k in range(n_z):
             rs_a_copy(kind, k, 1 - c).wait_send()
-            for way in range(6):
+            for way in range((4, 2, 0, 0)[k], 6):
                 rs_b_copy(kind, k, way).wait_send()
             if k < n_z - 1:
                 rs_c_copy(kind, k).wait_send()
@@ -1125,6 +1172,7 @@
         r.norm[layer, 4:5, :] = scale * sums[0]
         r.norm[layer, 5:6, :] = scale * r.norm[layer, 1:2, :] * sums[1]
 
+    pl.semaphore_wait(r.ready, 4)
     for k in range(n_z):
         rs_a(1, k)
     back_terms(2, 1)
@@ -1147,9 +1195,9 @@
     lax.fori_loop(0, n_lane, hidden_grad_1, 0)
     shift_in(lambda j: r.fbuf[j, 0:cols, :], r.dc, 1)
     shift_in(lambda j: r.fbuf[j, cols : 2 * cols, :], r.dc, 2)
+    halo_sent(1, r.xc1)
     halo_start(2, r.dc)
 
-    pl.semaphore_wait(r.ready, 3)
     for k in range(n_z):
         rs_b(1, k)
     for k in range(2):
@@ -1285,7 +1333,6 @@
     ex_sent(2)
     ex_sent(3)
     halo_sent(3, r.dc)
-    halo_sent(1, r.xc1)
     rs_dr(0)
     for kind in (1, 2, 0):
         rs_e(kind)
@@ -1356,7 +1403,10 @@
     vm = pltpu.VMEM
     dma = pltpu.SemaphoreType.DMA
     scratch = dict(
-        load=dma((5 + 2 * (width // 128) + tasks,)),
+        load=dma((8 + 2 * (width // 128) + tasks,)),
+        picks=vm(pool_index.shape, jnp.int32),
+        gain=vm(gain.shape, F32),
+        bias=vm(bias.shape, F32),
         sst=vm(squeeze_w.shape, F32),
         est=vm(expand_w.shape, F32),
         w0=vm((n_dp * conv_rows, width), BF16),
@@ -1367,8 +1417,8 @@
         ex_w=vm((2, tasks, bottle, width), BF16),
         ag_zs=dma((3, 2 * (n_z - 1))),
         ag_zr=dma((3, n_z - 1)),
-        ag_ps=dma((3, 4 * (n_z - 1))),
-        ag_pr=dma((3, 4 * (n_z - 1))),
+        ag_ps=dma((3, 6 * (n_z - 1))),
+        ag_pr=dma((3, 6 * (n_z - 1))),
         ag_ss=dma((3, 4 * (n_z - 1))),
         ag_sr=dma((3, 4 * (n_z - 1))),
         ag_os=dma((3,)),
@@ -1376,8 +1426,8 @@
         mp=vm((windows, 128), F32),
         pick=vm((windows, 128), jnp.int32),
         halo=vm((2, 2, cols, width), BF16),
-        halo_s=dma((4, 2)),
-        halo_r=dma((4, 2)),
+        halo_s=dma((2, 2)),
+        halo_r=dma((2, 2)),
         ex_out=vm((5, 8, 128), F32),
         ex_in=vm((5, n_dp, 8, 128), F32),
         total=vm((8, width), F32),
@@ -1406,13 +1456,9 @@
         sums_in=vm((4, 8, width), F32),
         sums_s=dma((3,)),
         sums_r=dma((3,)),
-        rs_as=dma((3, n_z)),
-        rs_ar=dma((3, n_z)),
         ready=pltpu.SemaphoreType.REGULAR,
         rs_cs=dma((3, n_z - 1)),
         rs_cr=dma((3, n_z - 1)),
-        rs_ds=dma((3, 6)),
-        rs_dr=dma((3, 6)),
     )
     quarters = [rows // 4 for rows in shard_rows]
     scratch.update(
@@ -1445,7 +1491,7 @@
             vm(gain.shape, F32),
             vm(bias.shape, F32),
         ),
-        in_specs=[smem_spec, vmem_spec, vmem_spec, vmem_spec] + [any_spec] * 5,
+        in_specs=[smem_spec] + [any_spec] * 8,
         out_specs=(vmem_spec,) * 7,
         scratch_shapes=tuple(buffers),
         compiler_params=pltpu.CompilerParams(

time: 132 us -> 130 us (0.985)
  Pallas kernels: 131 us -> 129 us
where the time goes in v6:
time: 130 us
  Pallas kernels  129 us (99%)
    pallas_call x1, Pallas kernels, fused(): pl.pallas_call(functools.partial(step_kernel, dims), out_shape=(vm((1, ta...  127 us
    pallas_call x1, Pallas kernels, fused(): pl.pallas_call(functools.partial(finish_kernel, dims), out_shape=(jax.Sha...  2.62 us

profile of v6, /device:TPU:0, one launch (start us, length us, event | category | flops | bytes accessed | tf_op | source)
XLA Modules:
  0.0 130.3 jit_solution(9200116373956403264)
XLA Ops:
  0.6 126.8 %shard_map.144 = (bf16[1,3,192,512]{3,2,1,0:T(8,128)(2,1)S(1)}, bf16[1,768,512]{2,1,0:T(8,128)(2,1)S(1)}, bf16[576,512]{1,0:T(8,128)(2,1)S(1)}, bf16[192,512]{1,...) custom-call(s32[4]{0:T(128)} %bitcast.1, s32[4,1,192]{2,1,0:T(1,128)} %picks_in.1, ...), custom_call_target="tpu_custom_call" | custom-call | tf_op jit(solution)/shard_map/pallas_call | solution.py:1485
  127.4 2.6 %shard_map.145 = (bf16[1,3,192,512]{3,2,1,0:T(8,128)(2,1)}, bf16[1,768,512]{2,1,0:T(8,128)(2,1)}, f32[2,576,512]{2,1,0:T(8,128)}, f32[2,3,64,128]{3,2,1,0:T(8,12...) custom-call(bf16[1,3,192,512]{3,2,1,0:T(8,128)(2,1)S(1)} %get-tuple-element.14.task, ...), custom_call_target="tpu_custom_call" | custom-call | tf_op jit(solution)/shard_map/pallas_call | solution.py:1502

commit v7 on v6

--- a/solution.py
+++ b/solution.py
@@ -255,7 +255,7 @@
 
 def step_kernel(
     dims,
-    counts,
+    counts_in,
     picks_in,
     gain_in,
     bias_in,
@@ -352,15 +352,19 @@
     ]
     small_at = 5 + 2 * n_lane + tasks
     picks, gain, bias = r.picks, r.gain, r.bias
+    counts = r.counts
+    count_load = load(small_at + 3, counts_in, counts)
     small = [
         load(small_at, picks_in, picks),
         load(small_at + 1, gain_in, gain),
         load(small_at + 2, bias_in, bias),
     ]
+    for j in range(n_lane):
+        conv_load(0, j).start()
+    count_load.start()
     loads[2].start()
-    for layer in range(2):
-        for j in range(n_lane):
-            conv_load(layer, j).start()
+    for j in range(n_lane):
+        conv_load(1, j).start()
     for item in small:
         item.start()
     for i in (0, 1, *range(3, 3 + tasks)):
@@ -434,6 +438,9 @@
 
     others = [s] + plane
 
+    def both(condition):
+        return (condition, condition)
+
     def ag_start(kind):
         if kind == 1:
             for step in range(1, n_z):
@@ -445,17 +452,21 @@
 
     at_end = jnp.logical_or(z == 0, z == n_z - 1)
 
-    def for_hop(kind, hop, do, also=True):
+    in_middle = jnp.logical_not(at_end)
+    from_end = (z == 1, z == n_z - 2)
+    not_from_end = (z != 1, z != n_z - 2)
+
+    def for_hop(kind, hop, do, also=(True, True)):
         if kind == 1:
             do(hop - 1, z_at(n_z - hop), None)
             return
         for way in range(2):
 
-            @pl.when(jnp.logical_and(has(way, hop), also))
+            @pl.when(jnp.logical_and(has(way, hop), also[way]))
             def _():
                 do(slot_of(way, hop), z_of(way, hop), way)
 
-    def ag_z(kind, hop):
+    def ag_z(kind, hop, also=(True, True), legs=True):
         def do(slot, owner, way):
             if kind == 1:
                 gate_z_copy(hop, owner).wait_recv()
@@ -463,12 +474,20 @@
                 ag_z_copy(kind, way, hop, owner).wait_recv()
                 if hop < n_z - 1:
                     ag_pass(kind, way, hop + 1, lambda copy: copy.start())
+            if legs:
+                for leg in (0, 3):
+                    ag_p_copy(kind, slot, owner, leg, s).start()
+
+        for_hop(kind, hop, do, also)
+
+    def ag_l(kind, hop, also):
+        def do(slot, owner, way):
             for leg in (0, 3):
                 ag_p_copy(kind, slot, owner, leg, s).start()
 
-        for_hop(kind, hop, do)
-
-    def ag_y(kind, hop):
+        for_hop(kind, hop, do, also)
+
+    def ag_y(kind, hop, also=(True, True)):
         def do(slot, owner, way):
             for leg in (0, 3):
                 ag_p_copy(kind, slot, owner, leg, s).wait_send()
@@ -476,9 +495,9 @@
                 ag_p_copy(kind, slot, owner, leg, s).start()
             ag_s_copy(kind, slot, owner, 0, c).start()
 
-        for_hop(kind, hop, do)
-
-    def ag_r(kind, hop, also=True):
+        for_hop(kind, hop, do, also)
+
+    def ag_r(kind, hop, also=(True, True)):
         def do(slot, owner, way):
             for h in range(2):
                 ag_p_copy(kind, slot, owner, 3 * h, plane[h]).wait_recv()
@@ -554,6 +573,10 @@
     def sq_row(which, l, t):
         return al(which * g_rows + (2 * tasks + l * tasks + t) * e_rows, 16)
 
+    cast_conv(0, r.w0)
+    pl.semaphore_wait(barrier, n_dp - 1 + 3)
+    ag_start(0)
+    count_load.wait()
     count = counts[s]
     pick_ref = r.pick
 
@@ -741,9 +764,6 @@
 
     shift_in(image_row(0), r.xc0, 1)
     shift_in(image_row(1), r.xc0, 2)
-    cast_conv(0, r.w0)
-    pl.semaphore_wait(barrier, n_dp - 1 + 3)
-    ag_start(0)
     r.ex_out[4] = jnp.broadcast_to(count.astype(F32), (8, lanes))
     ex_start(4)
     loads[0].wait()
@@ -757,6 +777,11 @@
                 ].astype(BF16)
     cast_conv(1, r.w1)
     ag_z(0, 1)
+
+    @pl.when(at_end)
+    def _():
+        ag_start(2)
+
     ag_y(0, 1)
     for item in small:
         item.wait()
@@ -773,38 +798,49 @@
     )
     r.mp[...] = jnp.where(slot_pick < count, 1.0, 0.0).astype(F32)
     ag_z(0, 2)
+    ag_z(2, 1, from_end, legs=False)
     ag_r(0, 1)
     ag_y(0, 2)
     ag_z(0, 3)
-    ag_start(2)
+
+    @pl.when(in_middle)
+    def _():
+        ag_start(2)
+
     halo_start(0, r.xc0)
     ag_q(0, 1)
+    ag_z(2, 2, both(in_middle), legs=False)
     ag_y(0, 3)
     ag_r(0, 2)
     ag_p(0, 1)
     ag_r(0, 3)
     ag_q(0, 2)
-    ag_z(2, 1)
+    ag_l(2, 1, from_end)
+    ag_z(2, 1, not_from_end)
+    ag_l(2, 2, both(in_middle))
     r.total[...] = jnp.concatenate([ex_finish(4)[0]] * 8, axis=0)
     ag_p(0, 2)
     ag_y(2, 1)
     ag_q(0, 3)
     ag_p(0, 3)
     ag_sib(0)
+    ag_z(2, 3)
     conv_forward(r.xc0, r.w0, r.h0, 0, 0)
     conv_forward(r.xc0, r.w0, r.h0, 1, 0)
-    ag_z(2, 2)
+    ag_z(2, 2, both(at_end))
     ag_r(2, 1)
     halo_finish(0, r.xc0)
-    ag_y(2, 2)
+    ag_y(2, 2, both(in_middle))
+    ag_y(2, 3)
     conv_forward(r.xc0, r.w0, r.h0, 0, 1, 0)
     conv_forward(r.xc0, r.w0, r.h0, 1, 1, 0)
     ex_start(0)
     halo_sent(0, r.xc0)
     ag_start(1)
-    ag_z(2, 3)
+    ag_y(2, 2, both(at_end))
     ag_q(2, 1)
-    ag_r(2, 2, at_end)
+    ag_r(2, 2, both(in_middle))
+    ag_r(2, 3)
     norm_of(ex_finish(0), 0)
 
     def block_0(j, _):
@@ -840,10 +876,8 @@
     shift_in(lambda j: r.fbuf[j, 0:cols, :], r.xc1, 1)
     shift_in(lambda j: r.fbuf[j, cols : 2 * cols, :], r.xc1, 2)
     halo_start(1, r.xc1)
-    ag_y(2, 3)
-    ag_r(2, 2, jnp.logical_not(at_end))
+    ag_r(2, 2, both(at_end))
     ag_p(2, 1)
-    ag_r(2, 3)
     ag_q(2, 2)
     for step in range(1, n_z):
         ag_z(1, step)
@@ -1048,10 +1082,15 @@
         out_reduced[kind][pl.ds(al(s * rows, 16), rows), :] = total.astype(BF16)
         for leg in range(6):
             rs_b_copy(kind, leg // 4, leg % 4).wait_send()
-        for leg in range(4):
+        for leg in range(2 if kind == 0 else 4):
             rs_d_copy(kind, leg, s).start()
 
     def rs_dr(kind):
+        if kind == 0:
+            for leg in range(2):
+                rs_d_copy(kind, leg, s).wait_send()
+            for leg in range(2, 4):
+                rs_d_copy(kind, leg, s).start()
         for leg in range(2):
             rs_d_copy(kind, leg, plane[leg]).wait_recv()
             rs_d_copy(kind, 4 + leg, plane[leg]).start()
@@ -1068,7 +1107,7 @@
                 rs_b_copy(kind, k, way).wait_send()
             if k < n_z - 1:
                 rs_c_copy(kind, k).wait_send()
-        for leg in range(4):
+        for leg in range(2 if kind == 0 else 0, 4):
             rs_d_copy(kind, leg, s).wait_send()
         for leg in range(2):
             rs_d_copy(kind, 4 + leg, plane[leg]).wait_send()
@@ -1403,7 +1442,8 @@
     vm = pltpu.VMEM
     dma = pltpu.SemaphoreType.DMA
     scratch = dict(
-        load=dma((8 + 2 * (width // 128) + tasks,)),
+        load=dma((9 + 2 * (width // 128) + tasks,)),
+        counts=pltpu.SMEM((micro,), jnp.int32),
         picks=vm(pool_index.shape, jnp.int32),
         gain=vm(gain.shape, F32),
         bias=vm(bias.shape, F32),
@@ -1481,7 +1521,6 @@
     )
     any_spec = pl.BlockSpec(memory_space=pl.ANY)
     vmem_spec = pl.BlockSpec(memory_space=pltpu.VMEM)
-    smem_spec = pl.BlockSpec(memory_space=pltpu.SMEM)
     results = pl.pallas_call(
         functools.partial(step_kernel, dims),
         out_shape=(
@@ -1491,7 +1530,7 @@
             vm(gain.shape, F32),
             vm(bias.shape, F32),
         ),
-        in_specs=[smem_spec] + [any_spec] * 8,
+        in_specs=[any_spec] * 9,
         out_specs=(vmem_spec,) * 7,
         scratch_shapes=tuple(buffers),
         compiler_params=pltpu.CompilerParams(

time: 130 us -> 128 us (0.985)
    pallas_call x1, Pallas kernels: 127 us -> 125 us  [fused(): pl.pallas_call(functools.partial(step_kernel, dims), out_shape=(vm((1, ta...]
where the time goes in v7:
time: 128 us
  Pallas kernels  128 us (100%)
    pallas_call x1, Pallas kernels, fused(): pl.pallas_call(functools.partial(step_kernel, dims), out_shape=(vm((1, ta...  125 us
    pallas_call x1, Pallas kernels, fused(): pl.pallas_call(functools.partial(finish_kernel, dims), out_shape=(jax.Sha...  2.62 us

profile of v7, /device:TPU:0, one launch (start us, length us, event | category | flops | bytes accessed | tf_op | source)
XLA Modules:
  0.0 128.3 jit_solution(15535987600731182006)
XLA Ops:
  0.6 124.9 %shard_map.144 = (bf16[1,3,192,512]{3,2,1,0:T(8,128)(2,1)S(1)}, bf16[1,768,512]{2,1,0:T(8,128)(2,1)S(1)}, bf16[576,512]{1,0:T(8,128)(2,1)S(1)}, bf16[192,512]{1,...) custom-call(s32[4]{0:T(128)} %bitcast.1, s32[4,1,192]{2,1,0:T(1,128)} %picks_in.1, ...), custom_call_target="tpu_custom_call" | custom-call | tf_op jit(solution)/shard_map/pallas_call | solution.py:1524
  125.5 2.6 %shard_map.145 = (bf16[1,3,192,512]{3,2,1,0:T(8,128)(2,1)}, bf16[1,768,512]{2,1,0:T(8,128)(2,1)}, f32[2,576,512]{2,1,0:T(8,128)}, f32[2,3,64,128]{3,2,1,0:T(8,12...) custom-call(bf16[1,3,192,512]{3,2,1,0:T(8,128)(2,1)S(1)} %get-tuple-element.14.task, ...), custom_call_target="tpu_custom_call" | custom-call | tf_op jit(solution)/shard_map/pallas_call | solution.py:1541

commit v8 on v7

--- a/solution.py
+++ b/solution.py
@@ -878,15 +878,15 @@
     halo_start(1, r.xc1)
     ag_r(2, 2, both(at_end))
     ag_p(2, 1)
-    ag_q(2, 2)
+    lax.fori_loop(0, n_lane, block_0_rest, 0)
     for step in range(1, n_z):
         ag_z(1, step)
-    lax.fori_loop(0, n_lane, block_0_rest, 0)
+    ag_q(2, 2)
     ag_q(2, 3)
     ag_p(2, 2)
+    ag_p(2, 3)
     for step in range(1, n_z):
         ag_y(1, step)
-    ag_p(2, 3)
     ag_sib(2)
     conv_forward(r.xc1, r.w1, r.h1, 0, 0)
     for step in range(1, n_z):

time: 128 us -> 128 us (level)
  no operation moved by 1% of the time
where the time goes in v8:
time: 128 us
  Pallas kernels  127 us (99%)
    pallas_call x1, Pallas kernels, fused(): pl.pallas_call(functools.partial(step_kernel, dims), out_shape=(vm((1, ta...  125 us
    pallas_call x1, Pallas kernels, fused(): pl.pallas_call(functools.partial(finish_kernel, dims), out_shape=(jax.Sha...  2.62 us

profile of v8, /device:TPU:0, one launch (start us, length us, event | category | flops | bytes accessed | tf_op | source)
XLA Modules:
  0.0 128.1 jit_solution(2987619580107387300)
XLA Ops:
  0.6 124.6 %shard_map.144 = (bf16[1,3,192,512]{3,2,1,0:T(8,128)(2,1)S(1)}, bf16[1,768,512]{2,1,0:T(8,128)(2,1)S(1)}, bf16[576,512]{1,0:T(8,128)(2,1)S(1)}, bf16[192,512]{1,...) custom-call(s32[4]{0:T(128)} %bitcast.1, s32[4,1,192]{2,1,0:T(1,128)} %picks_in.1, ...), custom_call_target="tpu_custom_call" | custom-call | tf_op jit(solution)/shard_map/pallas_call | solution.py:1524
  125.3 2.6 %shard_map.145 = (bf16[1,3,192,512]{3,2,1,0:T(8,128)(2,1)}, bf16[1,768,512]{2,1,0:T(8,128)(2,1)}, f32[2,576,512]{2,1,0:T(8,128)}, f32[2,3,64,128]{3,2,1,0:T(8,12...) custom-call(bf16[1,3,192,512]{3,2,1,0:T(8,128)(2,1)S(1)} %get-tuple-element.14.task, ...), custom_call_target="tpu_custom_call" | custom-call | tf_op jit(solution)/shard_map/pallas_call | solution.py:1541

commit v9 on v7

--- a/solution.py
+++ b/solution.py
@@ -330,7 +330,7 @@
     def conv_load(layer, j):
         lane = slice(j * lanes, (j + 1) * lanes)
         return load(
-            5 + layer * n_lane + j,
+            5 + layer,
             conv_w.at[layer, :, lane],
             staging[layer].at[j, 0:conv_rows],
         )
@@ -551,8 +551,8 @@
             for_hop(kind, hop, do)
 
     def cast_conv(layer, buf):
-        for j in range(n_lane):
-            conv_load(layer, j).wait()
+        view = staging[layer].at[:, 0:conv_rows]
+        load(5 + layer, view, view).wait()
 
         def body(j, _):
             buf[pl.ds(al(d * conv_rows, 16), conv_rows), pl.ds(al(j * lanes, lanes), lanes)] = (
@@ -661,14 +661,17 @@
         return remote(
             r.ex_out.at[k],
             r.ex_in.at[k, owner],
-            r.ex_s.at[turn, step - 1],
-            r.ex_r.at[turn, step - 1],
+            r.ex_s.at[turn],
+            r.ex_r.at[turn],
             (s, rem(d + step, n_dp)),
         )
 
     def ex_sent(k):
-        for step in range(1, n_dp):
-            ex_copy(k, step, d).wait_send()
+        ex_all(k, r.ex_s)
+
+    def ex_all(k, sem):
+        view = r.ex_in.at[k, 0 : n_dp - 1]
+        pltpu.make_async_copy(view, view, sem.at[(k + 1) % 5 % 2]).wait()
 
     def ex_start(k):
         if k in (1, 2, 3):
@@ -678,8 +681,7 @@
         r.ex_in[k, d] = r.ex_out[k]
 
     def ex_finish(k):
-        for step in range(1, n_dp):
-            ex_copy(k, step, rem(d + n_dp - step, n_dp)).wait_recv()
+        ex_all(k, r.ex_r)
         total = r.ex_in[k, 0]
         for i in range(1, n_dp):
             total = total + r.ex_in[k, i]
@@ -1471,8 +1473,8 @@
         ex_out=vm((5, 8, 128), F32),
         ex_in=vm((5, n_dp, 8, 128), F32),
         total=vm((8, width), F32),
-        ex_s=dma((2, n_dp - 1)),
-        ex_r=dma((2, n_dp - 1)),
+        ex_s=dma((2,)),
+        ex_r=dma((2,)),
         norm=vm((2, 8, width), F32),
         xc0=vm((4 * cols, 3 * width), BF16),
         xc1=vm((4 * cols, 3 * width), BF16),

time: 128 us -> 128 us (level)
  no operation moved by 1% of the time
where the time goes in v9:
time: 128 us
  Pallas kernels  127 us (99%)
    pallas_call x1, Pallas kernels, fused(): pl.pallas_call(functools.partial(step_kernel, dims), out_shape=(vm((1, ta...  125 us
    pallas_call x1, Pallas kernels, fused(): pl.pallas_call(functools.partial(finish_kernel, dims), out_shape=(jax.Sha...  2.62 us

profile of v9, /device:TPU:0, one launch (start us, length us, event | category | flops | bytes accessed | tf_op | source)
XLA Modules:
  0.0 128.1 jit_solution(884864051213413118)
XLA Ops:
  0.6 124.6 %shard_map.144 = (bf16[1,3,192,512]{3,2,1,0:T(8,128)(2,1)S(1)}, bf16[1,768,512]{2,1,0:T(8,128)(2,1)S(1)}, bf16[576,512]{1,0:T(8,128)(2,1)S(1)}, bf16[192,512]{1,...) custom-call(s32[4]{0:T(128)} %bitcast.1, s32[4,1,192]{2,1,0:T(1,128)} %picks_in.1, ...), custom_call_target="tpu_custom_call" | custom-call | tf_op jit(solution)/shard_map/pallas_call | solution.py:1526
  125.3 2.6 %shard_map.145 = (bf16[1,3,192,512]{3,2,1,0:T(8,128)(2,1)}, bf16[1,768,512]{2,1,0:T(8,128)(2,1)}, f32[2,576,512]{2,1,0:T(8,128)}, f32[2,3,64,128]{3,2,1,0:T(8,12...) custom-call(bf16[1,3,192,512]{3,2,1,0:T(8,128)(2,1)S(1)} %get-tuple-element.14.task, ...), custom_call_target="tpu_custom_call" | custom-call | tf_op jit(solution)/shard_map/pallas_call | solution.py:1543
